TPU v7x, 32 devices: a whole 2x2x4 slice. The times are simulated.
32 devices in a mesh: head: 4 (over y, x), seq: 8 (over z, core).
Axes of the slice: x: 2, y: 2, z: 4, core: 2. Of those that a mesh axis runs over, the one named last changes fastest.
Arguments:
- prompts: bfloat16 [16, 256, 4096], P('seq'), may hold values from -6 to 6
- prompt_len: int32 [16], replicated, may hold values from 32 to 256, as said below
- admitted: int32 [4], replicated, may hold values from -1 to 15, as said below
- cache_len: int32 [4], replicated, may hold values from 256 to 4096, as said below
- cache_kv: bfloat16 [4, 4, 4096, 256], P('head', None, 'seq'), may hold values from -12 to 12
- dec_tokens: bfloat16 [4, 4, 4096], replicated, may hold values from -6 to 6
- w_query: bfloat16 [4096, 4096], P(None, 'head'), may hold values from -0.09375 to 0.09375
- w_key: bfloat16 [4096, 512], P(None, 'head'), may hold values from -0.09375 to 0.09375
- w_value: bfloat16 [4096, 512], P(None, 'head'), may hold values from -0.09375 to 0.09375
- w_out: bfloat16 [4096, 4096], P('head'), may hold values from -0.09375 to 0.09375
- q_gain: float32 [128], replicated, may hold values from 0.25 to 16
- k_gain: float32 [128], replicated, may hold values from 0.25 to 16
Outputs:
- prefill_out: bfloat16 [16, 256, 4096], P('seq', None, 'head')
- handed_kv: bfloat16 [4, 16, 256, 256], P('head', None, 'seq')
- decode_out: bfloat16 [4, 4, 4096], P(None, None, 'head')
Inputs may be any that keep to these rules, and one draw needn't show every extreme that they name: `prompt_len`: some prompt has exactly 256 live tokens. `admitted`: slots with an entry of 0 or more name distinct prompts; in every draw some slot keeps its cache and some slot takes prompt 16 - 1. `cache_len`: some slot has exactly 4096 live positions.
All inputs are finite; a program needn't handle non-finite values.
Results may differ from a plain program's by a relative error of at most 0.02.
The roundings to bfloat16 on the way count: a program that leaves them out, or rounds other values in their place, can miss the bound.
Values may be sent and summed in bfloat16 or wider, within the bound.
No kernel may reach another device: no remote copies, remote signals or barrier semaphores. Data moves between devices by JAX's collectives and lax.ppermute only.
A program may use at most 128 MiB of HBM per device.

v0:
```python
import functools

import jax
import jax.numpy as jnp
import numpy as np
from jax import lax
from jax.experimental import pallas as pl
from jax.experimental.pallas import tpu as pltpu
from jax.sharding import PartitionSpec as P

HD = 128
EPS = 1e-06
THETA = 1000000.0
NEG = -1e30
LOG2E = 1.4426950408889634
SCALE = HD**-0.5
C2 = SCALE * LOG2E
BF = jnp.bfloat16
F32 = jnp.float32
HB = pl.BlockSpec(memory_space=pltpu.HBM)
VM = pl.BlockSpec(memory_space=pltpu.VMEM)
BRIEF = pl.CostEstimate(flops=1, bytes_accessed=1, transcendentals=0)
MIB = 1024 * 1024
LIMIT_A = 60
LIMIT_B = 50
LIMIT_C = 50


def frequencies():
    half = HD // 2
    freq = np.float32(THETA) ** (-np.arange(half, dtype=np.float32) / np.float32(half))
    return freq.astype(np.float32)


def turns(places):
    lane = lax.broadcasted_iota(jnp.int32, places.shape, 1)
    freq = jnp.zeros(places.shape, F32)
    spot = lax.rem(lane, HD // 2)
    for i, value in enumerate(frequencies()):
        freq = jnp.where(spot == i, float(value), freq)
    return freq


def cos_sin(places, freq):
    angle = places.astype(F32) * freq
    lane = lax.broadcasted_iota(jnp.int32, places.shape, 1)
    return jnp.cos(angle), jnp.where(lane < HD // 2, -1.0, 1.0) * jnp.sin(angle)


def prompt_table(length):
    angle = np.arange(length, dtype=np.float32)[:, None] * frequencies()[None, :]
    cosine, sine = np.cos(angle), np.sin(angle)
    return np.concatenate([cosine, cosine, -sine, sine], axis=1).astype(np.float32)


def dot(a, b):
    return jnp.dot(a, b, preferred_element_type=F32)


def dot_nt(a, b):
    return lax.dot_general(a, b, (((1,), (1,)), ((), ())), preferred_element_type=F32)


def norm(values, gain):
    square = jnp.mean(values * values, axis=-1, keepdims=True)
    return values * lax.rsqrt(square + EPS) * gain


def rope(values, cos2, sin2):
    return values * cos2 + pltpu.roll(values, HD // 2, 1) * sin2


def effective_lengths(plen, adm, clen, slots):
    out = []
    for r in range(slots):
        taken = adm[r]
        out.append(jnp.where(taken >= 0, plen[jnp.maximum(taken, 0)], clen[r]))
    return out


def by_slot(index, values):
    result = jnp.full(index.shape, values[0])
    for r in range(1, len(values)):
        result = jnp.where(index == r, values[r], result)
    return result


def partners():
    head, seq = lax.axis_index("head"), lax.axis_index("seq")
    flip_x = head + 1 - 2 * lax.rem(head, 2)
    flip_y = lax.rem(head + 2, 4)
    even = lax.rem(seq, 2) == 0
    return jnp.where(even, flip_x, flip_y), jnp.where(even, flip_y, flip_x)


def out_copy(wo_hbm, block, nb, dest, sem):
    return pltpu.make_async_copy(
        wo_hbm.at[:, pl.ds(pl.multiple_of(block * nb, nb), nb)], dest, sem
    )


def mask_bias(rows, length):
    row_at = lax.broadcasted_iota(jnp.int32, (rows, rows), 0)
    col_at = lax.broadcasted_iota(jnp.int32, (rows, rows), 1)
    return jnp.where((col_at <= row_at) & (col_at < length), 0.0, NEG).astype(F32)


def attention(heads, queries, kv, bias_v, s_v, w_v, attn):
    rows = kv.shape[0]
    half = rows // 2
    quarter = rows // 4
    for h in heads:
        at = slice(h * HD, (h + 1) * HD)
        s_v[h, :half, :half] = dot_nt(queries[:half, at], kv[:half, :HD])
        s_v[h, half:, :] = dot_nt(queries[half:, at], kv[:, :HD])
    for h in heads:
        for block in range(4):
            at = slice(block * quarter, (block + 1) * quarter)
            keys = half if block < 2 else rows
            scores = s_v[h, at, :keys] + bias_v[at, :keys]
            top = jnp.max(scores, axis=-1, keepdims=True)
            expo = jnp.exp2((scores - top) * C2)
            total = jnp.sum(expo, axis=-1, keepdims=True)
            w_v[h, at, :keys] = (expo * (1.0 / total)).astype(BF)
    for h in heads:
        at = slice(h * HD, (h + 1) * HD)
        attn[:half, at] = dot(w_v[h, :half, :half], kv[:half, HD:]).astype(BF)
        attn[half:, at] = dot(w_v[h, half:, :], kv[:, HD:]).astype(BF)


def attention_scratch(rows, heads):
    return [
        pltpu.VMEM((rows, rows), F32),
        pltpu.VMEM((heads, rows, rows), F32),
        pltpu.VMEM((heads, rows, rows), BF),
    ]


def unit(count):
    return lax.broadcasted_iota(jnp.int32, (count, count), 0) == lax.broadcasted_iota(
        jnp.int32, (count, count), 1
    )


def decode_attention(n_seq, slots, plen, adm, clen, raw, raw_kv, kvs, cache, qg, kg, part):
    seq = lax.axis_index("seq")
    dec_rows = raw.shape[0]
    width = cache.shape[1]
    rows = kvs[0].shape[0]
    eff = effective_lengths(plen, adm, clen, slots)
    row = lax.broadcasted_iota(jnp.int32, (dec_rows, HD), 0)
    places = by_slot(lax.rem(row, slots), eff) + row // slots
    cos2, sin2 = cos_sin(places, turns(row))
    new_key = rope(norm(raw_kv[:, :HD], kg[...]), cos2, sin2).astype(BF)
    new_value = raw_kv[:, HD:].astype(BF)
    queries = jnp.concatenate(
        [
            rope(norm(raw[:, h * HD : (h + 1) * HD], qg[...]), cos2, sin2).astype(BF)
            for h in range(raw.shape[1] // HD)
        ],
        axis=0,
    )
    count = queries.shape[0]

    row = lax.rem(lax.broadcasted_iota(jnp.int32, (count, 1), 0), dec_rows)
    slot, step = lax.rem(row, slots), row // slots
    taken = by_slot(slot, [adm[r] for r in range(slots)])
    scores, masks, values = [], [], []
    at = lax.broadcasted_iota(jnp.int32, (1, width), 1) * n_seq + seq
    for r in range(slots):
        limit = jnp.where(adm[r] >= 0, 0, clen[r])
        masks.append((slot == r) & (at < limit))
        scores.append(dot_nt(queries, cache[r, :, :HD]))
        values.append(cache[r, :, HD:])
    spot = lax.broadcasted_iota(jnp.int32, (1, rows), 1)
    for p, kv in enumerate(kvs):
        prompt = seq * len(kvs) + p
        masks.append((taken == prompt) & (spot < plen[prompt]))
        scores.append(dot_nt(queries, kv[:, :HD]))
        values.append(kv[:, HD:])
    other = lax.broadcasted_iota(jnp.int32, (1, dec_rows), 1)
    first = jnp.where(seq == 0, 1, 0)
    masks.append(
        (lax.rem(other, slots) == slot) & (other // slots <= step) & (first + 0 * other > 0)
    )
    scores.append(dot_nt(queries, new_key))
    values.append(new_value)

    top = jnp.full((count, 1), NEG, F32)
    scores = [jnp.where(mask, score, NEG) for mask, score in zip(masks, scores)]
    for score in scores:
        top = jnp.maximum(top, jnp.max(score, axis=-1, keepdims=True))
    total = jnp.zeros((count, 1), F32)
    acc = jnp.zeros((count, HD), F32)
    for mask, score, value in zip(masks, scores, values):
        expo = jnp.where(mask, jnp.exp2((score - top) * C2), 0.0)
        total = total + jnp.sum(expo, axis=-1, keepdims=True)
        acc = acc + dot(expo.astype(BF), value)
    some = total > 0.0
    safe = jnp.where(some, total, 1.0)
    part[:count, :] = acc * (1.0 / safe)
    level = jnp.where(some, top * C2 + jnp.log2(safe), NEG)
    part[count : count + 1, :] = jnp.sum(jnp.where(unit(count), level, 0.0), axis=0, keepdims=True)


def project_kernel(n_head, *refs):
    plen_h, qg_h, kg_h, table_h, x_hbm, dec_hbm, wq_hbm, wk_hbm, wv_hbm, wo_hbm = refs[:10]
    send_h, pack_h, new_h = refs[10:13]
    x_v, dec_v, flat_v, wkv_v, wq_v, wo_v, raw, raw_kv, send, pack = refs[13:23]
    plen, qg, kg, table = refs[23:27]
    bias_v, s_v, w_v = refs[27:30]
    x_sem, dec_sem, wkv_sem, wq_sem, wo_sem, small_sem, out_sem = refs[30:]
    prompts, rows, width = x_hbm.shape
    steps, slots, _ = dec_hbm.shape
    dec_rows = steps * slots
    local = wq_v.shape[1]
    nb = width // n_head
    lead = prompts - 1
    seq = lax.axis_index("seq")
    first, _ = partners()
    diag = 3 - lax.axis_index("head")
    front = rows + dec_rows

    cuts = cut_points(width)
    queue = []
    for c in range(len(cuts) - 1):
        at = pl.ds(cuts[c], cuts[c + 1] - cuts[c])
        queue.append(
            [
                pltpu.make_async_copy(
                    x_hbm.at[lead, :, at], x_v.at[pl.ds(0, rows), at], x_sem.at[0, c]
                ),
                pltpu.make_async_copy(
                    x_hbm.at[0, :, at], x_v.at[pl.ds(front, rows), at], x_sem.at[1, c]
                ),
                pltpu.make_async_copy(wk_hbm.at[at], wkv_v.at[at, pl.ds(0, HD)], wkv_sem.at[0, c]),
                pltpu.make_async_copy(wv_hbm.at[at], wkv_v.at[at, pl.ds(HD, HD)], wkv_sem.at[1, c]),
                pltpu.make_async_copy(wq_hbm.at[at], wq_v.at[at], wq_sem.at[c]),
            ]
        )
    small = [
        pltpu.make_async_copy(src, dst, small_sem.at[i])
        for i, (src, dst) in enumerate(
            [(plen_h, plen), (qg_h, qg), (kg_h, kg), (table_h, table)]
        )
    ]
    dec_copy = pltpu.make_async_copy(dec_hbm, dec_v, dec_sem)
    o_copies = [
        out_copy(wo_hbm, block, nb, wo_v.at[j], wo_sem.at[j]) for j, block in enumerate((diag, first))
    ]
    ahead = 3
    queue += [[copy] for copy in o_copies]
    for copy in [dec_copy] + queue[0] + small:
        copy.start()
    for group in queue[1:ahead]:
        for copy in group:
            copy.start()
    for copy in small:
        copy.wait()
    bias_v[...] = mask_bias(rows, plen[seq * prompts + lead])
    dec_copy.wait()
    for t in range(steps):
        flat_v[t * slots : (t + 1) * slots, :] = dec_v[t].astype(F32)
    x_v[rows:front, :] = flat_v[...].astype(BF)
    for c in range(len(cuts) - 1):
        for copy in queue[c]:
            copy.wait()
        if c + ahead < len(queue):
            for copy in queue[c + ahead]:
                copy.start()
        at = slice(cuts[c], cuts[c + 1])
        kv_part = dot(x_v[:, at], wkv_v[at, :])
        q_part = dot(x_v[:front, at], wq_v[at, :])
        if c == 0:
            raw_kv[...] = kv_part
            raw[...] = q_part
        else:
            raw_kv[...] += kv_part
            raw[...] += q_part
    cos2, sin2 = table[:, :HD], table[:, HD:]
    both = 2 * HD
    kvs = [pack.at[:, pl.ds(p * both, both)] for p in range(prompts)]
    for p, start in ((lead, 0), (0, front)):
        at = slice(start, start + rows)
        kvs[p][:, :HD] = rope(norm(raw_kv[at, :HD], kg[...]), cos2, sin2).astype(BF)
        kvs[p][:, HD:] = raw_kv[at, HD:].astype(BF)
    outs = [
        pltpu.make_async_copy(raw.at[pl.ds(rows, dec_rows)], new_h.at[:, pl.ds(0, local)], out_sem.at[0]),
        pltpu.make_async_copy(
            raw_kv.at[pl.ds(rows, dec_rows)], new_h.at[:, pl.ds(local, both)], out_sem.at[1]
        ),
    ]
    for copy in outs:
        copy.start()
    for copy in o_copies:
        copy.wait()
    base = prompts * both
    mine = pack.at[:, pl.ds(base, local)]
    pair = 2 * HD
    for j in range(local // pair):
        later = dot(x_v[front:, :], wq_v[:, j * pair : (j + 1) * pair])
        for h in (2 * j, 2 * j + 1):
            piece = raw[:rows, h * HD : (h + 1) * HD]
            mine[:, h * HD : (h + 1) * HD] = rope(norm(piece, qg[...]), cos2, sin2).astype(BF)
        attention((2 * j, 2 * j + 1), mine, kvs[lead], bias_v, s_v, w_v, mine)
        for i in range(2):
            col = base + local + (2 * j + i) * HD
            piece = later[:, i * HD : (i + 1) * HD]
            pack[:, col : col + HD] = rope(norm(piece, qg[...]), cos2, sin2).astype(BF)
    outs.append(pltpu.make_async_copy(pack, pack_h, out_sem.at[2]))
    outs[-1].start()
    for j in range(2):
        at = pl.ds(j * nb, nb)
        send[:, at] = dot(mine[...], wo_v[j]).astype(BF)
        outs.append(pltpu.make_async_copy(send.at[:, at], send_h.at[:, at], out_sem.at[3 + j]))
        outs[-1].start()
    for copy in outs:
        copy.wait()


def cut_points(width):
    step = width // 8
    return [0, step, 2 * step, 4 * step, 6 * step, 8 * step]


def project(n_head, plen, qg, kg, table, x, dec, wq, wk, wv, wo):
    prompts, rows, width = x.shape
    dec_rows = dec.shape[0] * dec.shape[1]
    local = wq.shape[1]
    nb = width // n_head
    every = prompts * rows + dec_rows
    send = (rows, 2 * nb)
    pack = (rows, 2 * prompts * HD + prompts * local)
    chunks = len(cut_points(width)) - 1
    return pl.pallas_call(
        functools.partial(project_kernel, n_head),
        out_shape=[
            jax.ShapeDtypeStruct(send, BF),
            jax.ShapeDtypeStruct(pack, BF),
            jax.ShapeDtypeStruct((dec_rows, local + 2 * HD), F32),
        ],
        in_specs=[HB] * 10,
        out_specs=[HB] * 3,
        scratch_shapes=[
            pltpu.VMEM((every, width), BF),
            pltpu.VMEM(dec.shape, BF),
            pltpu.VMEM((dec_rows, width), F32),
            pltpu.VMEM((width, 2 * HD), BF),
            pltpu.VMEM((width, local), BF),
            pltpu.VMEM((2, local, nb), BF),
            pltpu.VMEM((rows + dec_rows, local), F32),
            pltpu.VMEM((every, 2 * HD), F32),
            pltpu.VMEM(send, BF),
            pltpu.VMEM(pack, BF),
            pltpu.SMEM(plen.shape, jnp.int32),
            pltpu.VMEM(qg.shape, F32),
            pltpu.VMEM(kg.shape, F32),
            pltpu.VMEM(table.shape, F32),
        ]
        + attention_scratch(rows, local // HD)
        + [
            pltpu.SemaphoreType.DMA((2, chunks)),
            pltpu.SemaphoreType.DMA,
            pltpu.SemaphoreType.DMA((2, chunks)),
            pltpu.SemaphoreType.DMA((chunks,)),
            pltpu.SemaphoreType.DMA((2,)),
            pltpu.SemaphoreType.DMA((4,)),
            pltpu.SemaphoreType.DMA((5,)),
        ],
        compiler_params=pltpu.CompilerParams(vmem_limit_bytes=LIMIT_A * MIB),
        cost_estimate=BRIEF,
        name="project",
    )(plen, qg, kg, table, x, dec, wq, wk, wv, wo)


def second_kernel(n_seq, prompts, *refs):
    plen_h, adm_h, clen_h, qg_h, kg_h, pack_h, new_h, cache_h, wo_hbm = refs[:9]
    send, own0, own1, part, blocks, leave = refs[9:15]
    pack, attn, new, cache, wo_v, plen, adm, clen, qg, kg = refs[15:25]
    bias_v, s_v, w_v = refs[25:28]
    pack_sem, small_sem, wo_sem, cache_sem = refs[28:]
    rows = pack.shape[0]
    _, local, nb = wo_v.shape
    seq = lax.axis_index("seq")
    first, second = partners()
    head = lax.axis_index("head")
    pack_copy = pltpu.make_async_copy(pack_h, pack, pack_sem)
    cache_copy = pltpu.make_async_copy(cache_h, cache, cache_sem)
    small = [
        pltpu.make_async_copy(src, dst, small_sem.at[i])
        for i, (src, dst) in enumerate(
            [(plen_h, plen), (adm_h, adm), (clen_h, clen), (qg_h, qg), (kg_h, kg), (new_h, new)]
        )
    ]
    copies = [
        out_copy(wo_hbm, block, nb, wo_v.at[j], wo_sem.at[j])
        for j, block in enumerate((head, second, 3 - head, first))
    ]
    for copy in small + [pack_copy] + copies[:2] + [cache_copy] + copies[2:]:
        copy.start()
    for copy in small:
        copy.wait()
    bias_v[...] = mask_bias(rows, plen[seq * prompts])
    pack_copy.wait()
    both = 2 * HD
    base = prompts * both
    kvs = [pack.at[:, pl.ds(p * both, both)] for p in range(prompts)]
    other = pack.at[:, pl.ds(base, local)]
    queries = pack.at[:, pl.ds(base + local, local)]
    hb = nb // 2

    each = rows // n_seq
    to_row = lax.broadcasted_iota(jnp.int32, (rows, rows), 0)
    from_row = lax.broadcasted_iota(jnp.int32, (rows, rows), 1)
    move = jnp.where(from_row == lax.rem(to_row, each) * n_seq + to_row // each, 1.0, 0.0).astype(BF)
    for p, kv in enumerate(kvs):
        moved = dot(move, kv[...]).astype(BF)
        for d in range(n_seq):
            blocks[d, p * each : (p + 1) * each] = moved[d * each : (d + 1) * each]
    half = n_seq // 2
    leave[...] = blocks[pl.ds((1 - seq // half) * half, half)]
    for j in range(local // both):
        if j in (1, 2):
            copies[j - 1].wait()
            for i in range(2):
                at = slice(i * hb, (i + 1) * hb)
                to = slice((j - 1) * nb + i * hb, (j - 1) * nb + (i + 1) * hb)
                own1[:, to] = dot(other[...], wo_v[j - 1, :, at]).astype(BF)
        attention((2 * j, 2 * j + 1), queries, kvs[0], bias_v, s_v, w_v, attn)
    cache_copy.wait()
    for copy in copies[2:]:
        copy.wait()
    for j in range(2):
        send[:, j * nb : (j + 1) * nb] = dot(attn[...], wo_v[2 + j]).astype(BF)
    decode_attention(
        n_seq, cache.shape[0], plen, adm, clen, new.at[:, pl.ds(0, local)],
        new.at[:, pl.ds(local, both)], kvs, cache, qg, kg, part,
    )
    for j in range(2):
        own0[:, j * nb : (j + 1) * nb] = dot(attn[...], wo_v[j]).astype(BF)


def second(n_head, n_seq, prompts, plen, adm, clen, qg, kg, pack, new, cache, wo):
    rows = pack.shape[0]
    local, width = wo.shape
    nb = width // n_head
    blocks = (n_seq, prompts * rows // n_seq, 2 * HD)
    return pl.pallas_call(
        functools.partial(second_kernel, n_seq, prompts),
        out_shape=[jax.ShapeDtypeStruct((rows, 2 * nb), BF)] * 3
        + [
            jax.ShapeDtypeStruct((new.shape[0] * (local // HD) + 8, HD), F32),
            jax.ShapeDtypeStruct(blocks, BF),
            jax.ShapeDtypeStruct((n_seq // 2,) + blocks[1:], BF),
        ],
        in_specs=[HB] * 9,
        out_specs=[VM] * 6,
        scratch_shapes=[
            pltpu.VMEM(pack.shape, BF),
            pltpu.VMEM((rows, local), BF),
            pltpu.VMEM(new.shape, F32),
            pltpu.VMEM(cache.shape, BF),
            pltpu.VMEM((4, local, nb), BF),
            pltpu.SMEM(plen.shape, jnp.int32),
            pltpu.SMEM(adm.shape, jnp.int32),
            pltpu.SMEM(clen.shape, jnp.int32),
            pltpu.VMEM(qg.shape, F32),
            pltpu.VMEM(kg.shape, F32),
        ]
        + attention_scratch(rows, local // HD)
        + [
            pltpu.SemaphoreType.DMA,
            pltpu.SemaphoreType.DMA((6,)),
            pltpu.SemaphoreType.DMA((4,)),
            pltpu.SemaphoreType.DMA,
        ],
        compiler_params=pltpu.CompilerParams(vmem_limit_bytes=LIMIT_B * MIB),
        cost_estimate=BRIEF,
        name="second",
    )(plen, adm, clen, qg, kg, pack, new, cache, wo)


def joined(bit, mine, other):
    count = mine.shape[0] - 8
    swap = lax.rem(lax.axis_index("seq") // bit, 2) == 1
    one, two = mine[...], other[...]
    low = jnp.where(swap, two, one)
    high = jnp.where(swap, one, two)
    eye = unit(count)

    def column(row):
        return jnp.sum(jnp.where(eye, row, 0.0), axis=1, keepdims=True)

    row_a, row_b = low[count : count + 1, :], high[count : count + 1, :]
    best = jnp.maximum(row_a, row_b)
    scale_a, scale_b = jnp.exp2(row_a - best), jnp.exp2(row_b - best)
    total = scale_a + scale_b
    inverse = 1.0 / total
    mixed = low[:count] * column(scale_a * inverse) + high[:count] * column(scale_b * inverse)
    return mixed, best + jnp.log2(total)


def range_start(seq, size):
    return seq // size * size


def range_start(seq, size):
    return seq // size * size


def join_kernel(bit, mine, other, out):
    count = mine.shape[0] - 8
    mixed, level = joined(bit, mine, other)
    out[:count, :] = mixed
    out[count : count + 1, :] = level


def join(bit, mine, other):
    return pl.pallas_call(
        functools.partial(join_kernel, bit),
        out_shape=jax.ShapeDtypeStruct(mine.shape, F32),
        in_specs=[VM] * 2,
        out_specs=VM,
        compiler_params=pltpu.CompilerParams(vmem_limit_bytes=8 * MIB),
        cost_estimate=BRIEF,
        name="join_%d" % bit,
    )(mine, other)


def hop_kernel(bit, *refs):
    held, leave = refs[:-1], refs[-1]
    seq = lax.axis_index("seq")
    size = bit // 2
    target = range_start(seq, bit) + size * (1 - lax.rem(seq // size, 2))
    at = 0
    for array in held:
        sources, dests = array.shape[:2]
        skip = target - range_start(seq, dests)
        for k in range(sources):
            leave[at] = array[k, pl.ds(skip, size)]
            at += 1


def hop(bit, held):
    sources = sum(array.shape[0] for array in held)
    return pl.pallas_call(
        functools.partial(hop_kernel, bit),
        out_shape=jax.ShapeDtypeStruct((sources, bit // 2) + held[0].shape[2:], BF),
        in_specs=[VM] * len(held),
        out_specs=VM,
        compiler_params=pltpu.CompilerParams(vmem_limit_bytes=8 * MIB),
        cost_estimate=BRIEF,
        name="hop_%d" % bit,
    )(*held)


def pass_on_kernel(own, got, on):
    nb = on.shape[1]
    on[...] = (own[:, nb:].astype(F32) + got[:, :nb].astype(F32)).astype(BF)


def pass_on(p, own, got):
    rows, both = got.shape
    return pl.pallas_call(
        pass_on_kernel,
        out_shape=jax.ShapeDtypeStruct((rows, both // 2), BF),
        in_specs=[VM] * 2,
        out_specs=VM,
        compiler_params=pltpu.CompilerParams(vmem_limit_bytes=8 * MIB),
        cost_estimate=BRIEF,
        name="pass_on_%d" % p,
    )(own, got)


def decode_out_kernel(bit, mine, other, wo_hbm, *refs):
    outs, (wo_v, sems) = refs[:4], refs[4:]
    count = mine.shape[0] - 8
    rows, nb = outs[0].shape
    first, second = partners()
    head = lax.axis_index("head")
    copies = [
        out_copy(wo_hbm, block, nb, wo_v.at[j], sems.at[j])
        for j, block in enumerate((head, second, 3 - head, first))
    ]
    for copy in copies:
        copy.start()
    mixed, _ = joined(bit, mine, other)
    mixed = mixed.astype(BF)
    flat = jnp.concatenate([mixed[i * rows : (i + 1) * rows] for i in range(count // rows)], axis=1)
    for j, out in enumerate(outs):
        copies[j].wait()
        out[...] = dot(flat, wo_v[j]).astype(BF)


def decode_project(bit, n_head, dec_rows, mine, other, wo):
    local, width = wo.shape
    nb = width // n_head
    return pl.pallas_call(
        functools.partial(decode_out_kernel, bit),
        out_shape=[jax.ShapeDtypeStruct((dec_rows, nb), BF)] * 4,
        in_specs=[VM, VM, HB],
        out_specs=[VM] * 4,
        scratch_shapes=[pltpu.VMEM((4, local, nb), BF), pltpu.SemaphoreType.DMA((4,))],
        compiler_params=pltpu.CompilerParams(vmem_limit_bytes=LIMIT_C * MIB),
        cost_estimate=BRIEF,
        name="decode_project",
    )(mine, other, wo)


def sum_parts(stage, out, sems, own, got, last):
    rows, nb = last.shape
    step = rows // 2
    copies = []
    for i in range(2):
        at = pl.ds(i * step, step)
        stage[at] = (
            own[at, :nb].astype(F32) + got[at, nb:].astype(F32) + last[at].astype(F32)
        ).astype(BF)
        copies.append(pltpu.make_async_copy(stage.at[at], out.at[at], sems.at[i]))
        copies[-1].start()
    return copies


def finish_first_kernel(p, bits, own, got, last, *refs):
    held, (out, handed, stage, sems, keep_sem) = refs[: len(bits) + 1], refs[len(bits) + 1 :]
    seq = lax.axis_index("seq")
    copies = []
    sources = [0]
    for j, array in enumerate(held):
        if j:
            sources = sources + [bits[j - 1] ^ source for source in sources]
        for k in range(array.shape[0]):
            source = seq ^ sources[len(copies)]
            copies.append(
                pltpu.make_async_copy(
                    array.at[k, seq - range_start(seq, array.shape[1])],
                    handed.at[source],
                    keep_sem.at[len(copies)],
                )
            )
            copies[-1].start()
    for copy in sum_parts(stage, out.at[p], sems, own, got, last) + copies:
        copy.wait()


def finish_first(p, prompts, bits, own, got, last, held):
    rows, nb = last.shape
    n_seq = held[0].shape[1]
    return pl.pallas_call(
        functools.partial(finish_first_kernel, p, bits),
        out_shape=[
            jax.ShapeDtypeStruct((prompts, rows, nb), BF),
            jax.ShapeDtypeStruct((n_seq,) + held[0].shape[2:], BF),
        ],
        in_specs=[VM] * (3 + len(held)),
        out_specs=[HB] * 2,
        scratch_shapes=[
            pltpu.VMEM((rows, nb), BF),
            pltpu.SemaphoreType.DMA((2,)),
            pltpu.SemaphoreType.DMA((n_seq,)),
        ],
        compiler_params=pltpu.CompilerParams(vmem_limit_bytes=8 * MIB),
        cost_estimate=BRIEF,
        name="finish_%d" % p,
    )(own, got, last, *held)


def finish_last_kernel(p, slots, own, got, last, *refs):
    pieces, (_, out, dec_out, stage, sems) = refs[:-5], refs[-5:]
    copies = sum_parts(stage, out.at[p], sems, own, got, last)
    total = pieces[0][...].astype(F32)
    for piece in pieces[1:]:
        total = total + piece[...].astype(F32)
    for t in range(dec_out.shape[0]):
        dec_out[t] = total[t * slots : (t + 1) * slots].astype(BF)
    for copy in copies:
        copy.wait()


def finish_last(p, steps, slots, own, got, last, pieces, partial):
    rows, nb = last.shape
    return pl.pallas_call(
        functools.partial(finish_last_kernel, p, slots),
        out_shape=[
            jax.ShapeDtypeStruct(partial.shape, BF),
            jax.ShapeDtypeStruct((steps, slots, nb), BF),
        ],
        in_specs=[VM] * (3 + len(pieces)) + [HB],
        out_specs=[HB, VM],
        scratch_shapes=[pltpu.VMEM((rows, nb), BF), pltpu.SemaphoreType.DMA((2,))],
        input_output_aliases={3 + len(pieces): 0},
        compiler_params=pltpu.CompilerParams(vmem_limit_bytes=8 * MIB),
        cost_estimate=BRIEF,
        name="finish_%d" % p,
    )(own, got, last, *pieces, partial)


def after(value, other):
    return lax.optimization_barrier((value, other))[0]


def local(
    prompts, prompt_len, admitted, cache_len, cache_kv, dec_tokens, w_query, w_key, w_value, w_out, q_gain, k_gain
):
    n_seq = lax.axis_size("seq")
    n_head = lax.axis_size("head")
    pr_dev, rows, width = prompts.shape
    steps, slots, _ = dec_tokens.shape
    dec_rows = steps * slots
    each = rows // n_seq
    qg, kg = q_gain.reshape(1, HD), k_gain.reshape(1, HD)
    def head_move(value, masks):
        pairs = [
            (h * n_seq + s, (h ^ masks[s % 2]) * n_seq + s)
            for h in range(n_head)
            for s in range(n_seq)
        ]
        return lax.ppermute(value, ("head", "seq"), pairs)

    def seq_move(value, bit):
        return lax.ppermute(value, "seq", [(i, i ^ bit) for i in range(n_seq)])

    bits = []
    while 2 ** len(bits) < n_seq:
        bits.append(2 ** len(bits))
    bits = bits[::-1]

    table = jnp.asarray(prompt_table(rows))
    send1, pack, new = project(
        n_head, prompt_len, qg, kg, table, prompts, dec_tokens, w_query, w_key, w_value, w_out
    )
    got1 = head_move(send1, (1, 2))
    send0, own0, own1, part, blocks, leave = second(
        n_head, n_seq, pr_dev, prompt_len, admitted, cache_len, qg, kg, pack, new, cache_kv[0], w_out
    )
    got0 = head_move(send0, (1, 2))
    other = seq_move(part, bits[0])
    arrived = seq_move(leave, bits[0])
    for i, bit in enumerate(bits[:-1]):
        part = join(bit, part, other)
        other = seq_move(part, bits[i + 1])
    on1 = pass_on(1, own1, after(got1, part))
    last1 = head_move(on1, (2, 1))
    held = [blocks[None], after(arrived, part)[None]]
    leave = hop(bits[0], held)
    held.append(seq_move(leave, bits[1]))
    got0, other = lax.optimization_barrier((got0, other, on1, leave))[:2]
    on0 = pass_on(0, own0, got0)
    last0 = head_move(on0, (2, 1))
    for i, bit in enumerate(bits[1:-1]):
        leave = hop(bit, held)
        held.append(seq_move(leave, bits[i + 2]))
    other = lax.optimization_barrier((other, on0, leave))[0]
    pieces = decode_project(bits[-1], n_head, dec_rows, part, other, w_out)
    pieces = [
        pieces[0],
        head_move(pieces[1], (2, 1)),
        head_move(pieces[2], (3, 3)),
        head_move(pieces[3], (1, 2)),
    ]
    partial, handed = finish_first(1, pr_dev, bits, own1, got1, last1, held)
    prefill_out, decode_out = finish_last(0, steps, slots, own0, got0, last0, pieces, partial)
    return (prefill_out, handed.reshape(1, pr_dev * n_seq, each, 2 * HD), decode_out)


def solution(mesh):
    placed = (
        P("seq", None, None),
        P(),
        P(),
        P(),
        P("head", None, "seq", None),
        P(),
        P(None, "head"),
        P(None, "head"),
        P(None, "head"),
        P("head", None),
        P(),
        P(),
    )
    return jax.shard_map(
        local,
        mesh=mesh,
        in_specs=placed,
        out_specs=(P("seq", None, "head"), P("head", None, "seq", None), P(None, None, "head")),
        check_vma=False,
    )
```

profile of v0, /device:TPU:0, one launch (start us, length us, event | category | flops | bytes accessed | tf_op | source)
XLA Modules:
  0.0 62.9 jit_solution(8695961011796582122)
XLA Ops:
  0.6 0.0 copy-start.1
  0.6 0.0 copy-start.2
  0.7 0.0 copy-start.3
  0.7 0.0 copy-start.4
  0.7 0.0 copy-start.5
  0.7 12.9 %project.1 = (bf16[256,2048]{1,0:T(8,128)(2,1)}, bf16[256,2560]{1,0:T(8,128)(2,1)}, f32[16,1280]{1,0:T(8,128)}) custom-call(s32[16]{0:T(128)} %refs_0_.3, f32[1,128]{1,0:T(1,128)} %bitcast.12, f32[1,128]{1,0:T(1,128)} %bitcast.14, f32[256,256]{1,0:T(8,128)} %constant.2.clone.refs_3_, bf16[2,256,4096]{2,1,0:T(8,128)(2,1)} %refs_4_.1, ...), custom_call_target="tpu_custom_call" | custom-call | flops 1 | bytes 1 | tf_op jit(solution)/shard_map/project/pallas_call | solution.py:335
  13.6 3.0 %collective-permute-start.4 = (bf16[256,2048]{1,0:T(8,128)(2,1)}, bf16[256,2048]{1,0:T(8,128)(2,1)S(1)}, u32[]{:S(2)}, u32[]{:S(2)}) collective-permute-start(bf16[256,2048]{1,0:T(8,128)(2,1)} %get-tuple-element.31), channel_id=1, source_target_pairs={{0,8},{1,17},{2,10},{3,19},{4,12},{5,21},{6,14},{7,23},{8,0},{9,25... | collective-permute-start | bytes 3145736 | tf_op jit(solution)/shard_map/ppermute | solution.py:718
  16.6 0.0 copy-done.1
  16.6 0.0 copy-done.2
  16.6 0.0 copy-done.3
  16.6 0.0 copy-done.4
  16.7 0.0 copy-done.5
  16.7 0.0 copy-start
  16.7 0.9 %copy-done = f32[16,1280]{1,0:T(8,128)S(1)} copy-done((f32[16,1280]{1,0:T(8,128)S(1)}, f32[16,1280]{1,0:T(8,128)}, u32[]{:S(2)}) %copy-start) | copy-done | bytes 81944
  17.6 10.0 %second.1 = (bf16[256,2048]{1,0:T(8,128)(2,1)S(1)}, bf16[256,2048]{1,0:T(8,128)(2,1)S(1)}, bf16[256,2048]{1,0:T(8,128)(2,1)S(1)}, f32[136,128]{1,0:T(8,128)S(1)}...) custom-call(s32[16]{0:T(128)S(1)} %copy-done.1, s32[4]{0:T(128)S(1)} %copy-done.4, s32[4]{0:T(128)S(1)} %copy-done.5, ...), custom_call_target="tpu_custom_call" | custom-call | flops 1 | bytes 1 | tf_op jit(solution)/shard_map/second/pallas_call | solution.py:448
  27.6 0.1 collective-permute-start
  27.7 3.1 %collective-permute-start.1 = (f32[136,128]{1,0:T(8,128)S(1)}, f32[136,128]{1,0:T(8,128)S(1)}, u32[]{:S(2)}, u32[]{:S(2)}) collective-permute-start(f32[136,128]{1,0:T(8,128)S(1)} %get-tuple-element.29.mine), channel_id=1, source_target_pairs={{0,4},{1,5},{2,6},{3,7},{4,0},{5,1},{6,2},{7,3},{8,12},{9,13},{10,... | collective-permute-start | bytes 208904 | tf_op jit(solution)/shard_map/ppermute | solution.py:721
  30.8 2.7 %collective-permute-done.1.other = f32[136,128]{1,0:T(8,128)S(1)} collective-permute-done((f32[136,128]{1,0:T(8,128)S(1)}, f32[136,128]{1,0:T(8,128)S(1)}, u32[]{:S(2)}, u32[]{:S(2)}) %collective-permute-start.1) | collective-permute-done | bytes 69664 | tf_op jit(solution)/shard_map/ppermute | solution.py:721
  33.5 0.1 join_4.1.mine
  33.6 1.6 %collective-permute-start.2 = (f32[136,128]{1,0:T(8,128)S(1)}, f32[136,128]{1,0:T(8,128)S(1)}, u32[]{:S(2)}, u32[]{:S(2)}) collective-permute-start(f32[136,128]{1,0:T(8,128)S(1)} %join_4.1.mine), channel_id=1, source_target_pairs={{0,2},{1,3},{2,0},{3,1},{4,6},{5,7},{6,4},{7,5},{8,10},{9,11},{10,... | collective-permute-start | bytes 208904 | tf_op jit(solution)/shard_map/ppermute | solution.py:721
  35.2 3.2 %collective-permute-start.5 = (bf16[4,64,256]{2,1,0:T(8,128)(2,1)S(1)}, bf16[4,64,256]{2,1,0:T(8,128)(2,1)S(1)}, u32[]{:S(2)}, u32[]{:S(2)}) collective-permute-start(bf16[4,64,256]{2,1,0:T(8,128)(2,1)S(1)} %get-tuple-element.34), channel_id=1, source_target_pairs={{0,4},{1,5},{2,6},{3,7},{4,0},{5,1},{6,2},{7,3},{8,12},{9,13},{10,... | collective-permute-start | bytes 393224 | tf_op jit(solution)/shard_map/ppermute | solution.py:721
  38.4 0.0 collective-permute-done.2.other
  38.4 0.1 join_2.1.mine
  38.6 0.1 collective-permute-start.3
  38.6 4.1 %collective-permute-done.5 = bf16[4,64,256]{2,1,0:T(8,128)(2,1)S(1)} collective-permute-done((bf16[4,64,256]{2,1,0:T(8,128)(2,1)S(1)}, bf16[4,64,256]{2,1,0:T(8,128)(2,1)S(1)}, u32[]{:S(2)}, u32[]{:S(2)}) %collective-permute-start.5) | collective-permute-done | bytes 131104 | tf_op jit(solution)/shard_map/ppermute | solution.py:721
  42.8 0.0 collective-permute-done.4.got
  42.8 0.1 pass_on_1.1
  42.9 1.6 %collective-permute-start.11 = (bf16[256,1024]{1,0:T(8,128)(2,1)S(1)}, bf16[256,1024]{1,0:T(8,128)(2,1)S(1)}, u32[]{:S(2)}, u32[]{:S(2)}) collective-permute-start(bf16[256,1024]{1,0:T(8,128)(2,1)S(1)} %pass_on_1.1), channel_id=1, source_target_pairs={{0,16},{1,9},{2,18},{3,11},{4,20},{5,13},{6,22},{7,15},{8,24},{9,1... | collective-permute-start | bytes 1572872 | tf_op jit(solution)/shard_map/ppermute | solution.py:718
  44.5 0.0 collective-permute-done.3.other
  44.5 0.0 collective-permute-done.got
  44.5 0.1 pass_on_0.1
  44.7 0.6 collective-permute-start.6
  45.2 0.8 %collective-permute-start.7 = (bf16[2,2,64,256]{3,2,1,0:T(8,128)(2,1)S(1)}, bf16[2,2,64,256]{3,2,1,0:T(8,128)(2,1)S(1)}, u32[]{:S(2)}, u32[]{:S(2)}) collective-permute-start(bf16[2,2,64,256]{3,2,1,0:T(8,128)(2,1)S(1)} %hop_4.1), channel_id=1, source_target_pairs={{0,2},{1,3},{2,0},{3,1},{4,6},{5,7},{6,4},{7,5},{8,10},{9,11},{10,... | collective-permute-start | bytes 393224 | tf_op jit(solution)/shard_map/ppermute | solution.py:721
  46.1 4.1 %collective-permute-done.7.refs_2_ = bf16[2,2,64,256]{3,2,1,0:T(8,128)(2,1)S(1)} collective-permute-done((bf16[2,2,64,256]{3,2,1,0:T(8,128)(2,1)S(1)}, bf16[2,2,64,256]{3,2,1,0:T(8,128)(2,1)S(1)}, u32[]{:S(2)}, u32[]{:S(2)}) %collective-permute-start.7) | collective-permute-done | bytes 131104 | tf_op jit(solution)/shard_map/ppermute | solution.py:721
  50.2 0.1 collective-permute-start.12
  50.3 3.9 %decode_project.1 = (bf16[16,1024]{1,0:T(8,128)(2,1)S(1)}, bf16[16,1024]{1,0:T(8,128)(2,1)S(1)}, bf16[16,1024]{1,0:T(8,128)(2,1)S(1)}, bf16[16,1024]{1,0:T(8,128)(2,1)S(1)}) custom-call(f32[136,128]{1,0:T(8,128)S(1)} %join_2.1.mine, f32[136,128]{1,0:T(8,128)S(1)} %collective-permute-done.3.other, bf16[1024,4096]{1,0:T(8,128)(2,1)} %wo_hbm.1), custom_call_target="tpu_custom_call" | custom-call | flops 1 | bytes 1 | tf_op jit(solution)/shard_map/decode_project/pallas_call | solution.py:598
  54.2 1.6 %collective-permute-start.8 = (bf16[16,1024]{1,0:T(8,128)(2,1)S(1)}, bf16[16,1024]{1,0:T(8,128)(2,1)S(1)}, u32[]{:S(2)}, u32[]{:S(2)}) collective-permute-start(bf16[16,1024]{1,0:T(8,128)(2,1)S(1)} %get-tuple-element.40), channel_id=1, source_target_pairs={{0,16},{1,9},{2,18},{3,11},{4,20},{5,13},{6,22},{7,15},{8,24},{9,1... | collective-permute-start | bytes 98312 | tf_op jit(solution)/shard_map/ppermute | solution.py:718
  55.8 1.4 %collective-permute-start.9 = (bf16[16,1024]{1,0:T(8,128)(2,1)S(1)}, bf16[16,1024]{1,0:T(8,128)(2,1)S(1)}, u32[]{:S(2)}, u32[]{:S(2)}) collective-permute-start(bf16[16,1024]{1,0:T(8,128)(2,1)S(1)} %get-tuple-element.41), channel_id=1, source_target_pairs={{0,24},{1,25},{2,26},{3,27},{4,28},{5,29},{6,30},{7,31},{8,16},{9,... | collective-permute-start | bytes 98312 | tf_op jit(solution)/shard_map/ppermute | solution.py:718
  57.2 0.0 collective-permute-done.12.refs_3_
  57.3 0.5 collective-permute-start.10
  57.8 0.0 collective-permute-done.11.last
  57.8 1.0 %finish_1.1 = (bf16[2,256,1024]{2,1,0:T(8,128)(2,1)}, bf16[8,64,256]{2,1,0:T(8,128)(2,1)}) custom-call(bf16[256,2048]{1,0:T(8,128)(2,1)S(1)} %get-tuple-element.30.own, bf16[256,2048]{1,0:T(8,128)(2,1)S(1)} %collective-permute-done.4.got, bf16[256,1024]{1,0:T(8,128)(2,1)S(1)} %collective-permute-done.11.last, bf16[1,8,64,256]{3,2,1,0:T(8,128)(2,1)S(1)} %bitcast.8, ...), custom_call_target="tpu_custom_call" | custom-call | flops 1 | bytes 1 | tf_op jit(solution)/shard_map/finish_1/pallas_call | solution.py:649
  58.8 0.0 collective-permute-done.8.refs_1_
  58.8 1.8 %collective-permute-done.9.refs_2_ = bf16[16,1024]{1,0:T(8,128)(2,1)S(1)} collective-permute-done((bf16[16,1024]{1,0:T(8,128)(2,1)S(1)}, bf16[16,1024]{1,0:T(8,128)(2,1)S(1)}, u32[]{:S(2)}, u32[]{:S(2)}) %collective-permute-start.9) | collective-permute-done | bytes 32800 | tf_op jit(solution)/shard_map/ppermute | solution.py:718
  60.6 0.5 collective-permute-done.10.refs_3_
  61.2 0.0 collective-permute-done.6.last
  61.2 1.5 %finish_0.1 = (bf16[2,256,1024]{2,1,0:T(8,128)(2,1)}, bf16[4,4,1024]{2,1,0:T(4,128)(2,1)}) custom-call(bf16[256,2048]{1,0:T(8,128)(2,1)S(1)} %get-tuple-element.27.own, bf16[256,2048]{1,0:T(8,128)(2,1)S(1)} %collective-permute-done.got, bf16[256,1024]{1,0:T(8,128)(2,1)S(1)} %collective-permute-done.6.last, ...), custom_call_target="tpu_custom_call", output_to_operand_aliasing={{0}: (7, {})} | custom-call | flops 1 | bytes 1 | tf_op jit(solution)/shard_map/finish_0/pallas_call | solution.py:682
  (2 shorter events, 0.0 us)
Async XLA Ops:
  0.6 16.0 %copy-start.1 = (s32[16]{0:T(128)S(1)}, s32[16]{0:T(128)}, u32[]{:S(2)}) copy-start(s32[16]{0:T(128)} %refs_0_.3) | copy-start | bytes 196
  0.6 16.0 %copy-start.2 = (f32[128]{0:T(128)S(1)}, f32[128]{0:T(128)}, u32[]{:S(2)}) copy-start(f32[128]{0:T(128)} %param.23) | copy-start | bytes 1540
  0.7 16.0 %copy-start.3 = (f32[128]{0:T(128)S(1)}, f32[128]{0:T(128)}, u32[]{:S(2)}) copy-start(f32[128]{0:T(128)} %param.24) | copy-start | bytes 1540
  0.7 16.0 %copy-start.4 = (s32[4]{0:T(128)S(1)}, s32[4]{0:T(128)}, u32[]{:S(2)}) copy-start(s32[4]{0:T(128)} %refs_1_.1) | copy-start | bytes 52
  0.7 16.0 %copy-start.5 = (s32[4]{0:T(128)S(1)}, s32[4]{0:T(128)}, u32[]{:S(2)}) copy-start(s32[4]{0:T(128)} %refs_2_.1) | copy-start | bytes 52
  13.6 29.1 %collective-permute-start.4 = (bf16[256,2048]{1,0:T(8,128)(2,1)}, bf16[256,2048]{1,0:T(8,128)(2,1)S(1)}, u32[]{:S(2)}, u32[]{:S(2)}) collective-permute-start(bf16[256,2048]{1,0:T(8,128)(2,1)} %get-tuple-element.31), channel_id=1, source_target_pairs={{0,8},{1,17},{2,10},{3,19},{4,12},{5,21},{6,14},{7,23},{8,0},{9,25... | collective-permute-start | bytes 3145736 | tf_op jit(solution)/shard_map/ppermute | solution.py:718
  16.7 0.9 %copy-start = (f32[16,1280]{1,0:T(8,128)S(1)}, f32[16,1280]{1,0:T(8,128)}, u32[]{:S(2)}) copy-start(f32[16,1280]{1,0:T(8,128)} %get-tuple-element.26.refs_6_) | copy-start | bytes 245764
  27.6 16.9 %collective-permute-start = (bf16[256,2048]{1,0:T(8,128)(2,1)S(1)}, bf16[256,2048]{1,0:T(8,128)(2,1)S(1)}, u32[]{:S(2)}, u32[]{:S(2)}) collective-permute-start(bf16[256,2048]{1,0:T(8,128)(2,1)S(1)} %get-tuple-element.28), channel_id=1, source_target_pairs={{0,8},{1,17},{2,10},{3,19},{4,12},{5,21},{6,14},{7,23},{8,0},{9,25... | collective-permute-start | bytes 3145736 | tf_op jit(solution)/shard_map/ppermute | solution.py:718
  27.7 5.8 %collective-permute-start.1 = (f32[136,128]{1,0:T(8,128)S(1)}, f32[136,128]{1,0:T(8,128)S(1)}, u32[]{:S(2)}, u32[]{:S(2)}) collective-permute-start(f32[136,128]{1,0:T(8,128)S(1)} %get-tuple-element.29.mine), channel_id=1, source_target_pairs={{0,4},{1,5},{2,6},{3,7},{4,0},{5,1},{6,2},{7,3},{8,12},{9,13},{10,... | collective-permute-start | bytes 208904 | tf_op jit(solution)/shard_map/ppermute | solution.py:721
  33.6 4.8 %collective-permute-start.2 = (f32[136,128]{1,0:T(8,128)S(1)}, f32[136,128]{1,0:T(8,128)S(1)}, u32[]{:S(2)}, u32[]{:S(2)}) collective-permute-start(f32[136,128]{1,0:T(8,128)S(1)} %join_4.1.mine), channel_id=1, source_target_pairs={{0,2},{1,3},{2,0},{3,1},{4,6},{5,7},{6,4},{7,5},{8,10},{9,11},{10,... | collective-permute-start | bytes 208904 | tf_op jit(solution)/shard_map/ppermute | solution.py:721
  35.2 7.6 %collective-permute-start.5 = (bf16[4,64,256]{2,1,0:T(8,128)(2,1)S(1)}, bf16[4,64,256]{2,1,0:T(8,128)(2,1)S(1)}, u32[]{:S(2)}, u32[]{:S(2)}) collective-permute-start(bf16[4,64,256]{2,1,0:T(8,128)(2,1)S(1)} %get-tuple-element.34), channel_id=1, source_target_pairs={{0,4},{1,5},{2,6},{3,7},{4,0},{5,1},{6,2},{7,3},{8,12},{9,13},{10,... | collective-permute-start | bytes 393224 | tf_op jit(solution)/shard_map/ppermute | solution.py:721
  38.6 6.0 %collective-permute-start.3 = (f32[136,128]{1,0:T(8,128)S(1)}, f32[136,128]{1,0:T(8,128)S(1)}, u32[]{:S(2)}, u32[]{:S(2)}) collective-permute-start(f32[136,128]{1,0:T(8,128)S(1)} %join_2.1.mine), channel_id=1, source_target_pairs={{0,1},{1,0},{2,3},{3,2},{4,5},{5,4},{6,7},{7,6},{8,9},{9,8},{10,11... | collective-permute-start | bytes 208904 | tf_op jit(solution)/shard_map/ppermute | solution.py:721
  42.9 14.9 %collective-permute-start.11 = (bf16[256,1024]{1,0:T(8,128)(2,1)S(1)}, bf16[256,1024]{1,0:T(8,128)(2,1)S(1)}, u32[]{:S(2)}, u32[]{:S(2)}) collective-permute-start(bf16[256,1024]{1,0:T(8,128)(2,1)S(1)} %pass_on_1.1), channel_id=1, source_target_pairs={{0,16},{1,9},{2,18},{3,11},{4,20},{5,13},{6,22},{7,15},{8,24},{9,1... | collective-permute-start | bytes 1572872 | tf_op jit(solution)/shard_map/ppermute | solution.py:718
  44.7 16.5 %collective-permute-start.6 = (bf16[256,1024]{1,0:T(8,128)(2,1)S(1)}, bf16[256,1024]{1,0:T(8,128)(2,1)S(1)}, u32[]{:S(2)}, u32[]{:S(2)}) collective-permute-start(bf16[256,1024]{1,0:T(8,128)(2,1)S(1)} %pass_on_0.1), channel_id=1, source_target_pairs={{0,16},{1,9},{2,18},{3,11},{4,20},{5,13},{6,22},{7,15},{8,24},{9,1... | collective-permute-start | bytes 1572872 | tf_op jit(solution)/shard_map/ppermute | solution.py:718
  45.2 5.0 %collective-permute-start.7 = (bf16[2,2,64,256]{3,2,1,0:T(8,128)(2,1)S(1)}, bf16[2,2,64,256]{3,2,1,0:T(8,128)(2,1)S(1)}, u32[]{:S(2)}, u32[]{:S(2)}) collective-permute-start(bf16[2,2,64,256]{3,2,1,0:T(8,128)(2,1)S(1)} %hop_4.1), channel_id=1, source_target_pairs={{0,2},{1,3},{2,0},{3,1},{4,6},{5,7},{6,4},{7,5},{8,10},{9,11},{10,... | collective-permute-start | bytes 393224 | tf_op jit(solution)/shard_map/ppermute | solution.py:721
  50.2 7.0 %collective-permute-start.12 = (bf16[4,1,64,256]{3,2,1,0:T(8,128)(2,1)S(1)}, bf16[4,1,64,256]{3,2,1,0:T(8,128)(2,1)S(1)}, u32[]{:S(2)}, u32[]{:S(2)}) collective-permute-start(bf16[4,1,64,256]{3,2,1,0:T(8,128)(2,1)S(1)} %hop_2.1), channel_id=1, source_target_pairs={{0,1},{1,0},{2,3},{3,2},{4,5},{5,4},{6,7},{7,6},{8,9},{9,8},{10,11... | collective-permute-start | bytes 393224 | tf_op jit(solution)/shard_map/ppermute | solution.py:721
  54.2 4.6 %collective-permute-start.8 = (bf16[16,1024]{1,0:T(8,128)(2,1)S(1)}, bf16[16,1024]{1,0:T(8,128)(2,1)S(1)}, u32[]{:S(2)}, u32[]{:S(2)}) collective-permute-start(bf16[16,1024]{1,0:T(8,128)(2,1)S(1)} %get-tuple-element.40), channel_id=1, source_target_pairs={{0,16},{1,9},{2,18},{3,11},{4,20},{5,13},{6,22},{7,15},{8,24},{9,1... | collective-permute-start | bytes 98312 | tf_op jit(solution)/shard_map/ppermute | solution.py:718
  55.8 4.8 %collective-permute-start.9 = (bf16[16,1024]{1,0:T(8,128)(2,1)S(1)}, bf16[16,1024]{1,0:T(8,128)(2,1)S(1)}, u32[]{:S(2)}, u32[]{:S(2)}) collective-permute-start(bf16[16,1024]{1,0:T(8,128)(2,1)S(1)} %get-tuple-element.41), channel_id=1, source_target_pairs={{0,24},{1,25},{2,26},{3,27},{4,28},{5,29},{6,30},{7,31},{8,16},{9,... | collective-permute-start | bytes 98312 | tf_op jit(solution)/shard_map/ppermute | solution.py:718
  57.3 3.9 %collective-permute-start.10 = (bf16[16,1024]{1,0:T(8,128)(2,1)S(1)}, bf16[16,1024]{1,0:T(8,128)(2,1)S(1)}, u32[]{:S(2)}, u32[]{:S(2)}) collective-permute-start(bf16[16,1024]{1,0:T(8,128)(2,1)S(1)} %get-tuple-element.42), channel_id=1, source_target_pairs={{0,8},{1,17},{2,10},{3,19},{4,12},{5,21},{6,14},{7,23},{8,0},{9,25... | collective-permute-start | bytes 98312 | tf_op jit(solution)/shard_map/ppermute | solution.py:718
where the time goes:
time: 63 us; the launch traced here: 62.9 us
  Pallas kernels  30 us (48%)
  starting transfers between devices  17.7 us (28%)
  waiting for transfers between devices  13.3 us (21%)
  between operations  0.96 us (2%)
  local copies, waits for them, and re-layouts  0.9 us (1%)
    pallas_call x1, Pallas kernels, project(): pl.pallas_call(functools.partial(project_kernel, n_head), out_shape=[jax....  12.9 us
    ppermute x6, waiting for transfers between devices, seq_move(): return lax.ppermute(value, 'seq', [(i, i ^ bit) for i in range(n_seq)])  11 us
    pallas_call x1, Pallas kernels, second(): pl.pallas_call(functools.partial(second_kernel, n_seq, prompts), out_shap...  10 us
    ppermute x6, starting transfers between devices, seq_move(): return lax.ppermute(value, 'seq', [(i, i ^ bit) for i in range(n_seq)])  8.85 us
    ppermute x7, starting transfers between devices, head_move(): return lax.ppermute(value, ('head', 'seq'), pairs)  8.82 us
    pallas_call x1, Pallas kernels, decode_project(): pl.pallas_call(functools.partial(decode_out_kernel, bit), out_shape=[jax....  3.93 us
    ppermute x7, waiting for transfers between devices, head_move(): return lax.ppermute(value, ('head', 'seq'), pairs)  2.36 us
    pallas_call x1, Pallas kernels, finish_last(): pl.pallas_call(functools.partial(finish_last_kernel, p, slots), out_shape...  1.54 us
  transfers between devices with their start and end apart: 13, of which 5 were waited for; matrix products, arithmetic and copies ran while one was open for 0% of the time, Pallas kernels for 25%

commit v1 on v0

--- a/solution.py
+++ b/solution.py
@@ -23,7 +23,7 @@
 MIB = 1024 * 1024
 LIMIT_A = 60
 LIMIT_B = 50
-LIMIT_C = 50
+LIMIT_C = 42
 
 
 def frequencies():
@@ -142,23 +142,20 @@
     )
 
 
-def decode_attention(n_seq, slots, plen, adm, clen, raw, raw_kv, kvs, cache, qg, kg, part):
+def decode_places(plen, adm, clen, slots, dec_rows):
+    eff = effective_lengths(plen, adm, clen, slots)
+    row = lax.broadcasted_iota(jnp.int32, (dec_rows, HD), 0)
+    return by_slot(lax.rem(row, slots), eff) + row // slots
+
+
+def decode_attention(n_seq, slots, plen, adm, clen, rotated, new, kvs, cache, part):
     seq = lax.axis_index("seq")
-    dec_rows = raw.shape[0]
+    dec_rows = rotated.shape[0]
     width = cache.shape[1]
     rows = kvs[0].shape[0]
-    eff = effective_lengths(plen, adm, clen, slots)
-    row = lax.broadcasted_iota(jnp.int32, (dec_rows, HD), 0)
-    places = by_slot(lax.rem(row, slots), eff) + row // slots
-    cos2, sin2 = cos_sin(places, turns(row))
-    new_key = rope(norm(raw_kv[:, :HD], kg[...]), cos2, sin2).astype(BF)
-    new_value = raw_kv[:, HD:].astype(BF)
+    new_key, new_value = new[:, :HD], new[:, HD:]
     queries = jnp.concatenate(
-        [
-            rope(norm(raw[:, h * HD : (h + 1) * HD], qg[...]), cos2, sin2).astype(BF)
-            for h in range(raw.shape[1] // HD)
-        ],
-        axis=0,
+        [rotated[:, h * HD : (h + 1) * HD] for h in range(rotated.shape[1] // HD)], axis=0
     )
     count = queries.shape[0]
 
@@ -203,13 +200,13 @@
     part[count : count + 1, :] = jnp.sum(jnp.where(unit(count), level, 0.0), axis=0, keepdims=True)
 
 
-def project_kernel(n_head, *refs):
-    plen_h, qg_h, kg_h, table_h, x_hbm, dec_hbm, wq_hbm, wk_hbm, wv_hbm, wo_hbm = refs[:10]
-    send_h, pack_h, new_h = refs[10:13]
-    x_v, dec_v, flat_v, wkv_v, wq_v, wo_v, raw, raw_kv, send, pack = refs[13:23]
-    plen, qg, kg, table = refs[23:27]
-    bias_v, s_v, w_v = refs[27:30]
-    x_sem, dec_sem, wkv_sem, wq_sem, wo_sem, small_sem, out_sem = refs[30:]
+def project_kernel(n_head, n_seq, *refs):
+    plen_h, adm_h, clen_h, qg_h, kg_h, table_h, x_hbm, dec_hbm, wq_hbm, wk_hbm, wv_hbm, wo_hbm = refs[:12]
+    send_h, pack_h, blocks_h, leave_h = refs[12:16]
+    x_v, dec_v, flat_v, wkv_v, wq_v, wo_v, raw, raw_kv, send, pack, blocks = refs[16:27]
+    plen, adm, clen, qg, kg, table = refs[27:33]
+    bias_v, s_v, w_v = refs[33:36]
+    x_sem, dec_sem, wkv_sem, wq_sem, wo_sem, small_sem, out_sem = refs[36:]
     prompts, rows, width = x_hbm.shape
     steps, slots, _ = dec_hbm.shape
     dec_rows = steps * slots
@@ -241,7 +238,7 @@
     small = [
         pltpu.make_async_copy(src, dst, small_sem.at[i])
         for i, (src, dst) in enumerate(
-            [(plen_h, plen), (qg_h, qg), (kg_h, kg), (table_h, table)]
+            [(plen_h, plen), (qg_h, qg), (kg_h, kg), (table_h, table), (adm_h, adm), (clen_h, clen)]
         )
     ]
     dec_copy = pltpu.make_async_copy(dec_hbm, dec_v, dec_sem)
@@ -279,23 +276,42 @@
             raw[...] += q_part
     cos2, sin2 = table[:, :HD], table[:, HD:]
     both = 2 * HD
-    kvs = [pack.at[:, pl.ds(p * both, both)] for p in range(prompts)]
+    base = prompts * both
+    whole = pl.ds(0, rows)
+    kvs = [pack.at[whole, pl.ds(p * both, both)] for p in range(prompts)]
     for p, start in ((lead, 0), (0, front)):
         at = slice(start, start + rows)
         kvs[p][:, :HD] = rope(norm(raw_kv[at, :HD], kg[...]), cos2, sin2).astype(BF)
         kvs[p][:, HD:] = raw_kv[at, HD:].astype(BF)
+    each = rows // n_seq
+    to_row = lax.broadcasted_iota(jnp.int32, (rows, rows), 0)
+    from_row = lax.broadcasted_iota(jnp.int32, (rows, rows), 1)
+    move = jnp.where(from_row == lax.rem(to_row, each) * n_seq + to_row // each, 1.0, 0.0).astype(BF)
+    for p, kv in enumerate(kvs):
+        moved = dot(move, kv[...]).astype(BF)
+        for d in range(n_seq):
+            blocks[d, p * each : (p + 1) * each] = moved[d * each : (d + 1) * each]
+    half = n_seq // 2
+    away = (1 - seq // half) * half
     outs = [
-        pltpu.make_async_copy(raw.at[pl.ds(rows, dec_rows)], new_h.at[:, pl.ds(0, local)], out_sem.at[0]),
-        pltpu.make_async_copy(
-            raw_kv.at[pl.ds(rows, dec_rows)], new_h.at[:, pl.ds(local, both)], out_sem.at[1]
-        ),
+        pltpu.make_async_copy(blocks, blocks_h, out_sem.at[0]),
+        pltpu.make_async_copy(blocks.at[pl.ds(away, half)], leave_h, out_sem.at[1]),
     ]
     for copy in outs:
         copy.start()
+    places = decode_places(plen, adm, clen, slots, dec_rows)
+    dcos2, dsin2 = cos_sin(places, turns(places))
+    new_at = slice(rows, front)
+    pack[new_at, :] = jnp.zeros((dec_rows, pack.shape[1]), BF)
+    pack[new_at, :HD] = rope(norm(raw_kv[new_at, :HD], kg[...]), dcos2, dsin2).astype(BF)
+    pack[new_at, HD:both] = raw_kv[new_at, HD:].astype(BF)
+    for h in range(local // HD):
+        piece = raw[new_at, h * HD : (h + 1) * HD]
+        col = base + h * HD
+        pack[new_at, col : col + HD] = rope(norm(piece, qg[...]), dcos2, dsin2).astype(BF)
     for copy in o_copies:
         copy.wait()
-    base = prompts * both
-    mine = pack.at[:, pl.ds(base, local)]
+    mine = pack.at[whole, pl.ds(base, local)]
     pair = 2 * HD
     for j in range(local // pair):
         later = dot(x_v[front:, :], wq_v[:, j * pair : (j + 1) * pair])
@@ -306,7 +322,7 @@
         for i in range(2):
             col = base + local + (2 * j + i) * HD
             piece = later[:, i * HD : (i + 1) * HD]
-            pack[:, col : col + HD] = rope(norm(piece, qg[...]), cos2, sin2).astype(BF)
+            pack[:rows, col : col + HD] = rope(norm(piece, qg[...]), cos2, sin2).astype(BF)
     outs.append(pltpu.make_async_copy(pack, pack_h, out_sem.at[2]))
     outs[-1].start()
     for j in range(2):
@@ -323,24 +339,26 @@
     return [0, step, 2 * step, 4 * step, 6 * step, 8 * step]
 
 
-def project(n_head, plen, qg, kg, table, x, dec, wq, wk, wv, wo):
+def project(n_head, n_seq, plen, adm, clen, qg, kg, table, x, dec, wq, wk, wv, wo):
     prompts, rows, width = x.shape
     dec_rows = dec.shape[0] * dec.shape[1]
     local = wq.shape[1]
     nb = width // n_head
     every = prompts * rows + dec_rows
     send = (rows, 2 * nb)
-    pack = (rows, 2 * prompts * HD + prompts * local)
+    pack = (rows + dec_rows, 2 * prompts * HD + prompts * local)
+    blocks = (n_seq, prompts * rows // n_seq, 2 * HD)
     chunks = len(cut_points(width)) - 1
     return pl.pallas_call(
-        functools.partial(project_kernel, n_head),
+        functools.partial(project_kernel, n_head, n_seq),
         out_shape=[
             jax.ShapeDtypeStruct(send, BF),
             jax.ShapeDtypeStruct(pack, BF),
-            jax.ShapeDtypeStruct((dec_rows, local + 2 * HD), F32),
+            jax.ShapeDtypeStruct(blocks, BF),
+            jax.ShapeDtypeStruct((n_seq // 2,) + blocks[1:], BF),
         ],
-        in_specs=[HB] * 10,
-        out_specs=[HB] * 3,
+        in_specs=[HB] * 12,
+        out_specs=[HB] * 4,
         scratch_shapes=[
             pltpu.VMEM((every, width), BF),
             pltpu.VMEM(dec.shape, BF),
@@ -352,7 +370,10 @@
             pltpu.VMEM((every, 2 * HD), F32),
             pltpu.VMEM(send, BF),
             pltpu.VMEM(pack, BF),
+            pltpu.VMEM(blocks, BF),
             pltpu.SMEM(plen.shape, jnp.int32),
+            pltpu.SMEM(adm.shape, jnp.int32),
+            pltpu.SMEM(clen.shape, jnp.int32),
             pltpu.VMEM(qg.shape, F32),
             pltpu.VMEM(kg.shape, F32),
             pltpu.VMEM(table.shape, F32),
@@ -364,22 +385,23 @@
             pltpu.SemaphoreType.DMA((2, chunks)),
             pltpu.SemaphoreType.DMA((chunks,)),
             pltpu.SemaphoreType.DMA((2,)),
-            pltpu.SemaphoreType.DMA((4,)),
+            pltpu.SemaphoreType.DMA((6,)),
             pltpu.SemaphoreType.DMA((5,)),
         ],
         compiler_params=pltpu.CompilerParams(vmem_limit_bytes=LIMIT_A * MIB),
         cost_estimate=BRIEF,
         name="project",
-    )(plen, qg, kg, table, x, dec, wq, wk, wv, wo)
+    )(plen, adm, clen, qg, kg, table, x, dec, wq, wk, wv, wo)
 
 
 def second_kernel(n_seq, prompts, *refs):
-    plen_h, adm_h, clen_h, qg_h, kg_h, pack_h, new_h, cache_h, wo_hbm = refs[:9]
-    send, own0, own1, part, blocks, leave = refs[9:15]
-    pack, attn, new, cache, wo_v, plen, adm, clen, qg, kg = refs[15:25]
-    bias_v, s_v, w_v = refs[25:28]
-    pack_sem, small_sem, wo_sem, cache_sem = refs[28:]
-    rows = pack.shape[0]
+    plen_h, adm_h, clen_h, pack_h, cache_h, wo_hbm = refs[:6]
+    send, attn, own1, part = refs[6:10]
+    pack, cache, wo_v, plen, adm, clen = refs[10:16]
+    bias_v, s_v, w_v = refs[16:19]
+    pack_sem, small_sem, wo_sem, cache_sem = refs[19:]
+    rows = attn.shape[0]
+    dec_rows = pack.shape[0] - rows
     _, local, nb = wo_v.shape
     seq = lax.axis_index("seq")
     first, second = partners()
@@ -388,9 +410,7 @@
     cache_copy = pltpu.make_async_copy(cache_h, cache, cache_sem)
     small = [
         pltpu.make_async_copy(src, dst, small_sem.at[i])
-        for i, (src, dst) in enumerate(
-            [(plen_h, plen), (adm_h, adm), (clen_h, clen), (qg_h, qg), (kg_h, kg), (new_h, new)]
-        )
+        for i, (src, dst) in enumerate([(plen_h, plen), (adm_h, adm), (clen_h, clen)])
     ]
     copies = [
         out_copy(wo_hbm, block, nb, wo_v.at[j], wo_sem.at[j])
@@ -404,21 +424,12 @@
     pack_copy.wait()
     both = 2 * HD
     base = prompts * both
-    kvs = [pack.at[:, pl.ds(p * both, both)] for p in range(prompts)]
-    other = pack.at[:, pl.ds(base, local)]
-    queries = pack.at[:, pl.ds(base + local, local)]
+    whole = pl.ds(0, rows)
+    kvs = [pack.at[whole, pl.ds(p * both, both)] for p in range(prompts)]
+    other = pack.at[whole, pl.ds(base, local)]
+    queries = pack.at[whole, pl.ds(base + local, local)]
     hb = nb // 2
 
-    each = rows // n_seq
-    to_row = lax.broadcasted_iota(jnp.int32, (rows, rows), 0)
-    from_row = lax.broadcasted_iota(jnp.int32, (rows, rows), 1)
-    move = jnp.where(from_row == lax.rem(to_row, each) * n_seq + to_row // each, 1.0, 0.0).astype(BF)
-    for p, kv in enumerate(kvs):
-        moved = dot(move, kv[...]).astype(BF)
-        for d in range(n_seq):
-            blocks[d, p * each : (p + 1) * each] = moved[d * each : (d + 1) * each]
-    half = n_seq // 2
-    leave[...] = blocks[pl.ds((1 - seq // half) * half, half)]
     for j in range(local // both):
         if j in (1, 2):
             copies[j - 1].wait()
@@ -433,51 +444,79 @@
     for j in range(2):
         send[:, j * nb : (j + 1) * nb] = dot(attn[...], wo_v[2 + j]).astype(BF)
     decode_attention(
-        n_seq, cache.shape[0], plen, adm, clen, new.at[:, pl.ds(0, local)],
-        new.at[:, pl.ds(local, both)], kvs, cache, qg, kg, part,
+        n_seq, cache.shape[0], plen, adm, clen, pack.at[pl.ds(rows, dec_rows), pl.ds(base, local)],
+        pack.at[pl.ds(rows, dec_rows), pl.ds(0, both)], kvs, cache, part,
     )
-    for j in range(2):
-        own0[:, j * nb : (j + 1) * nb] = dot(attn[...], wo_v[j]).astype(BF)
-
-
-def second(n_head, n_seq, prompts, plen, adm, clen, qg, kg, pack, new, cache, wo):
-    rows = pack.shape[0]
+
+
+def second(n_head, n_seq, prompts, rows, plen, adm, clen, pack, cache, wo):
     local, width = wo.shape
     nb = width // n_head
-    blocks = (n_seq, prompts * rows // n_seq, 2 * HD)
+    dec_rows = pack.shape[0] - rows
     return pl.pallas_call(
         functools.partial(second_kernel, n_seq, prompts),
-        out_shape=[jax.ShapeDtypeStruct((rows, 2 * nb), BF)] * 3
-        + [
-            jax.ShapeDtypeStruct((new.shape[0] * (local // HD) + 8, HD), F32),
-            jax.ShapeDtypeStruct(blocks, BF),
-            jax.ShapeDtypeStruct((n_seq // 2,) + blocks[1:], BF),
+        out_shape=[
+            jax.ShapeDtypeStruct((rows, 2 * nb), BF),
+            jax.ShapeDtypeStruct((rows, local), BF),
+            jax.ShapeDtypeStruct((rows, 2 * nb), BF),
+            jax.ShapeDtypeStruct((dec_rows * (local // HD) + 8, HD), F32),
         ],
-        in_specs=[HB] * 9,
-        out_specs=[VM] * 6,
+        in_specs=[HB] * 6,
+        out_specs=[VM] * 4,
         scratch_shapes=[
             pltpu.VMEM(pack.shape, BF),
-            pltpu.VMEM((rows, local), BF),
-            pltpu.VMEM(new.shape, F32),
             pltpu.VMEM(cache.shape, BF),
             pltpu.VMEM((4, local, nb), BF),
             pltpu.SMEM(plen.shape, jnp.int32),
             pltpu.SMEM(adm.shape, jnp.int32),
             pltpu.SMEM(clen.shape, jnp.int32),
-            pltpu.VMEM(qg.shape, F32),
-            pltpu.VMEM(kg.shape, F32),
         ]
         + attention_scratch(rows, local // HD)
         + [
             pltpu.SemaphoreType.DMA,
-            pltpu.SemaphoreType.DMA((6,)),
+            pltpu.SemaphoreType.DMA((3,)),
             pltpu.SemaphoreType.DMA((4,)),
             pltpu.SemaphoreType.DMA,
         ],
         compiler_params=pltpu.CompilerParams(vmem_limit_bytes=LIMIT_B * MIB),
         cost_estimate=BRIEF,
         name="second",
-    )(plen, adm, clen, qg, kg, pack, new, cache, wo)
+    )(plen, adm, clen, pack, cache, wo)
+
+
+def third_kernel(attn, wo_hbm, own, wo_a, wo_b, wo_sem):
+    nb = wo_a.shape[2]
+    first, second = partners()
+    head = lax.axis_index("head")
+    wo_v = [wo_a.at[0], wo_a.at[1], wo_b.at[0], wo_b.at[1]]
+    copies = [
+        out_copy(wo_hbm, block, nb, wo_v[j], wo_sem.at[j])
+        for j, block in enumerate((head, second, 3 - head, first))
+    ]
+    for copy in copies:
+        copy.start()
+    for j in range(2):
+        copies[j].wait()
+        own[:, j * nb : (j + 1) * nb] = dot(attn[...], wo_v[j][...]).astype(BF)
+    for copy in copies[2:]:
+        copy.wait()
+
+
+def third(n_head, attn, wo):
+    rows = attn.shape[0]
+    local, width = wo.shape
+    nb = width // n_head
+    return pl.pallas_call(
+        third_kernel,
+        out_shape=[jax.ShapeDtypeStruct((rows, 2 * nb), BF)]
+        + [jax.ShapeDtypeStruct((2, local, nb), BF)] * 2,
+        in_specs=[VM, HB],
+        out_specs=[VM] * 3,
+        scratch_shapes=[pltpu.SemaphoreType.DMA((4,))],
+        compiler_params=pltpu.CompilerParams(vmem_limit_bytes=LIMIT_C * MIB),
+        cost_estimate=BRIEF,
+        name="third",
+    )(attn, wo)
 
 
 def joined(bit, mine, other):
@@ -572,39 +611,27 @@
     )(own, got)
 
 
-def decode_out_kernel(bit, mine, other, wo_hbm, *refs):
-    outs, (wo_v, sems) = refs[:4], refs[4:]
+def decode_out_kernel(bit, mine, other, wo_a, wo_b, *outs):
     count = mine.shape[0] - 8
-    rows, nb = outs[0].shape
-    first, second = partners()
-    head = lax.axis_index("head")
-    copies = [
-        out_copy(wo_hbm, block, nb, wo_v.at[j], sems.at[j])
-        for j, block in enumerate((head, second, 3 - head, first))
-    ]
-    for copy in copies:
-        copy.start()
+    rows = outs[0].shape[0]
     mixed, _ = joined(bit, mine, other)
     mixed = mixed.astype(BF)
     flat = jnp.concatenate([mixed[i * rows : (i + 1) * rows] for i in range(count // rows)], axis=1)
     for j, out in enumerate(outs):
-        copies[j].wait()
-        out[...] = dot(flat, wo_v[j]).astype(BF)
-
-
-def decode_project(bit, n_head, dec_rows, mine, other, wo):
-    local, width = wo.shape
-    nb = width // n_head
+        out[...] = dot(flat, (wo_a, wo_b)[j // 2][j % 2]).astype(BF)
+
+
+def decode_project(bit, dec_rows, mine, other, wo_a, wo_b):
+    nb = wo_a.shape[2]
     return pl.pallas_call(
         functools.partial(decode_out_kernel, bit),
         out_shape=[jax.ShapeDtypeStruct((dec_rows, nb), BF)] * 4,
-        in_specs=[VM, VM, HB],
+        in_specs=[VM] * 4,
         out_specs=[VM] * 4,
-        scratch_shapes=[pltpu.VMEM((4, local, nb), BF), pltpu.SemaphoreType.DMA((4,))],
-        compiler_params=pltpu.CompilerParams(vmem_limit_bytes=LIMIT_C * MIB),
+        compiler_params=pltpu.CompilerParams(vmem_limit_bytes=16 * MIB),
         cost_estimate=BRIEF,
         name="decode_project",
-    )(mine, other, wo)
+    )(mine, other, wo_a, wo_b)
 
 
 def sum_parts(stage, out, sems, own, got, last):
@@ -726,32 +753,37 @@
     bits = bits[::-1]
 
     table = jnp.asarray(prompt_table(rows))
-    send1, pack, new = project(
-        n_head, prompt_len, qg, kg, table, prompts, dec_tokens, w_query, w_key, w_value, w_out
+    scalars = (prompt_len, admitted, cache_len)
+    send1, pack, blocks, leave = project(
+        n_head, n_seq, *scalars, qg, kg, table, prompts, dec_tokens, w_query, w_key, w_value, w_out
     )
     got1 = head_move(send1, (1, 2))
-    send0, own0, own1, part, blocks, leave = second(
-        n_head, n_seq, pr_dev, prompt_len, admitted, cache_len, qg, kg, pack, new, cache_kv[0], w_out
+    arrived = seq_move(leave, bits[0])
+    send0, attn0, own1, part = second(
+        n_head, n_seq, pr_dev, rows, *scalars, pack, cache_kv[0], w_out
     )
+    send0, arrived = lax.optimization_barrier((send0, arrived))
     got0 = head_move(send0, (1, 2))
     other = seq_move(part, bits[0])
-    arrived = seq_move(leave, bits[0])
+    own0, *wo = third(n_head, attn0, w_out)
+    other, got1 = lax.optimization_barrier((other, got1, own0))[:2]
     for i, bit in enumerate(bits[:-1]):
         part = join(bit, part, other)
         other = seq_move(part, bits[i + 1])
-    on1 = pass_on(1, own1, after(got1, part))
-    last1 = head_move(on1, (2, 1))
     held = [blocks[None], after(arrived, part)[None]]
     leave = hop(bits[0], held)
     held.append(seq_move(leave, bits[1]))
-    got0, other = lax.optimization_barrier((got0, other, on1, leave))[:2]
+    on1 = pass_on(1, own1, after(got1, part))
+    last1 = head_move(on1, (2, 1))
+    got0, other, held[-1] = lax.optimization_barrier((got0, other, held[-1], on1))[:3]
     on0 = pass_on(0, own0, got0)
     last0 = head_move(on0, (2, 1))
+    held[-1] = after(held[-1], on0)
     for i, bit in enumerate(bits[1:-1]):
         leave = hop(bit, held)
         held.append(seq_move(leave, bits[i + 2]))
     other = lax.optimization_barrier((other, on0, leave))[0]
-    pieces = decode_project(bits[-1], n_head, dec_rows, part, other, w_out)
+    pieces = decode_project(bits[-1], dec_rows, part, other, *wo)
     pieces = [
         pieces[0],
         head_move(pieces[1], (2, 1)),

time: 63 us -> 57.9 us (0.919)
  Pallas kernels: 30 us -> 28 us
  starting transfers between devices: 17.7 us -> 16.1 us
  local copies, waits for them, and re-layouts: 0.9 us -> 0.02 us
    ppermute x6, waiting for transfers between devices: 11 us -> 5.25 us  [seq_move(): return lax.ppermute(value, 'seq', [(i, i ^ bit) for i in range(n_seq)])]
    ppermute x7, waiting for transfers between devices: 2.36 us -> 7.41 us  [head_move(): return lax.ppermute(value, ('head', 'seq'), pairs)]
    pallas_call x1 -> x2, Pallas kernels: 12.9 us -> 16.7 us  [the longest x1 13.1 us: project(): pl.pallas_call(functools.partial(project_kernel, n_head, n_seq), out_shap...]
    pallas_call x1, Pallas kernels: 10 us -> 6.95 us  [second(): pl.pallas_call(functools.partial(second_kernel, n_seq, prompts), out_shap...]
    pallas_call x1, Pallas kernels: 3.93 us -> 1.28 us  [decode_project(): pl.pallas_call(functools.partial(decode_out_kernel, bit), out_shape=[jax....]
    ppermute x6, starting transfers between devices: 8.85 us -> 7.25 us  [seq_move(): return lax.ppermute(value, 'seq', [(i, i ^ bit) for i in range(n_seq)])]
    unnamed x12 -> x10, local copies, waits for them, and re-layouts: 0.9 us -> 0.02 us
  transfers between devices with their start and end apart: 13 -> 13, of which waited for: 5 -> 6; matrix products, arithmetic and copies ran while one was open for 0% -> 0% of each run, Pallas kernels for 25% -> 23%
where the time goes in v1:
time: 57.9 us; the launch traced here: 57.8 us
  Pallas kernels  28 us (48%)
  starting transfers between devices  16.1 us (28%)
  waiting for transfers between devices  12.7 us (22%)
  between operations  0.93 us (2%)
    pallas_call x1, Pallas kernels, project(): pl.pallas_call(functools.partial(project_kernel, n_head, n_seq), out_shap...  13.1 us
    ppermute x7, starting transfers between devices, head_move(): return lax.ppermute(value, ('head', 'seq'), pairs)  8.85 us
    ppermute x7, waiting for transfers between devices, head_move(): return lax.ppermute(value, ('head', 'seq'), pairs)  7.41 us
    ppermute x6, starting transfers between devices, seq_move(): return lax.ppermute(value, 'seq', [(i, i ^ bit) for i in range(n_seq)])  7.25 us
    pallas_call x1, Pallas kernels, second(): pl.pallas_call(functools.partial(second_kernel, n_seq, prompts), out_shap...  6.95 us
    ppermute x6, waiting for transfers between devices, seq_move(): return lax.ppermute(value, 'seq', [(i, i ^ bit) for i in range(n_seq)])  5.25 us
    pallas_call x1, Pallas kernels, third(): pl.pallas_call(third_kernel, out_shape=[jax.ShapeDtypeStruct((rows, 2 * n...  3.56 us
    pallas_call x1, Pallas kernels, finish_last(): pl.pallas_call(functools.partial(finish_last_kernel, p, slots), out_shape...  1.53 us
  transfers between devices with their start and end apart: 13, of which 6 were waited for; matrix products, arithmetic and copies ran while one was open for 0% of the time, Pallas kernels for 23%

profile of v1, /device:TPU:0, one launch (start us, length us, event | category | flops | bytes accessed | tf_op | source)
XLA Modules:
  0.0 57.8 jit_solution(14202598731671754670)
XLA Ops:
  0.6 0.0 copy-start.1
  0.6 0.0 copy-start.2
  0.7 0.0 copy-start.3
  0.7 0.0 copy-start.4
  0.7 13.1 %project.1 = (bf16[256,2048]{1,0:T(8,128)(2,1)}, bf16[272,2560]{1,0:T(8,128)(2,1)}, bf16[8,64,256]{2,1,0:T(8,128)(2,1)}, bf16[4,64,256]{2,1,0:T(8,128)(2,1)}) custom-call(s32[16]{0:T(128)} %refs_0_.3, s32[4]{0:T(128)} %refs_1_.3, s32[4]{0:T(128)} %refs_2_.3, f32[1,128]{1,0:T(1,128)} %bitcast.13, f32[1,128]{1,0:T(1,128)} %bitcast.14, ...), custom_call_target="tpu_custom_call" | custom-call | flops 1 | bytes 1 | tf_op jit(solution)/shard_map/project/pallas_call | solution.py:352
  13.8 3.0 %collective-permute-start.3 = (bf16[256,2048]{1,0:T(8,128)(2,1)}, bf16[256,2048]{1,0:T(8,128)(2,1)S(1)}, u32[]{:S(2)}, u32[]{:S(2)}) collective-permute-start(bf16[256,2048]{1,0:T(8,128)(2,1)} %get-tuple-element.40), channel_id=1, source_target_pairs={{0,8},{1,17},{2,10},{3,19},{4,12},{5,21},{6,14},{7,23},{8,0},{9,25... | collective-permute-start | bytes 3145736 | tf_op jit(solution)/shard_map/ppermute | solution.py:745
  16.8 2.6 %collective-permute-start = (bf16[4,64,256]{2,1,0:T(8,128)(2,1)}, bf16[4,64,256]{2,1,0:T(8,128)(2,1)S(1)}, u32[]{:S(2)}, u32[]{:S(2)}) collective-permute-start(bf16[4,64,256]{2,1,0:T(8,128)(2,1)} %get-tuple-element.37), channel_id=1, source_target_pairs={{0,4},{1,5},{2,6},{3,7},{4,0},{5,1},{6,2},{7,3},{8,12},{9,13},{10,... | collective-permute-start | bytes 393224 | tf_op jit(solution)/shard_map/ppermute | solution.py:748
  19.4 0.0 copy-done.1
  19.4 0.0 copy-done.2
  19.4 0.0 copy-done.3
  19.4 0.0 copy-done.4
  19.4 7.0 %second.1 = (bf16[256,2048]{1,0:T(8,128)(2,1)S(1)}, bf16[256,1024]{1,0:T(8,128)(2,1)S(1)}, bf16[256,2048]{1,0:T(8,128)(2,1)S(1)}, f32[136,128]{1,0:T(8,128)S(1)}) custom-call(s32[16]{0:T(128)S(1)} %copy-done.2, s32[4]{0:T(128)S(1)} %copy-done.3, s32[4]{0:T(128)S(1)} %copy-done.4, bf16[272,2560]{1,0:T(8,128)(2,1)} %get-tuple-element.33.refs_3_, ...), custom_call_target="tpu_custom_call" | custom-call | flops 1 | bytes 1 | tf_op jit(solution)/shard_map/second/pallas_call | solution.py:456
  26.4 0.0 collective-permute-done
  26.4 0.8 %collective-permute-start.1 = (bf16[256,2048]{1,0:T(8,128)(2,1)S(1)}, bf16[256,2048]{1,0:T(8,128)(2,1)S(1)}, u32[]{:S(2)}, u32[]{:S(2)}) collective-permute-start(bf16[256,2048]{1,0:T(8,128)(2,1)S(1)} %get-tuple-element.38), channel_id=1, source_target_pairs={{0,8},{1,17},{2,10},{3,19},{4,12},{5,21},{6,14},{7,23},{8,0},{9,25... | collective-permute-start | bytes 3145736 | tf_op jit(solution)/shard_map/ppermute | solution.py:745
  27.2 0.0 collective-permute-start.2
  27.2 0.0 copy-start
  27.2 3.6 %third.1 = (bf16[256,2048]{1,0:T(8,128)(2,1)S(1)}, bf16[2,1024,1024]{2,1,0:T(8,128)(2,1)S(1)}, bf16[2,1024,1024]{2,1,0:T(8,128)(2,1)S(1)}) custom-call(bf16[256,1024]{1,0:T(8,128)(2,1)S(1)} %get-tuple-element.34.attn, bf16[1024,4096]{1,0:T(8,128)(2,1)} %wo_hbm.1), custom_call_target="tpu_custom_call" | custom-call | flops 1 | bytes 1 | tf_op jit(solution)/shard_map/third/pallas_call | solution.py:509
  30.8 1.6 %collective-permute-done.2.other = f32[136,128]{1,0:T(8,128)S(1)} collective-permute-done((f32[136,128]{1,0:T(8,128)S(1)}, f32[136,128]{1,0:T(8,128)S(1)}, u32[]{:S(2)}, u32[]{:S(2)}) %collective-permute-start.2) | collective-permute-done | bytes 69664 | tf_op jit(solution)/shard_map/ppermute | solution.py:748
  32.4 0.0 collective-permute-done.3.got
  32.4 0.1 join_4.1.mine
  32.6 2.5 %collective-permute-start.4 = (f32[136,128]{1,0:T(8,128)S(1)}, f32[136,128]{1,0:T(8,128)S(1)}, u32[]{:S(2)}, u32[]{:S(2)}) collective-permute-start(f32[136,128]{1,0:T(8,128)S(1)} %join_4.1.mine), channel_id=1, source_target_pairs={{0,2},{1,3},{2,0},{3,1},{4,6},{5,7},{6,4},{7,5},{8,10},{9,11},{10,... | collective-permute-start | bytes 208904 | tf_op jit(solution)/shard_map/ppermute | solution.py:748
  35.1 2.3 %collective-permute-done.4.other = f32[136,128]{1,0:T(8,128)S(1)} collective-permute-done((f32[136,128]{1,0:T(8,128)S(1)}, f32[136,128]{1,0:T(8,128)S(1)}, u32[]{:S(2)}, u32[]{:S(2)}) %collective-permute-start.4) | collective-permute-done | bytes 69664 | tf_op jit(solution)/shard_map/ppermute | solution.py:748
  37.4 0.1 join_2.1.mine
  37.5 0.0 copy-done
  37.6 2.1 %collective-permute-start.6 = (bf16[2,2,64,256]{3,2,1,0:T(8,128)(2,1)S(1)}, bf16[2,2,64,256]{3,2,1,0:T(8,128)(2,1)S(1)}, u32[]{:S(2)}, u32[]{:S(2)}) collective-permute-start(bf16[2,2,64,256]{3,2,1,0:T(8,128)(2,1)S(1)} %hop_4.1), channel_id=1, source_target_pairs={{0,2},{1,3},{2,0},{3,1},{4,6},{5,7},{6,4},{7,5},{8,10},{9,11},{10,... | collective-permute-start | bytes 393224 | tf_op jit(solution)/shard_map/ppermute | solution.py:748
  39.6 0.0 collective-permute-start.5
  39.6 0.1 pass_on_1.1
  39.8 0.6 collective-permute-start.11
  40.4 0.9 %collective-permute-done.1.got = bf16[256,2048]{1,0:T(8,128)(2,1)S(1)} collective-permute-done((bf16[256,2048]{1,0:T(8,128)(2,1)S(1)}, bf16[256,2048]{1,0:T(8,128)(2,1)S(1)}, u32[]{:S(2)}, u32[]{:S(2)}) %collective-permute-start.1) | collective-permute-done | bytes 1048608 | tf_op jit(solution)/shard_map/ppermute | solution.py:745
  41.3 0.0 collective-permute-done.5.other
  41.3 1.3 %collective-permute-done.6.refs_2_ = bf16[2,2,64,256]{3,2,1,0:T(8,128)(2,1)S(1)} collective-permute-done((bf16[2,2,64,256]{3,2,1,0:T(8,128)(2,1)S(1)}, bf16[2,2,64,256]{3,2,1,0:T(8,128)(2,1)S(1)}, u32[]{:S(2)}, u32[]{:S(2)}) %collective-permute-start.6) | collective-permute-done | bytes 131104 | tf_op jit(solution)/shard_map/ppermute | solution.py:748
  42.6 0.1 pass_on_0.1
  42.7 0.9 %collective-permute-start.7 = (bf16[256,1024]{1,0:T(8,128)(2,1)S(1)}, bf16[256,1024]{1,0:T(8,128)(2,1)S(1)}, u32[]{:S(2)}, u32[]{:S(2)}) collective-permute-start(bf16[256,1024]{1,0:T(8,128)(2,1)S(1)} %pass_on_0.1), channel_id=1, source_target_pairs={{0,16},{1,9},{2,18},{3,11},{4,20},{5,13},{6,22},{7,15},{8,24},{9,1... | collective-permute-start | bytes 1572872 | tf_op jit(solution)/shard_map/ppermute | solution.py:745
  43.7 0.1 collective-permute-start.12
  43.8 1.3 %decode_project.1 = (bf16[16,1024]{1,0:T(8,128)(2,1)S(1)}, bf16[16,1024]{1,0:T(8,128)(2,1)S(1)}, bf16[16,1024]{1,0:T(8,128)(2,1)S(1)}, bf16[16,1024]{1,0:T(8,128)(2,1)S(1)}) custom-call(f32[136,128]{1,0:T(8,128)S(1)} %join_2.1.mine, f32[136,128]{1,0:T(8,128)S(1)} %collective-permute-done.5.other, bf16[2,1024,1024]{2,1,0:T(8,128)(2,1)S(1)} %get-tuple-element.53.wo_a, ...), custom_call_target="tpu_custom_call" | custom-call | flops 1 | bytes 1 | tf_op jit(solution)/shard_map/decode_project/pallas_call | solution.py:626
  45.0 1.2 %collective-permute-start.8 = (bf16[16,1024]{1,0:T(8,128)(2,1)S(1)}, bf16[16,1024]{1,0:T(8,128)(2,1)S(1)}, u32[]{:S(2)}, u32[]{:S(2)}) collective-permute-start(bf16[16,1024]{1,0:T(8,128)(2,1)S(1)} %get-tuple-element.56), channel_id=1, source_target_pairs={{0,16},{1,9},{2,18},{3,11},{4,20},{5,13},{6,22},{7,15},{8,24},{9,1... | collective-permute-start | bytes 98312 | tf_op jit(solution)/shard_map/ppermute | solution.py:745
  46.2 1.8 %collective-permute-start.9 = (bf16[16,1024]{1,0:T(8,128)(2,1)S(1)}, bf16[16,1024]{1,0:T(8,128)(2,1)S(1)}, u32[]{:S(2)}, u32[]{:S(2)}) collective-permute-start(bf16[16,1024]{1,0:T(8,128)(2,1)S(1)} %get-tuple-element.57), channel_id=1, source_target_pairs={{0,24},{1,25},{2,26},{3,27},{4,28},{5,29},{6,30},{7,31},{8,16},{9,... | collective-permute-start | bytes 98312 | tf_op jit(solution)/shard_map/ppermute | solution.py:745
  48.0 0.0 collective-permute-done.12.refs_3_
  48.0 0.5 collective-permute-start.10
  48.5 0.5 collective-permute-done.11.last
  49.0 1.0 %finish_1.1 = (bf16[2,256,1024]{2,1,0:T(8,128)(2,1)}, bf16[8,64,256]{2,1,0:T(8,128)(2,1)}) custom-call(bf16[256,2048]{1,0:T(8,128)(2,1)S(1)} %get-tuple-element.45.own, bf16[256,2048]{1,0:T(8,128)(2,1)S(1)} %collective-permute-done.3.got, bf16[256,1024]{1,0:T(8,128)(2,1)S(1)} %collective-permute-done.11.last, bf16[1,8,64,256]{3,2,1,0:T(8,128)(2,1)S(1)} %bitcast.8, ...), custom_call_target="tpu_custom_call" | custom-call | flops 1 | bytes 1 | tf_op jit(solution)/shard_map/finish_1/pallas_call | solution.py:676
  50.1 6.0 %collective-permute-done.8.refs_1_ = bf16[16,1024]{1,0:T(8,128)(2,1)S(1)} collective-permute-done((bf16[16,1024]{1,0:T(8,128)(2,1)S(1)}, bf16[16,1024]{1,0:T(8,128)(2,1)S(1)}, u32[]{:S(2)}, u32[]{:S(2)}) %collective-permute-start.8) | collective-permute-done | bytes 32800 | tf_op jit(solution)/shard_map/ppermute | solution.py:745
  56.1 0.0 collective-permute-done.9.refs_2_
  56.1 0.0 collective-permute-done.10.refs_3_
  56.1 0.0 collective-permute-done.7.last
  56.1 1.5 %finish_0.1 = (bf16[2,256,1024]{2,1,0:T(8,128)(2,1)}, bf16[4,4,1024]{2,1,0:T(4,128)(2,1)}) custom-call(bf16[256,2048]{1,0:T(8,128)(2,1)S(1)} %get-tuple-element.35.own, bf16[256,2048]{1,0:T(8,128)(2,1)S(1)} %collective-permute-done.1.got, bf16[256,1024]{1,0:T(8,128)(2,1)S(1)} %collective-permute-done.7.last, ...), custom_call_target="tpu_custom_call", output_to_operand_aliasing={{0}: (7, {})} | custom-call | flops 1 | bytes 1 | tf_op jit(solution)/shard_map/finish_0/pallas_call | solution.py:709
  (2 shorter events, 0.0 us)
Async XLA Ops:
  0.6 18.8 %copy-start.1 = (bf16[1,4,512,256]{3,2,1,0:T(8,128)(2,1)S(1)}, bf16[1,4,512,256]{3,2,1,0:T(8,128)(2,1)}, u32[]{:S(2)}) copy-start(bf16[1,4,512,256]{3,2,1,0:T(8,128)(2,1)} %param.17) | copy-start | bytes 3145732
  0.6 18.8 %copy-start.2 = (s32[16]{0:T(128)S(1)}, s32[16]{0:T(128)}, u32[]{:S(2)}) copy-start(s32[16]{0:T(128)} %refs_0_.3) | copy-start | bytes 196
  0.7 18.8 %copy-start.3 = (s32[4]{0:T(128)S(1)}, s32[4]{0:T(128)}, u32[]{:S(2)}) copy-start(s32[4]{0:T(128)} %refs_1_.3) | copy-start | bytes 52
  0.7 18.8 %copy-start.4 = (s32[4]{0:T(128)S(1)}, s32[4]{0:T(128)}, u32[]{:S(2)}) copy-start(s32[4]{0:T(128)} %refs_2_.3) | copy-start | bytes 52
  13.8 18.6 %collective-permute-start.3 = (bf16[256,2048]{1,0:T(8,128)(2,1)}, bf16[256,2048]{1,0:T(8,128)(2,1)S(1)}, u32[]{:S(2)}, u32[]{:S(2)}) collective-permute-start(bf16[256,2048]{1,0:T(8,128)(2,1)} %get-tuple-element.40), channel_id=1, source_target_pairs={{0,8},{1,17},{2,10},{3,19},{4,12},{5,21},{6,14},{7,23},{8,0},{9,25... | collective-permute-start | bytes 3145736 | tf_op jit(solution)/shard_map/ppermute | solution.py:745
  16.8 9.6 %collective-permute-start = (bf16[4,64,256]{2,1,0:T(8,128)(2,1)}, bf16[4,64,256]{2,1,0:T(8,128)(2,1)S(1)}, u32[]{:S(2)}, u32[]{:S(2)}) collective-permute-start(bf16[4,64,256]{2,1,0:T(8,128)(2,1)} %get-tuple-element.37), channel_id=1, source_target_pairs={{0,4},{1,5},{2,6},{3,7},{4,0},{5,1},{6,2},{7,3},{8,12},{9,13},{10,... | collective-permute-start | bytes 393224 | tf_op jit(solution)/shard_map/ppermute | solution.py:748
  26.4 14.9 %collective-permute-start.1 = (bf16[256,2048]{1,0:T(8,128)(2,1)S(1)}, bf16[256,2048]{1,0:T(8,128)(2,1)S(1)}, u32[]{:S(2)}, u32[]{:S(2)}) collective-permute-start(bf16[256,2048]{1,0:T(8,128)(2,1)S(1)} %get-tuple-element.38), channel_id=1, source_target_pairs={{0,8},{1,17},{2,10},{3,19},{4,12},{5,21},{6,14},{7,23},{8,0},{9,25... | collective-permute-start | bytes 3145736 | tf_op jit(solution)/shard_map/ppermute | solution.py:745
  27.2 5.2 %collective-permute-start.2 = (f32[136,128]{1,0:T(8,128)S(1)}, f32[136,128]{1,0:T(8,128)S(1)}, u32[]{:S(2)}, u32[]{:S(2)}) collective-permute-start(f32[136,128]{1,0:T(8,128)S(1)} %get-tuple-element.39.mine), channel_id=1, source_target_pairs={{0,4},{1,5},{2,6},{3,7},{4,0},{5,1},{6,2},{7,3},{8,12},{9,13},{10,... | collective-permute-start | bytes 208904 | tf_op jit(solution)/shard_map/ppermute | solution.py:748
  27.2 10.3 %copy-start = (bf16[8,64,256]{2,1,0:T(8,128)(2,1)S(1)}, bf16[8,64,256]{2,1,0:T(8,128)(2,1)}, u32[]{:S(2)}) copy-start(bf16[8,64,256]{2,1,0:T(8,128)(2,1)} %get-tuple-element.42) | copy-start | bytes 786436
  32.6 4.8 %collective-permute-start.4 = (f32[136,128]{1,0:T(8,128)S(1)}, f32[136,128]{1,0:T(8,128)S(1)}, u32[]{:S(2)}, u32[]{:S(2)}) collective-permute-start(f32[136,128]{1,0:T(8,128)S(1)} %join_4.1.mine), channel_id=1, source_target_pairs={{0,2},{1,3},{2,0},{3,1},{4,6},{5,7},{6,4},{7,5},{8,10},{9,11},{10,... | collective-permute-start | bytes 208904 | tf_op jit(solution)/shard_map/ppermute | solution.py:748
  37.6 5.0 %collective-permute-start.6 = (bf16[2,2,64,256]{3,2,1,0:T(8,128)(2,1)S(1)}, bf16[2,2,64,256]{3,2,1,0:T(8,128)(2,1)S(1)}, u32[]{:S(2)}, u32[]{:S(2)}) collective-permute-start(bf16[2,2,64,256]{3,2,1,0:T(8,128)(2,1)S(1)} %hop_4.1), channel_id=1, source_target_pairs={{0,2},{1,3},{2,0},{3,1},{4,6},{5,7},{6,4},{7,5},{8,10},{9,11},{10,... | collective-permute-start | bytes 393224 | tf_op jit(solution)/shard_map/ppermute | solution.py:748
  39.6 1.6 %collective-permute-start.5 = (f32[136,128]{1,0:T(8,128)S(1)}, f32[136,128]{1,0:T(8,128)S(1)}, u32[]{:S(2)}, u32[]{:S(2)}) collective-permute-start(f32[136,128]{1,0:T(8,128)S(1)} %join_2.1.mine), channel_id=1, source_target_pairs={{0,1},{1,0},{2,3},{3,2},{4,5},{5,4},{6,7},{7,6},{8,9},{9,8},{10,11... | collective-permute-start | bytes 208904 | tf_op jit(solution)/shard_map/ppermute | solution.py:748
  39.8 9.2 %collective-permute-start.11 = (bf16[256,1024]{1,0:T(8,128)(2,1)S(1)}, bf16[256,1024]{1,0:T(8,128)(2,1)S(1)}, u32[]{:S(2)}, u32[]{:S(2)}) collective-permute-start(bf16[256,1024]{1,0:T(8,128)(2,1)S(1)} %pass_on_1.1), channel_id=1, source_target_pairs={{0,16},{1,9},{2,18},{3,11},{4,20},{5,13},{6,22},{7,15},{8,24},{9,1... | collective-permute-start | bytes 1572872 | tf_op jit(solution)/shard_map/ppermute | solution.py:745
  42.7 13.3 %collective-permute-start.7 = (bf16[256,1024]{1,0:T(8,128)(2,1)S(1)}, bf16[256,1024]{1,0:T(8,128)(2,1)S(1)}, u32[]{:S(2)}, u32[]{:S(2)}) collective-permute-start(bf16[256,1024]{1,0:T(8,128)(2,1)S(1)} %pass_on_0.1), channel_id=1, source_target_pairs={{0,16},{1,9},{2,18},{3,11},{4,20},{5,13},{6,22},{7,15},{8,24},{9,1... | collective-permute-start | bytes 1572872 | tf_op jit(solution)/shard_map/ppermute | solution.py:745
  43.7 4.3 %collective-permute-start.12 = (bf16[4,1,64,256]{3,2,1,0:T(8,128)(2,1)S(1)}, bf16[4,1,64,256]{3,2,1,0:T(8,128)(2,1)S(1)}, u32[]{:S(2)}, u32[]{:S(2)}) collective-permute-start(bf16[4,1,64,256]{3,2,1,0:T(8,128)(2,1)S(1)} %hop_2.1), channel_id=1, source_target_pairs={{0,1},{1,0},{2,3},{3,2},{4,5},{5,4},{6,7},{7,6},{8,9},{9,8},{10,11... | collective-permute-start | bytes 393224 | tf_op jit(solution)/shard_map/ppermute | solution.py:748
  45.0 11.0 %collective-permute-start.8 = (bf16[16,1024]{1,0:T(8,128)(2,1)S(1)}, bf16[16,1024]{1,0:T(8,128)(2,1)S(1)}, u32[]{:S(2)}, u32[]{:S(2)}) collective-permute-start(bf16[16,1024]{1,0:T(8,128)(2,1)S(1)} %get-tuple-element.56), channel_id=1, source_target_pairs={{0,16},{1,9},{2,18},{3,11},{4,20},{5,13},{6,22},{7,15},{8,24},{9,1... | collective-permute-start | bytes 98312 | tf_op jit(solution)/shard_map/ppermute | solution.py:745
  46.2 9.9 %collective-permute-start.9 = (bf16[16,1024]{1,0:T(8,128)(2,1)S(1)}, bf16[16,1024]{1,0:T(8,128)(2,1)S(1)}, u32[]{:S(2)}, u32[]{:S(2)}) collective-permute-start(bf16[16,1024]{1,0:T(8,128)(2,1)S(1)} %get-tuple-element.57), channel_id=1, source_target_pairs={{0,24},{1,25},{2,26},{3,27},{4,28},{5,29},{6,30},{7,31},{8,16},{9,... | collective-permute-start | bytes 98312 | tf_op jit(solution)/shard_map/ppermute | solution.py:745
  48.0 8.1 %collective-permute-start.10 = (bf16[16,1024]{1,0:T(8,128)(2,1)S(1)}, bf16[16,1024]{1,0:T(8,128)(2,1)S(1)}, u32[]{:S(2)}, u32[]{:S(2)}) collective-permute-start(bf16[16,1024]{1,0:T(8,128)(2,1)S(1)} %get-tuple-element.58), channel_id=1, source_target_pairs={{0,8},{1,17},{2,10},{3,19},{4,12},{5,21},{6,14},{7,23},{8,0},{9,25... | collective-permute-start | bytes 98312 | tf_op jit(solution)/shard_map/ppermute | solution.py:745

commit v2 on v1

--- a/solution.py
+++ b/solution.py
@@ -105,12 +105,12 @@
     return jnp.where((col_at <= row_at) & (col_at < length), 0.0, NEG).astype(F32)
 
 
-def attention(heads, queries, kv, bias_v, s_v, w_v, attn):
+def attention(heads, queries, kv, bias_v, s_v, w_v, attn, skip=0):
     rows = kv.shape[0]
     half = rows // 2
     quarter = rows // 4
     for h in heads:
-        at = slice(h * HD, (h + 1) * HD)
+        at = slice((h - skip) * HD, (h - skip + 1) * HD)
         s_v[h, :half, :half] = dot_nt(queries[:half, at], kv[:half, :HD])
         s_v[h, half:, :] = dot_nt(queries[half:, at], kv[:, :HD])
     for h in heads:
@@ -245,7 +245,7 @@
     o_copies = [
         out_copy(wo_hbm, block, nb, wo_v.at[j], wo_sem.at[j]) for j, block in enumerate((diag, first))
     ]
-    ahead = 3
+    ahead = 4
     queue += [[copy] for copy in o_copies]
     for copy in [dec_copy] + queue[0] + small:
         copy.start()
@@ -314,20 +314,24 @@
     mine = pack.at[whole, pl.ds(base, local)]
     pair = 2 * HD
     for j in range(local // pair):
-        later = dot(x_v[front:, :], wq_v[:, j * pair : (j + 1) * pair])
+        later = None
+        if j % 2 == 0:
+            later = dot(x_v[front:, :], wq_v[:, j // 2 * pair : (j // 2 + 1) * pair])
         for h in (2 * j, 2 * j + 1):
             piece = raw[:rows, h * HD : (h + 1) * HD]
             mine[:, h * HD : (h + 1) * HD] = rope(norm(piece, qg[...]), cos2, sin2).astype(BF)
         attention((2 * j, 2 * j + 1), mine, kvs[lead], bias_v, s_v, w_v, mine)
-        for i in range(2):
-            col = base + local + (2 * j + i) * HD
-            piece = later[:, i * HD : (i + 1) * HD]
-            pack[:rows, col : col + HD] = rope(norm(piece, qg[...]), cos2, sin2).astype(BF)
+        if later is not None:
+            for i in range(2):
+                col = base + local + (j + i) * HD
+                piece = later[:, i * HD : (i + 1) * HD]
+                pack[:rows, col : col + HD] = rope(norm(piece, qg[...]), cos2, sin2).astype(BF)
     outs.append(pltpu.make_async_copy(pack, pack_h, out_sem.at[2]))
     outs[-1].start()
-    for j in range(2):
-        at = pl.ds(j * nb, nb)
-        send[:, at] = dot(mine[...], wo_v[j]).astype(BF)
+    hb = nb // 2
+    for j in range(4):
+        at = pl.ds(j * hb, hb)
+        send[:, at] = dot(mine[...], wo_v[j // 2, :, (j % 2) * hb : (j % 2 + 1) * hb]).astype(BF)
         outs.append(pltpu.make_async_copy(send.at[:, at], send_h.at[:, at], out_sem.at[3 + j]))
         outs[-1].start()
     for copy in outs:
@@ -335,8 +339,8 @@
 
 
 def cut_points(width):
-    step = width // 8
-    return [0, step, 2 * step, 4 * step, 6 * step, 8 * step]
+    step = width // 16
+    return [step * i for i in (0, 1, 2, 4, 8, 12, 16)]
 
 
 def project(n_head, n_seq, plen, adm, clen, qg, kg, table, x, dec, wq, wk, wv, wo):
@@ -346,7 +350,7 @@
     nb = width // n_head
     every = prompts * rows + dec_rows
     send = (rows, 2 * nb)
-    pack = (rows + dec_rows, 2 * prompts * HD + prompts * local)
+    pack = (rows + dec_rows, 2 * prompts * HD + local + local // 2)
     blocks = (n_seq, prompts * rows // n_seq, 2 * HD)
     chunks = len(cut_points(width)) - 1
     return pl.pallas_call(
@@ -386,7 +390,7 @@
             pltpu.SemaphoreType.DMA((chunks,)),
             pltpu.SemaphoreType.DMA((2,)),
             pltpu.SemaphoreType.DMA((6,)),
-            pltpu.SemaphoreType.DMA((5,)),
+            pltpu.SemaphoreType.DMA((7,)),
         ],
         compiler_params=pltpu.CompilerParams(vmem_limit_bytes=LIMIT_A * MIB),
         cost_estimate=BRIEF,
@@ -395,11 +399,11 @@
 
 
 def second_kernel(n_seq, prompts, *refs):
-    plen_h, adm_h, clen_h, pack_h, cache_h, wo_hbm = refs[:6]
-    send, attn, own1, part = refs[6:10]
-    pack, cache, wo_v, plen, adm, clen = refs[10:16]
-    bias_v, s_v, w_v = refs[16:19]
-    pack_sem, small_sem, wo_sem, cache_sem = refs[19:]
+    plen_h, adm_h, clen_h, qg_h, table_h, pack_h, x_hbm, wq_hbm, cache_h, wo_hbm = refs[:10]
+    send, attn, own1, part = refs[10:14]
+    pack, x_v, wq_v, q_v, cache, wo_v, plen, adm, clen, qg, table = refs[14:25]
+    bias_v, s_v, w_v = refs[25:28]
+    pack_sem, small_sem, wo_sem, cache_sem, more_sem = refs[28:]
     rows = attn.shape[0]
     dec_rows = pack.shape[0] - rows
     _, local, nb = wo_v.shape
@@ -410,13 +414,19 @@
     cache_copy = pltpu.make_async_copy(cache_h, cache, cache_sem)
     small = [
         pltpu.make_async_copy(src, dst, small_sem.at[i])
-        for i, (src, dst) in enumerate([(plen_h, plen), (adm_h, adm), (clen_h, clen)])
+        for i, (src, dst) in enumerate(
+            [(plen_h, plen), (adm_h, adm), (clen_h, clen), (qg_h, qg), (table_h, table)]
+        )
     ]
     copies = [
         out_copy(wo_hbm, block, nb, wo_v.at[j], wo_sem.at[j])
         for j, block in enumerate((head, second, 3 - head, first))
     ]
-    for copy in small + [pack_copy] + copies[:2] + [cache_copy] + copies[2:]:
+    more = [
+        pltpu.make_async_copy(x_hbm.at[0], x_v, more_sem.at[0]),
+        pltpu.make_async_copy(wq_hbm.at[:, pl.ds(local // 2, local // 2)], wq_v, more_sem.at[1]),
+    ]
+    for copy in small + [pack_copy] + more + copies[:1]:
         copy.start()
     for copy in small:
         copy.wait()
@@ -427,17 +437,36 @@
     whole = pl.ds(0, rows)
     kvs = [pack.at[whole, pl.ds(p * both, both)] for p in range(prompts)]
     other = pack.at[whole, pl.ds(base, local)]
-    queries = pack.at[whole, pl.ds(base + local, local)]
+    queries = pack.at[whole, pl.ds(base + local, local // 2)]
     hb = nb // 2
 
-    for j in range(local // both):
+    cos2, sin2 = table[:, :HD], table[:, HD:]
+    pairs = local // both
+    middle = pairs // 2
+    for j in range(pairs):
+        if j == 1:
+            for copy in more:
+                copy.wait()
+            for copy in copies[1:2] + [cache_copy] + copies[2:]:
+                copy.start()
         if j in (1, 2):
-            copies[j - 1].wait()
+            at = slice((j - 1) * both, j * both)
+            later = dot(x_v[...], wq_v[:, at])
+            for i in range(2):
+                piece = later[:, i * HD : (i + 1) * HD]
+                col = (j - 1) * both + i * HD
+                q_v[:, col : col + HD] = rope(norm(piece, qg[...]), cos2, sin2).astype(BF)
+        if j in (2, 3):
+            copies[j - 2].wait()
             for i in range(2):
                 at = slice(i * hb, (i + 1) * hb)
-                to = slice((j - 1) * nb + i * hb, (j - 1) * nb + (i + 1) * hb)
-                own1[:, to] = dot(other[...], wo_v[j - 1, :, at]).astype(BF)
-        attention((2 * j, 2 * j + 1), queries, kvs[0], bias_v, s_v, w_v, attn)
+                to = slice((j - 2) * nb + i * hb, (j - 2) * nb + (i + 1) * hb)
+                own1[:, to] = dot(other[...], wo_v[j - 2, :, at]).astype(BF)
+        heads = (2 * j, 2 * j + 1)
+        if j < middle:
+            attention(heads, queries, kvs[0], bias_v, s_v, w_v, attn)
+        else:
+            attention(heads, q_v, kvs[0], bias_v, s_v, w_v, attn, 2 * middle)
     cache_copy.wait()
     for copy in copies[2:]:
         copy.wait()
@@ -449,7 +478,8 @@
     )
 
 
-def second(n_head, n_seq, prompts, rows, plen, adm, clen, pack, cache, wo):
+def second(n_head, n_seq, plen, adm, clen, qg, table, pack, x, wq, cache, wo):
+    prompts, rows, _ = x.shape
     local, width = wo.shape
     nb = width // n_head
     dec_rows = pack.shape[0] - rows
@@ -461,27 +491,33 @@
             jax.ShapeDtypeStruct((rows, 2 * nb), BF),
             jax.ShapeDtypeStruct((dec_rows * (local // HD) + 8, HD), F32),
         ],
-        in_specs=[HB] * 6,
+        in_specs=[HB] * 10,
         out_specs=[VM] * 4,
         scratch_shapes=[
             pltpu.VMEM(pack.shape, BF),
+            pltpu.VMEM((rows, width), BF),
+            pltpu.VMEM((width, local // 2), BF),
+            pltpu.VMEM((rows, local // 2), BF),
             pltpu.VMEM(cache.shape, BF),
             pltpu.VMEM((4, local, nb), BF),
             pltpu.SMEM(plen.shape, jnp.int32),
             pltpu.SMEM(adm.shape, jnp.int32),
             pltpu.SMEM(clen.shape, jnp.int32),
+            pltpu.VMEM(qg.shape, F32),
+            pltpu.VMEM(table.shape, F32),
         ]
         + attention_scratch(rows, local // HD)
         + [
             pltpu.SemaphoreType.DMA,
-            pltpu.SemaphoreType.DMA((3,)),
+            pltpu.SemaphoreType.DMA((5,)),
             pltpu.SemaphoreType.DMA((4,)),
             pltpu.SemaphoreType.DMA,
+            pltpu.SemaphoreType.DMA((2,)),
         ],
         compiler_params=pltpu.CompilerParams(vmem_limit_bytes=LIMIT_B * MIB),
         cost_estimate=BRIEF,
         name="second",
-    )(plen, adm, clen, pack, cache, wo)
+    )(plen, adm, clen, qg, table, pack, x, wq, cache, wo)
 
 
 def third_kernel(attn, wo_hbm, own, wo_a, wo_b, wo_sem):
@@ -692,34 +728,45 @@
     )(own, got, last, *held)
 
 
-def finish_last_kernel(p, slots, own, got, last, *refs):
-    pieces, (_, out, dec_out, stage, sems) = refs[:-5], refs[-5:]
-    copies = sum_parts(stage, out.at[p], sems, own, got, last)
+def finish_last_kernel(p, own, got, last, _, out, stage, sems):
+    for copy in sum_parts(stage, out.at[p], sems, own, got, last):
+        copy.wait()
+
+
+def finish_last(p, own, got, last, partial):
+    rows, nb = last.shape
+    return pl.pallas_call(
+        functools.partial(finish_last_kernel, p),
+        out_shape=jax.ShapeDtypeStruct(partial.shape, BF),
+        in_specs=[VM] * 3 + [HB],
+        out_specs=HB,
+        scratch_shapes=[pltpu.VMEM((rows, nb), BF), pltpu.SemaphoreType.DMA((2,))],
+        input_output_aliases={3: 0},
+        compiler_params=pltpu.CompilerParams(vmem_limit_bytes=8 * MIB),
+        cost_estimate=BRIEF,
+        name="finish_%d" % p,
+    )(own, got, last, partial)
+
+
+def decode_sum_kernel(slots, *refs):
+    pieces, out = refs[:-1], refs[-1]
     total = pieces[0][...].astype(F32)
     for piece in pieces[1:]:
         total = total + piece[...].astype(F32)
-    for t in range(dec_out.shape[0]):
-        dec_out[t] = total[t * slots : (t + 1) * slots].astype(BF)
-    for copy in copies:
-        copy.wait()
-
-
-def finish_last(p, steps, slots, own, got, last, pieces, partial):
-    rows, nb = last.shape
-    return pl.pallas_call(
-        functools.partial(finish_last_kernel, p, slots),
-        out_shape=[
-            jax.ShapeDtypeStruct(partial.shape, BF),
-            jax.ShapeDtypeStruct((steps, slots, nb), BF),
-        ],
-        in_specs=[VM] * (3 + len(pieces)) + [HB],
-        out_specs=[HB, VM],
-        scratch_shapes=[pltpu.VMEM((rows, nb), BF), pltpu.SemaphoreType.DMA((2,))],
-        input_output_aliases={3 + len(pieces): 0},
+    for t in range(out.shape[0]):
+        out[t] = total[t * slots : (t + 1) * slots].astype(BF)
+
+
+def decode_sum(steps, slots, pieces):
+    return pl.pallas_call(
+        functools.partial(decode_sum_kernel, slots),
+        out_shape=jax.ShapeDtypeStruct((steps, slots, pieces[0].shape[1]), BF),
+        in_specs=[VM] * len(pieces),
+        out_specs=VM,
         compiler_params=pltpu.CompilerParams(vmem_limit_bytes=8 * MIB),
         cost_estimate=BRIEF,
-        name="finish_%d" % p,
-    )(own, got, last, *pieces, partial)
+        name="decode_sum",
+    )(*pieces)
 
 
 def after(value, other):
@@ -760,7 +807,7 @@
     got1 = head_move(send1, (1, 2))
     arrived = seq_move(leave, bits[0])
     send0, attn0, own1, part = second(
-        n_head, n_seq, pr_dev, rows, *scalars, pack, cache_kv[0], w_out
+        n_head, n_seq, *scalars, qg, table, pack, prompts, w_query, cache_kv[0], w_out
     )
     send0, arrived = lax.optimization_barrier((send0, arrived))
     got0 = head_move(send0, (1, 2))
@@ -791,7 +838,9 @@
         head_move(pieces[3], (1, 2)),
     ]
     partial, handed = finish_first(1, pr_dev, bits, own1, got1, last1, held)
-    prefill_out, decode_out = finish_last(0, steps, slots, own0, got0, last0, pieces, partial)
+    prefill_out = finish_last(0, own0, got0, last0, partial)
+    pieces[1] = after(pieces[1], prefill_out)
+    decode_out = decode_sum(steps, slots, pieces)
     return (prefill_out, handed.reshape(1, pr_dev * n_seq, each, 2 * HD), decode_out)
 
 

time: 57.9 us -> 58.9 us (1.017)
  Pallas kernels: 28 us -> 30.7 us
  waiting for transfers between devices: 12.7 us -> 11 us
    pallas_call x1, Pallas kernels: 6.95 us -> 9.91 us  [second(): pl.pallas_call(functools.partial(second_kernel, n_seq, prompts), out_shap...]
    ppermute x7, waiting for transfers between devices: 7.41 us -> 5.51 us  [head_move(): return lax.ppermute(value, ('head', 'seq'), pairs)]
    ppermute x7, starting transfers between devices: 8.85 us -> 10.3 us  [head_move(): return lax.ppermute(value, ('head', 'seq'), pairs)]
    ppermute x6, starting transfers between devices: 7.25 us -> 5.97 us  [seq_move(): return lax.ppermute(value, 'seq', [(i, i ^ bit) for i in range(n_seq)])]
    pallas_call x1 -> x2, Pallas kernels: 1.53 us -> 1.55 us  [the longest x1 0.91 us: finish_last(): pl.pallas_call(functools.partial(finish_last_kernel, p), out_shape=jax.Sh...]
  transfers between devices with their start and end apart: 13 -> 13, of which waited for: 6 -> 5; matrix products, arithmetic and copies ran while one was open for 0% -> 0% of each run, Pallas kernels for 23% -> 29%
where the time goes in v2:
time: 58.9 us; the launch traced here: 58.7 us
  Pallas kernels  30.7 us (52%)
  starting transfers between devices  16.2 us (28%)
  waiting for transfers between devices  11 us (19%)
  between operations  0.83 us (1%)
    pallas_call x1, Pallas kernels, project(): pl.pallas_call(functools.partial(project_kernel, n_head, n_seq), out_shap...  12.8 us
    ppermute x7, starting transfers between devices, head_move(): return lax.ppermute(value, ('head', 'seq'), pairs)  10.3 us
    pallas_call x1, Pallas kernels, second(): pl.pallas_call(functools.partial(second_kernel, n_seq, prompts), out_shap...  9.91 us
    ppermute x6, starting transfers between devices, seq_move(): return lax.ppermute(value, 'seq', [(i, i ^ bit) for i in range(n_seq)])  5.97 us
    ppermute x7, waiting for transfers between devices, head_move(): return lax.ppermute(value, ('head', 'seq'), pairs)  5.51 us
    ppermute x6, waiting for transfers between devices, seq_move(): return lax.ppermute(value, 'seq', [(i, i ^ bit) for i in range(n_seq)])  5.47 us
    pallas_call x1, Pallas kernels, third(): pl.pallas_call(third_kernel, out_shape=[jax.ShapeDtypeStruct((rows, 2 * n...  3.56 us
    pallas_call x1, Pallas kernels, decode_project(): pl.pallas_call(functools.partial(decode_out_kernel, bit), out_shape=[jax....  1.28 us
  transfers between devices with their start and end apart: 13, of which 5 were waited for; matrix products, arithmetic and copies ran while one was open for 0% of the time, Pallas kernels for 29%

profile of v2, /device:TPU:0, one launch (start us, length us, event | category | flops | bytes accessed | tf_op | source)
XLA Modules:
  0.0 58.7 jit_solution(5279187281823597387)
XLA Ops:
  0.6 0.0 copy-start.1
  0.6 0.0 copy-start.2
  0.7 0.0 copy-start.3
  0.7 0.0 copy-start.4
  0.7 0.0 copy-start.5
  0.7 0.0 copy-start.6
  0.7 12.8 %project.1 = (bf16[256,2048]{1,0:T(8,128)(2,1)}, bf16[272,2048]{1,0:T(8,128)(2,1)}, bf16[8,64,256]{2,1,0:T(8,128)(2,1)}, bf16[4,64,256]{2,1,0:T(8,128)(2,1)}) custom-call(s32[16]{0:T(128)} %refs_0_.3, s32[4]{0:T(128)} %refs_1_.3, s32[4]{0:T(128)} %refs_2_.3, f32[1,128]{1,0:T(1,128)} %bitcast.13, f32[1,128]{1,0:T(1,128)} %bitcast.15, ...), custom_call_target="tpu_custom_call" | custom-call | flops 1 | bytes 1 | tf_op jit(solution)/shard_map/project/pallas_call | solution.py:356
  13.5 3.0 %collective-permute-start.3 = (bf16[256,2048]{1,0:T(8,128)(2,1)}, bf16[256,2048]{1,0:T(8,128)(2,1)S(1)}, u32[]{:S(2)}, u32[]{:S(2)}) collective-permute-start(bf16[256,2048]{1,0:T(8,128)(2,1)} %get-tuple-element.39), channel_id=1, source_target_pairs={{0,8},{1,17},{2,10},{3,19},{4,12},{5,21},{6,14},{7,23},{8,0},{9,25... | collective-permute-start | bytes 3145736 | tf_op jit(solution)/shard_map/ppermute | solution.py:792
  16.5 2.6 %collective-permute-start = (bf16[4,64,256]{2,1,0:T(8,128)(2,1)}, bf16[4,64,256]{2,1,0:T(8,128)(2,1)S(1)}, u32[]{:S(2)}, u32[]{:S(2)}) collective-permute-start(bf16[4,64,256]{2,1,0:T(8,128)(2,1)} %get-tuple-element.36), channel_id=1, source_target_pairs={{0,4},{1,5},{2,6},{3,7},{4,0},{5,1},{6,2},{7,3},{8,12},{9,13},{10,... | collective-permute-start | bytes 393224 | tf_op jit(solution)/shard_map/ppermute | solution.py:795
  19.1 0.0 copy-done.1
  19.1 0.0 copy-done.2
  19.1 0.0 copy-done.3
  19.1 0.0 copy-done.4
  19.1 0.0 copy-done.5
  19.1 0.0 copy-done.6
  19.1 9.9 %second.1 = (bf16[256,2048]{1,0:T(8,128)(2,1)S(1)}, bf16[256,1024]{1,0:T(8,128)(2,1)S(1)}, bf16[256,2048]{1,0:T(8,128)(2,1)S(1)}, f32[136,128]{1,0:T(8,128)S(1)}) custom-call(s32[16]{0:T(128)S(1)} %copy-done.3, s32[4]{0:T(128)S(1)} %copy-done.4, s32[4]{0:T(128)S(1)} %copy-done.5, f32[1,128]{1,0:T(1,128)S(1)} %bitcast.14, f32[256,256]{1,0:T(8,128)S(1)} %copy-done.1, ...), custom_call_target="tpu_custom_call" | custom-call | flops 1 | bytes 1 | tf_op jit(solution)/shard_map/second/pallas_call | solution.py:486
  29.1 0.0 collective-permute-done
  29.1 0.6 %collective-permute-start.1 = (bf16[256,2048]{1,0:T(8,128)(2,1)S(1)}, bf16[256,2048]{1,0:T(8,128)(2,1)S(1)}, u32[]{:S(2)}, u32[]{:S(2)}) collective-permute-start(bf16[256,2048]{1,0:T(8,128)(2,1)S(1)} %get-tuple-element.37), channel_id=1, source_target_pairs={{0,8},{1,17},{2,10},{3,19},{4,12},{5,21},{6,14},{7,23},{8,0},{9,25... | collective-permute-start | bytes 3145736 | tf_op jit(solution)/shard_map/ppermute | solution.py:792
  29.7 0.0 collective-permute-start.2
  29.7 0.0 copy-start
  29.7 3.6 %third.1 = (bf16[256,2048]{1,0:T(8,128)(2,1)S(1)}, bf16[2,1024,1024]{2,1,0:T(8,128)(2,1)S(1)}, bf16[2,1024,1024]{2,1,0:T(8,128)(2,1)S(1)}) custom-call(bf16[256,1024]{1,0:T(8,128)(2,1)S(1)} %get-tuple-element.33.attn, bf16[1024,4096]{1,0:T(8,128)(2,1)} %wo_hbm.1), custom_call_target="tpu_custom_call" | custom-call | flops 1 | bytes 1 | tf_op jit(solution)/shard_map/third/pallas_call | solution.py:545
  33.3 1.6 %collective-permute-done.2.other = f32[136,128]{1,0:T(8,128)S(1)} collective-permute-done((f32[136,128]{1,0:T(8,128)S(1)}, f32[136,128]{1,0:T(8,128)S(1)}, u32[]{:S(2)}, u32[]{:S(2)}) %collective-permute-start.2) | collective-permute-done | bytes 69664 | tf_op jit(solution)/shard_map/ppermute | solution.py:795
  34.9 0.0 collective-permute-done.3.got
  34.9 0.1 join_4.1.mine
  35.0 1.6 %collective-permute-start.4 = (f32[136,128]{1,0:T(8,128)S(1)}, f32[136,128]{1,0:T(8,128)S(1)}, u32[]{:S(2)}, u32[]{:S(2)}) collective-permute-start(f32[136,128]{1,0:T(8,128)S(1)} %join_4.1.mine), channel_id=1, source_target_pairs={{0,2},{1,3},{2,0},{3,1},{4,6},{5,7},{6,4},{7,5},{8,10},{9,11},{10,... | collective-permute-start | bytes 208904 | tf_op jit(solution)/shard_map/ppermute | solution.py:795
  36.7 3.0 %collective-permute-done.4.other = f32[136,128]{1,0:T(8,128)S(1)} collective-permute-done((f32[136,128]{1,0:T(8,128)S(1)}, f32[136,128]{1,0:T(8,128)S(1)}, u32[]{:S(2)}, u32[]{:S(2)}) %collective-permute-start.4) | collective-permute-done | bytes 69664 | tf_op jit(solution)/shard_map/ppermute | solution.py:795
  39.6 0.1 join_2.1.mine
  39.7 0.0 copy-done
  39.8 1.6 %collective-permute-start.6 = (bf16[2,2,64,256]{3,2,1,0:T(8,128)(2,1)S(1)}, bf16[2,2,64,256]{3,2,1,0:T(8,128)(2,1)S(1)}, u32[]{:S(2)}, u32[]{:S(2)}) collective-permute-start(bf16[2,2,64,256]{3,2,1,0:T(8,128)(2,1)S(1)} %hop_4.1), channel_id=1, source_target_pairs={{0,2},{1,3},{2,0},{3,1},{4,6},{5,7},{6,4},{7,5},{8,10},{9,11},{10,... | collective-permute-start | bytes 393224 | tf_op jit(solution)/shard_map/ppermute | solution.py:795
  41.4 0.0 collective-permute-start.5
  41.4 0.1 pass_on_1.1
  41.6 1.6 %collective-permute-start.8 = (bf16[256,1024]{1,0:T(8,128)(2,1)S(1)}, bf16[256,1024]{1,0:T(8,128)(2,1)S(1)}, u32[]{:S(2)}, u32[]{:S(2)}) collective-permute-start(bf16[256,1024]{1,0:T(8,128)(2,1)S(1)} %pass_on_1.1), channel_id=1, source_target_pairs={{0,16},{1,9},{2,18},{3,11},{4,20},{5,13},{6,22},{7,15},{8,24},{9,1... | collective-permute-start | bytes 1572872 | tf_op jit(solution)/shard_map/ppermute | solution.py:792
  43.2 0.8 %collective-permute-done.1.got = bf16[256,2048]{1,0:T(8,128)(2,1)S(1)} collective-permute-done((bf16[256,2048]{1,0:T(8,128)(2,1)S(1)}, bf16[256,2048]{1,0:T(8,128)(2,1)S(1)}, u32[]{:S(2)}, u32[]{:S(2)}) %collective-permute-start.1) | collective-permute-done | bytes 1048608 | tf_op jit(solution)/shard_map/ppermute | solution.py:792
  43.9 0.0 collective-permute-done.5.other
  43.9 0.9 %collective-permute-done.6.refs_2_ = bf16[2,2,64,256]{3,2,1,0:T(8,128)(2,1)S(1)} collective-permute-done((bf16[2,2,64,256]{3,2,1,0:T(8,128)(2,1)S(1)}, bf16[2,2,64,256]{3,2,1,0:T(8,128)(2,1)S(1)}, u32[]{:S(2)}, u32[]{:S(2)}) %collective-permute-start.6) | collective-permute-done | bytes 131104 | tf_op jit(solution)/shard_map/ppermute | solution.py:795
  44.8 0.1 pass_on_0.1
  45.0 1.6 %collective-permute-start.7 = (bf16[256,1024]{1,0:T(8,128)(2,1)S(1)}, bf16[256,1024]{1,0:T(8,128)(2,1)S(1)}, u32[]{:S(2)}, u32[]{:S(2)}) collective-permute-start(bf16[256,1024]{1,0:T(8,128)(2,1)S(1)} %pass_on_0.1), channel_id=1, source_target_pairs={{0,16},{1,9},{2,18},{3,11},{4,20},{5,13},{6,22},{7,15},{8,24},{9,1... | collective-permute-start | bytes 1572872 | tf_op jit(solution)/shard_map/ppermute | solution.py:792
  46.5 0.1 collective-permute-start.9
  46.6 1.3 %decode_project.1 = (bf16[16,1024]{1,0:T(8,128)(2,1)S(1)}, bf16[16,1024]{1,0:T(8,128)(2,1)S(1)}, bf16[16,1024]{1,0:T(8,128)(2,1)S(1)}, bf16[16,1024]{1,0:T(8,128)(2,1)S(1)}) custom-call(f32[136,128]{1,0:T(8,128)S(1)} %join_2.1.mine, f32[136,128]{1,0:T(8,128)S(1)} %collective-permute-done.5.other, bf16[2,1024,1024]{2,1,0:T(8,128)(2,1)S(1)} %get-tuple-element.54.wo_a, ...), custom_call_target="tpu_custom_call" | custom-call | flops 1 | bytes 1 | tf_op jit(solution)/shard_map/decode_project/pallas_call | solution.py:662
  47.9 0.5 collective-permute-start.10
  48.4 2.4 %collective-permute-start.11 = (bf16[16,1024]{1,0:T(8,128)(2,1)S(1)}, bf16[16,1024]{1,0:T(8,128)(2,1)S(1)}, u32[]{:S(2)}, u32[]{:S(2)}) collective-permute-start(bf16[16,1024]{1,0:T(8,128)(2,1)S(1)} %get-tuple-element.59), channel_id=1, source_target_pairs={{0,24},{1,25},{2,26},{3,27},{4,28},{5,29},{6,30},{7,31},{8,16},{9,... | collective-permute-start | bytes 98312 | tf_op jit(solution)/shard_map/ppermute | solution.py:792
  50.9 0.0 collective-permute-done.9.refs_3_
  50.9 0.5 collective-permute-start.12
  51.4 0.0 collective-permute-done.8.last
  51.4 1.0 %finish_1.1 = (bf16[2,256,1024]{2,1,0:T(8,128)(2,1)}, bf16[8,64,256]{2,1,0:T(8,128)(2,1)}) custom-call(bf16[256,2048]{1,0:T(8,128)(2,1)S(1)} %get-tuple-element.44.own, bf16[256,2048]{1,0:T(8,128)(2,1)S(1)} %collective-permute-done.3.got, bf16[256,1024]{1,0:T(8,128)(2,1)S(1)} %collective-permute-done.8.last, bf16[1,8,64,256]{3,2,1,0:T(8,128)(2,1)S(1)} %bitcast.8, ...), custom_call_target="tpu_custom_call" | custom-call | flops 1 | bytes 1 | tf_op jit(solution)/shard_map/finish_1/pallas_call | solution.py:712
  52.4 4.7 %collective-permute-done.7.last = bf16[256,1024]{1,0:T(8,128)(2,1)S(1)} collective-permute-done((bf16[256,1024]{1,0:T(8,128)(2,1)S(1)}, bf16[256,1024]{1,0:T(8,128)(2,1)S(1)}, u32[]{:S(2)}, u32[]{:S(2)}) %collective-permute-start.7) | collective-permute-done | bytes 524320 | tf_op jit(solution)/shard_map/ppermute | solution.py:792
  57.1 0.9 %finish_0.1 = bf16[2,256,1024]{2,1,0:T(8,128)(2,1)} custom-call(bf16[256,2048]{1,0:T(8,128)(2,1)S(1)} %get-tuple-element.34.own, bf16[256,2048]{1,0:T(8,128)(2,1)S(1)} %collective-permute-done.1.got, bf16[256,1024]{1,0:T(8,128)(2,1)S(1)} %collective-permute-done.7.last, bf16[2,256,1024]{2,1,0:T(8,128)(2,1)} %get-tuple-element.50._), custom_call_target="tpu_custom_call", output_to_operand_aliasing={{}: (3, {})} | custom-call | flops 1 | bytes 1 | tf_op jit(solution)/shard_map/finish_0/pallas_call | solution.py:738
  58.1 0.0 collective-permute-done.10.refs_1_
  58.1 0.0 collective-permute-done.11.refs_2_
  58.1 0.0 collective-permute-done.12.refs_3_
  58.1 0.6 %decode_sum.1 = bf16[4,4,1024]{2,1,0:T(4,128)(2,1)} custom-call(bf16[16,1024]{1,0:T(8,128)(2,1)S(1)} %get-tuple-element.56.refs_0_, bf16[16,1024]{1,0:T(8,128)(2,1)S(1)} %collective-permute-done.10.refs_1_, bf16[16,1024]{1,0:T(8,128)(2,1)S(1)} %collective-permute-done.11.refs_2_, bf16[16,1024]{1,0:T(8,128)(2,1)S(1)} %collective-permute-done.12.refs_3_), custom_call_target="tpu_custom_call" | custom-call | flops 1 | bytes 1 | tf_op jit(solution)/shard_map/decode_sum/pallas_call | solution.py:761
  (2 shorter events, 0.0 us)
Async XLA Ops:
  0.6 18.5 %copy-start.1 = (f32[256,256]{1,0:T(8,128)S(1)}, f32[256,256]{1,0:T(8,128)}, u32[]{:S(2)}) copy-start(f32[256,256]{1,0:T(8,128)} %constant.2.clone.refs_5_.refs_4_) | copy-start | bytes 786436
  0.6 18.5 %copy-start.2 = (bf16[1,4,512,256]{3,2,1,0:T(8,128)(2,1)S(1)}, bf16[1,4,512,256]{3,2,1,0:T(8,128)(2,1)}, u32[]{:S(2)}) copy-start(bf16[1,4,512,256]{3,2,1,0:T(8,128)(2,1)} %param.17) | copy-start | bytes 3145732
  0.7 18.4 %copy-start.3 = (s32[16]{0:T(128)S(1)}, s32[16]{0:T(128)}, u32[]{:S(2)}) copy-start(s32[16]{0:T(128)} %refs_0_.3) | copy-start | bytes 196
  0.7 18.4 %copy-start.4 = (s32[4]{0:T(128)S(1)}, s32[4]{0:T(128)}, u32[]{:S(2)}) copy-start(s32[4]{0:T(128)} %refs_1_.3) | copy-start | bytes 52
  0.7 18.4 %copy-start.5 = (s32[4]{0:T(128)S(1)}, s32[4]{0:T(128)}, u32[]{:S(2)}) copy-start(s32[4]{0:T(128)} %refs_2_.3) | copy-start | bytes 52
  0.7 18.4 %copy-start.6 = (f32[128]{0:T(128)S(1)}, f32[128]{0:T(128)}, u32[]{:S(2)}) copy-start(f32[128]{0:T(128)} %param.23) | copy-start | bytes 1540
  13.5 21.4 %collective-permute-start.3 = (bf16[256,2048]{1,0:T(8,128)(2,1)}, bf16[256,2048]{1,0:T(8,128)(2,1)S(1)}, u32[]{:S(2)}, u32[]{:S(2)}) collective-permute-start(bf16[256,2048]{1,0:T(8,128)(2,1)} %get-tuple-element.39), channel_id=1, source_target_pairs={{0,8},{1,17},{2,10},{3,19},{4,12},{5,21},{6,14},{7,23},{8,0},{9,25... | collective-permute-start | bytes 3145736 | tf_op jit(solution)/shard_map/ppermute | solution.py:792
  16.5 12.5 %collective-permute-start = (bf16[4,64,256]{2,1,0:T(8,128)(2,1)}, bf16[4,64,256]{2,1,0:T(8,128)(2,1)S(1)}, u32[]{:S(2)}, u32[]{:S(2)}) collective-permute-start(bf16[4,64,256]{2,1,0:T(8,128)(2,1)} %get-tuple-element.36), channel_id=1, source_target_pairs={{0,4},{1,5},{2,6},{3,7},{4,0},{5,1},{6,2},{7,3},{8,12},{9,13},{10,... | collective-permute-start | bytes 393224 | tf_op jit(solution)/shard_map/ppermute | solution.py:795
  29.1 14.9 %collective-permute-start.1 = (bf16[256,2048]{1,0:T(8,128)(2,1)S(1)}, bf16[256,2048]{1,0:T(8,128)(2,1)S(1)}, u32[]{:S(2)}, u32[]{:S(2)}) collective-permute-start(bf16[256,2048]{1,0:T(8,128)(2,1)S(1)} %get-tuple-element.37), channel_id=1, source_target_pairs={{0,8},{1,17},{2,10},{3,19},{4,12},{5,21},{6,14},{7,23},{8,0},{9,25... | collective-permute-start | bytes 3145736 | tf_op jit(solution)/shard_map/ppermute | solution.py:792
  29.7 5.2 %collective-permute-start.2 = (f32[136,128]{1,0:T(8,128)S(1)}, f32[136,128]{1,0:T(8,128)S(1)}, u32[]{:S(2)}, u32[]{:S(2)}) collective-permute-start(f32[136,128]{1,0:T(8,128)S(1)} %get-tuple-element.38.mine), channel_id=1, source_target_pairs={{0,4},{1,5},{2,6},{3,7},{4,0},{5,1},{6,2},{7,3},{8,12},{9,13},{10,... | collective-permute-start | bytes 208904 | tf_op jit(solution)/shard_map/ppermute | solution.py:795
  29.7 10.1 %copy-start = (bf16[8,64,256]{2,1,0:T(8,128)(2,1)S(1)}, bf16[8,64,256]{2,1,0:T(8,128)(2,1)}, u32[]{:S(2)}) copy-start(bf16[8,64,256]{2,1,0:T(8,128)(2,1)} %get-tuple-element.41) | copy-start | bytes 786436
  35.0 4.6 %collective-permute-start.4 = (f32[136,128]{1,0:T(8,128)S(1)}, f32[136,128]{1,0:T(8,128)S(1)}, u32[]{:S(2)}, u32[]{:S(2)}) collective-permute-start(f32[136,128]{1,0:T(8,128)S(1)} %join_4.1.mine), channel_id=1, source_target_pairs={{0,2},{1,3},{2,0},{3,1},{4,6},{5,7},{6,4},{7,5},{8,10},{9,11},{10,... | collective-permute-start | bytes 208904 | tf_op jit(solution)/shard_map/ppermute | solution.py:795
  39.8 5.0 %collective-permute-start.6 = (bf16[2,2,64,256]{3,2,1,0:T(8,128)(2,1)S(1)}, bf16[2,2,64,256]{3,2,1,0:T(8,128)(2,1)S(1)}, u32[]{:S(2)}, u32[]{:S(2)}) collective-permute-start(bf16[2,2,64,256]{3,2,1,0:T(8,128)(2,1)S(1)} %hop_4.1), channel_id=1, source_target_pairs={{0,2},{1,3},{2,0},{3,1},{4,6},{5,7},{6,4},{7,5},{8,10},{9,11},{10,... | collective-permute-start | bytes 393224 | tf_op jit(solution)/shard_map/ppermute | solution.py:795
  41.4 2.5 %collective-permute-start.5 = (f32[136,128]{1,0:T(8,128)S(1)}, f32[136,128]{1,0:T(8,128)S(1)}, u32[]{:S(2)}, u32[]{:S(2)}) collective-permute-start(f32[136,128]{1,0:T(8,128)S(1)} %join_2.1.mine), channel_id=1, source_target_pairs={{0,1},{1,0},{2,3},{3,2},{4,5},{5,4},{6,7},{7,6},{8,9},{9,8},{10,11... | collective-permute-start | bytes 208904 | tf_op jit(solution)/shard_map/ppermute | solution.py:795
  41.6 9.8 %collective-permute-start.8 = (bf16[256,1024]{1,0:T(8,128)(2,1)S(1)}, bf16[256,1024]{1,0:T(8,128)(2,1)S(1)}, u32[]{:S(2)}, u32[]{:S(2)}) collective-permute-start(bf16[256,1024]{1,0:T(8,128)(2,1)S(1)} %pass_on_1.1), channel_id=1, source_target_pairs={{0,16},{1,9},{2,18},{3,11},{4,20},{5,13},{6,22},{7,15},{8,24},{9,1... | collective-permute-start | bytes 1572872 | tf_op jit(solution)/shard_map/ppermute | solution.py:792
  45.0 12.2 %collective-permute-start.7 = (bf16[256,1024]{1,0:T(8,128)(2,1)S(1)}, bf16[256,1024]{1,0:T(8,128)(2,1)S(1)}, u32[]{:S(2)}, u32[]{:S(2)}) collective-permute-start(bf16[256,1024]{1,0:T(8,128)(2,1)S(1)} %pass_on_0.1), channel_id=1, source_target_pairs={{0,16},{1,9},{2,18},{3,11},{4,20},{5,13},{6,22},{7,15},{8,24},{9,1... | collective-permute-start | bytes 1572872 | tf_op jit(solution)/shard_map/ppermute | solution.py:792
  46.5 4.3 %collective-permute-start.9 = (bf16[4,1,64,256]{3,2,1,0:T(8,128)(2,1)S(1)}, bf16[4,1,64,256]{3,2,1,0:T(8,128)(2,1)S(1)}, u32[]{:S(2)}, u32[]{:S(2)}) collective-permute-start(bf16[4,1,64,256]{3,2,1,0:T(8,128)(2,1)S(1)} %hop_2.1), channel_id=1, source_target_pairs={{0,1},{1,0},{2,3},{3,2},{4,5},{5,4},{6,7},{7,6},{8,9},{9,8},{10,11... | collective-permute-start | bytes 393224 | tf_op jit(solution)/shard_map/ppermute | solution.py:795
  47.9 10.2 %collective-permute-start.10 = (bf16[16,1024]{1,0:T(8,128)(2,1)S(1)}, bf16[16,1024]{1,0:T(8,128)(2,1)S(1)}, u32[]{:S(2)}, u32[]{:S(2)}) collective-permute-start(bf16[16,1024]{1,0:T(8,128)(2,1)S(1)} %get-tuple-element.57), channel_id=1, source_target_pairs={{0,16},{1,9},{2,18},{3,11},{4,20},{5,13},{6,22},{7,15},{8,24},{9,1... | collective-permute-start | bytes 98312 | tf_op jit(solution)/shard_map/ppermute | solution.py:792
  48.4 9.6 %collective-permute-start.11 = (bf16[16,1024]{1,0:T(8,128)(2,1)S(1)}, bf16[16,1024]{1,0:T(8,128)(2,1)S(1)}, u32[]{:S(2)}, u32[]{:S(2)}) collective-permute-start(bf16[16,1024]{1,0:T(8,128)(2,1)S(1)} %get-tuple-element.59), channel_id=1, source_target_pairs={{0,24},{1,25},{2,26},{3,27},{4,28},{5,29},{6,30},{7,31},{8,16},{9,... | collective-permute-start | bytes 98312 | tf_op jit(solution)/shard_map/ppermute | solution.py:792
  50.9 7.2 %collective-permute-start.12 = (bf16[16,1024]{1,0:T(8,128)(2,1)S(1)}, bf16[16,1024]{1,0:T(8,128)(2,1)S(1)}, u32[]{:S(2)}, u32[]{:S(2)}) collective-permute-start(bf16[16,1024]{1,0:T(8,128)(2,1)S(1)} %get-tuple-element.60), channel_id=1, source_target_pairs={{0,8},{1,17},{2,10},{3,19},{4,12},{5,21},{6,14},{7,23},{8,0},{9,25... | collective-permute-start | bytes 98312 | tf_op jit(solution)/shard_map/ppermute | solution.py:792

commit v3 on v1

--- a/solution.py
+++ b/solution.py
@@ -105,12 +105,12 @@
     return jnp.where((col_at <= row_at) & (col_at < length), 0.0, NEG).astype(F32)
 
 
-def attention(heads, queries, kv, bias_v, s_v, w_v, attn):
+def attention(heads, queries, kv, bias_v, s_v, w_v, attn, skip=0):
     rows = kv.shape[0]
     half = rows // 2
     quarter = rows // 4
     for h in heads:
-        at = slice(h * HD, (h + 1) * HD)
+        at = slice((h - skip) * HD, (h - skip + 1) * HD)
         s_v[h, :half, :half] = dot_nt(queries[:half, at], kv[:half, :HD])
         s_v[h, half:, :] = dot_nt(queries[half:, at], kv[:, :HD])
     for h in heads:
@@ -202,11 +202,11 @@
 
 def project_kernel(n_head, n_seq, *refs):
     plen_h, adm_h, clen_h, qg_h, kg_h, table_h, x_hbm, dec_hbm, wq_hbm, wk_hbm, wv_hbm, wo_hbm = refs[:12]
-    send_h, pack_h, blocks_h, leave_h = refs[12:16]
-    x_v, dec_v, flat_v, wkv_v, wq_v, wo_v, raw, raw_kv, send, pack, blocks = refs[16:27]
-    plen, adm, clen, qg, kg, table = refs[27:33]
-    bias_v, s_v, w_v = refs[33:36]
-    x_sem, dec_sem, wkv_sem, wq_sem, wo_sem, small_sem, out_sem = refs[36:]
+    pass_h, keep_h, pack_h, blocks_h, leave_h = refs[12:17]
+    x_v, dec_v, flat_v, wkv_v, wq_v, wo_v, raw, raw_kv, send, pack, blocks = refs[17:28]
+    plen, adm, clen, qg, kg, table = refs[28:34]
+    bias_v, s_v, w_v = refs[34:37]
+    x_sem, dec_sem, wkv_sem, wq_sem, wo_sem, small_sem, out_sem = refs[37:]
     prompts, rows, width = x_hbm.shape
     steps, slots, _ = dec_hbm.shape
     dec_rows = steps * slots
@@ -245,7 +245,7 @@
     o_copies = [
         out_copy(wo_hbm, block, nb, wo_v.at[j], wo_sem.at[j]) for j, block in enumerate((diag, first))
     ]
-    ahead = 3
+    ahead = 4
     queue += [[copy] for copy in o_copies]
     for copy in [dec_copy] + queue[0] + small:
         copy.start()
@@ -325,18 +325,22 @@
             pack[:rows, col : col + HD] = rope(norm(piece, qg[...]), cos2, sin2).astype(BF)
     outs.append(pltpu.make_async_copy(pack, pack_h, out_sem.at[2]))
     outs[-1].start()
-    for j in range(2):
-        at = pl.ds(j * nb, nb)
-        send[:, at] = dot(mine[...], wo_v[j]).astype(BF)
-        outs.append(pltpu.make_async_copy(send.at[:, at], send_h.at[:, at], out_sem.at[3 + j]))
+    hb = nb // 2
+    for j in range(4):
+        at = pl.ds(j % 2 * hb, hb)
+        send[j // 2, :, at] = dot(mine[...], wo_v[j // 2, :, at]).astype(BF)
+        target = (pass_h, keep_h)[j // 2]
+        outs.append(
+            pltpu.make_async_copy(send.at[j // 2, :, at], target.at[:, at], out_sem.at[3 + j])
+        )
         outs[-1].start()
     for copy in outs:
         copy.wait()
 
 
 def cut_points(width):
-    step = width // 8
-    return [0, step, 2 * step, 4 * step, 6 * step, 8 * step]
+    step = width // 16
+    return [step * i for i in (0, 1, 2, 4, 8, 12, 16)]
 
 
 def project(n_head, n_seq, plen, adm, clen, qg, kg, table, x, dec, wq, wk, wv, wo):
@@ -345,20 +349,21 @@
     local = wq.shape[1]
     nb = width // n_head
     every = prompts * rows + dec_rows
-    send = (rows, 2 * nb)
+    send = (rows, nb)
     pack = (rows + dec_rows, 2 * prompts * HD + prompts * local)
     blocks = (n_seq, prompts * rows // n_seq, 2 * HD)
     chunks = len(cut_points(width)) - 1
     return pl.pallas_call(
         functools.partial(project_kernel, n_head, n_seq),
         out_shape=[
+            jax.ShapeDtypeStruct(send, BF),
             jax.ShapeDtypeStruct(send, BF),
             jax.ShapeDtypeStruct(pack, BF),
             jax.ShapeDtypeStruct(blocks, BF),
             jax.ShapeDtypeStruct((n_seq // 2,) + blocks[1:], BF),
         ],
         in_specs=[HB] * 12,
-        out_specs=[HB] * 4,
+        out_specs=[HB] * 5,
         scratch_shapes=[
             pltpu.VMEM((every, width), BF),
             pltpu.VMEM(dec.shape, BF),
@@ -368,7 +373,7 @@
             pltpu.VMEM((2, local, nb), BF),
             pltpu.VMEM((rows + dec_rows, local), F32),
             pltpu.VMEM((every, 2 * HD), F32),
-            pltpu.VMEM(send, BF),
+            pltpu.VMEM((2,) + send, BF),
             pltpu.VMEM(pack, BF),
             pltpu.VMEM(blocks, BF),
             pltpu.SMEM(plen.shape, jnp.int32),
@@ -386,7 +391,7 @@
             pltpu.SemaphoreType.DMA((chunks,)),
             pltpu.SemaphoreType.DMA((2,)),
             pltpu.SemaphoreType.DMA((6,)),
-            pltpu.SemaphoreType.DMA((5,)),
+            pltpu.SemaphoreType.DMA((7,)),
         ],
         compiler_params=pltpu.CompilerParams(vmem_limit_bytes=LIMIT_A * MIB),
         cost_estimate=BRIEF,
@@ -396,10 +401,10 @@
 
 def second_kernel(n_seq, prompts, *refs):
     plen_h, adm_h, clen_h, pack_h, cache_h, wo_hbm = refs[:6]
-    send, attn, own1, part = refs[6:10]
-    pack, cache, wo_v, plen, adm, clen = refs[10:16]
-    bias_v, s_v, w_v = refs[16:19]
-    pack_sem, small_sem, wo_sem, cache_sem = refs[19:]
+    pass_v, keep_v, attn, own1, part = refs[6:11]
+    pack, cache, wo_v, plen, adm, clen = refs[11:17]
+    bias_v, s_v, w_v = refs[17:20]
+    pack_sem, small_sem, wo_sem, cache_sem = refs[20:]
     rows = attn.shape[0]
     dec_rows = pack.shape[0] - rows
     _, local, nb = wo_v.shape
@@ -441,8 +446,8 @@
     cache_copy.wait()
     for copy in copies[2:]:
         copy.wait()
-    for j in range(2):
-        send[:, j * nb : (j + 1) * nb] = dot(attn[...], wo_v[2 + j]).astype(BF)
+    for j, send in enumerate((pass_v, keep_v)):
+        send[...] = dot(attn[...], wo_v[2 + j]).astype(BF)
     decode_attention(
         n_seq, cache.shape[0], plen, adm, clen, pack.at[pl.ds(rows, dec_rows), pl.ds(base, local)],
         pack.at[pl.ds(rows, dec_rows), pl.ds(0, both)], kvs, cache, part,
@@ -456,13 +461,14 @@
     return pl.pallas_call(
         functools.partial(second_kernel, n_seq, prompts),
         out_shape=[
-            jax.ShapeDtypeStruct((rows, 2 * nb), BF),
+            jax.ShapeDtypeStruct((rows, nb), BF),
+            jax.ShapeDtypeStruct((rows, nb), BF),
             jax.ShapeDtypeStruct((rows, local), BF),
             jax.ShapeDtypeStruct((rows, 2 * nb), BF),
             jax.ShapeDtypeStruct((dec_rows * (local // HD) + 8, HD), F32),
         ],
         in_specs=[HB] * 6,
-        out_specs=[VM] * 4,
+        out_specs=[VM] * 5,
         scratch_shapes=[
             pltpu.VMEM(pack.shape, BF),
             pltpu.VMEM(cache.shape, BF),
@@ -595,14 +601,13 @@
 
 def pass_on_kernel(own, got, on):
     nb = on.shape[1]
-    on[...] = (own[:, nb:].astype(F32) + got[:, :nb].astype(F32)).astype(BF)
+    on[...] = (own[:, nb:].astype(F32) + got[...].astype(F32)).astype(BF)
 
 
 def pass_on(p, own, got):
-    rows, both = got.shape
     return pl.pallas_call(
         pass_on_kernel,
-        out_shape=jax.ShapeDtypeStruct((rows, both // 2), BF),
+        out_shape=jax.ShapeDtypeStruct(got.shape, BF),
         in_specs=[VM] * 2,
         out_specs=VM,
         compiler_params=pltpu.CompilerParams(vmem_limit_bytes=8 * MIB),
@@ -641,7 +646,7 @@
     for i in range(2):
         at = pl.ds(i * step, step)
         stage[at] = (
-            own[at, :nb].astype(F32) + got[at, nb:].astype(F32) + last[at].astype(F32)
+            own[at, :nb].astype(F32) + got[at].astype(F32) + last[at].astype(F32)
         ).astype(BF)
         copies.append(pltpu.make_async_copy(stage.at[at], out.at[at], sems.at[i]))
         copies[-1].start()
@@ -692,34 +697,45 @@
     )(own, got, last, *held)
 
 
-def finish_last_kernel(p, slots, own, got, last, *refs):
-    pieces, (_, out, dec_out, stage, sems) = refs[:-5], refs[-5:]
-    copies = sum_parts(stage, out.at[p], sems, own, got, last)
+def finish_last_kernel(p, own, got, last, _, out, stage, sems):
+    for copy in sum_parts(stage, out.at[p], sems, own, got, last):
+        copy.wait()
+
+
+def finish_last(p, own, got, last, partial):
+    rows, nb = last.shape
+    return pl.pallas_call(
+        functools.partial(finish_last_kernel, p),
+        out_shape=jax.ShapeDtypeStruct(partial.shape, BF),
+        in_specs=[VM] * 3 + [HB],
+        out_specs=HB,
+        scratch_shapes=[pltpu.VMEM((rows, nb), BF), pltpu.SemaphoreType.DMA((2,))],
+        input_output_aliases={3: 0},
+        compiler_params=pltpu.CompilerParams(vmem_limit_bytes=8 * MIB),
+        cost_estimate=BRIEF,
+        name="finish_%d" % p,
+    )(own, got, last, partial)
+
+
+def decode_sum_kernel(slots, *refs):
+    pieces, out = refs[:-1], refs[-1]
     total = pieces[0][...].astype(F32)
     for piece in pieces[1:]:
         total = total + piece[...].astype(F32)
-    for t in range(dec_out.shape[0]):
-        dec_out[t] = total[t * slots : (t + 1) * slots].astype(BF)
-    for copy in copies:
-        copy.wait()
-
-
-def finish_last(p, steps, slots, own, got, last, pieces, partial):
-    rows, nb = last.shape
-    return pl.pallas_call(
-        functools.partial(finish_last_kernel, p, slots),
-        out_shape=[
-            jax.ShapeDtypeStruct(partial.shape, BF),
-            jax.ShapeDtypeStruct((steps, slots, nb), BF),
-        ],
-        in_specs=[VM] * (3 + len(pieces)) + [HB],
-        out_specs=[HB, VM],
-        scratch_shapes=[pltpu.VMEM((rows, nb), BF), pltpu.SemaphoreType.DMA((2,))],
-        input_output_aliases={3 + len(pieces): 0},
+    for t in range(out.shape[0]):
+        out[t] = total[t * slots : (t + 1) * slots].astype(BF)
+
+
+def decode_sum(steps, slots, pieces):
+    return pl.pallas_call(
+        functools.partial(decode_sum_kernel, slots),
+        out_shape=jax.ShapeDtypeStruct((steps, slots, pieces[0].shape[1]), BF),
+        in_specs=[VM] * len(pieces),
+        out_specs=VM,
         compiler_params=pltpu.CompilerParams(vmem_limit_bytes=8 * MIB),
         cost_estimate=BRIEF,
-        name="finish_%d" % p,
-    )(own, got, last, *pieces, partial)
+        name="decode_sum",
+    )(*pieces)
 
 
 def after(value, other):
@@ -754,29 +770,31 @@
 
     table = jnp.asarray(prompt_table(rows))
     scalars = (prompt_len, admitted, cache_len)
-    send1, pack, blocks, leave = project(
+    pass1, keep1, pack, blocks, leave = project(
         n_head, n_seq, *scalars, qg, kg, table, prompts, dec_tokens, w_query, w_key, w_value, w_out
     )
-    got1 = head_move(send1, (1, 2))
+    pass1 = head_move(pass1, (1, 2))
+    keep1 = head_move(keep1, (1, 2))
     arrived = seq_move(leave, bits[0])
-    send0, attn0, own1, part = second(
+    pass0, keep0, attn0, own1, part = second(
         n_head, n_seq, pr_dev, rows, *scalars, pack, cache_kv[0], w_out
     )
-    send0, arrived = lax.optimization_barrier((send0, arrived))
-    got0 = head_move(send0, (1, 2))
+    pass0, keep0, arrived = lax.optimization_barrier((pass0, keep0, arrived))
+    pass0 = head_move(pass0, (1, 2))
+    keep0 = head_move(keep0, (1, 2))
     other = seq_move(part, bits[0])
     own0, *wo = third(n_head, attn0, w_out)
-    other, got1 = lax.optimization_barrier((other, got1, own0))[:2]
+    other, pass1, keep1 = lax.optimization_barrier((other, pass1, keep1, own0))[:3]
     for i, bit in enumerate(bits[:-1]):
         part = join(bit, part, other)
         other = seq_move(part, bits[i + 1])
     held = [blocks[None], after(arrived, part)[None]]
     leave = hop(bits[0], held)
     held.append(seq_move(leave, bits[1]))
-    on1 = pass_on(1, own1, after(got1, part))
+    on1 = pass_on(1, own1, after(pass1, part))
     last1 = head_move(on1, (2, 1))
-    got0, other, held[-1] = lax.optimization_barrier((got0, other, held[-1], on1))[:3]
-    on0 = pass_on(0, own0, got0)
+    pass0, keep0, other, held[-1] = lax.optimization_barrier((pass0, keep0, other, held[-1], on1))[:4]
+    on0 = pass_on(0, own0, pass0)
     last0 = head_move(on0, (2, 1))
     held[-1] = after(held[-1], on0)
     for i, bit in enumerate(bits[1:-1]):
@@ -790,8 +808,10 @@
         head_move(pieces[2], (3, 3)),
         head_move(pieces[3], (1, 2)),
     ]
-    partial, handed = finish_first(1, pr_dev, bits, own1, got1, last1, held)
-    prefill_out, decode_out = finish_last(0, steps, slots, own0, got0, last0, pieces, partial)
+    partial, handed = finish_first(1, pr_dev, bits, own1, keep1, last1, held)
+    prefill_out = finish_last(0, own0, keep0, last0, partial)
+    pieces[1] = after(pieces[1], prefill_out)
+    decode_out = decode_sum(steps, slots, pieces)
     return (prefill_out, handed.reshape(1, pr_dev * n_seq, each, 2 * HD), decode_out)
 
 

time: 57.9 us -> 58.2 us (level)
  starting transfers between devices: 16.1 us -> 18.3 us
  waiting for transfers between devices: 12.7 us -> 10.8 us
    ppermute x7 -> x9, starting transfers between devices: 8.85 us -> 11.8 us  [head_move(): return lax.ppermute(value, ('head', 'seq'), pairs)]
    ppermute x7 -> x9, waiting for transfers between devices: 7.41 us -> 4.73 us  [head_move(): return lax.ppermute(value, ('head', 'seq'), pairs)]
    ppermute x6, starting transfers between devices: 7.25 us -> 6.42 us  [seq_move(): return lax.ppermute(value, 'seq', [(i, i ^ bit) for i in range(n_seq)])]
    ppermute x6, waiting for transfers between devices: 5.25 us -> 6.02 us  [seq_move(): return lax.ppermute(value, 'seq', [(i, i ^ bit) for i in range(n_seq)])]
    pallas_call x3 -> x4, Pallas kernels: 1.79 us -> 1.81 us  [the longest x1 0.91 us: finish_last(): pl.pallas_call(functools.partial(finish_last_kernel, p), out_shape=jax.Sh...]
  transfers between devices with their start and end apart: 13 -> 15, of which waited for: 6 -> 4; matrix products, arithmetic and copies ran while one was open for 0% -> 0% of each run, Pallas kernels for 23% -> 25%
where the time goes in v3:
time: 58.2 us; the launch traced here: 58 us
  Pallas kernels  28.2 us (48%)
  starting transfers between devices  18.3 us (31%)
  waiting for transfers between devices  10.8 us (19%)
  between operations  0.8 us (1%)
    pallas_call x1, Pallas kernels, project(): pl.pallas_call(functools.partial(project_kernel, n_head, n_seq), out_shap...  13.2 us
    ppermute x9, starting transfers between devices, head_move(): return lax.ppermute(value, ('head', 'seq'), pairs)  11.8 us
    pallas_call x1, Pallas kernels, second(): pl.pallas_call(functools.partial(second_kernel, n_seq, prompts), out_shap...  6.99 us
    ppermute x6, starting transfers between devices, seq_move(): return lax.ppermute(value, 'seq', [(i, i ^ bit) for i in range(n_seq)])  6.42 us
    ppermute x6, waiting for transfers between devices, seq_move(): return lax.ppermute(value, 'seq', [(i, i ^ bit) for i in range(n_seq)])  6.02 us
    ppermute x9, waiting for transfers between devices, head_move(): return lax.ppermute(value, ('head', 'seq'), pairs)  4.73 us
    pallas_call x1, Pallas kernels, third(): pl.pallas_call(third_kernel, out_shape=[jax.ShapeDtypeStruct((rows, 2 * n...  3.56 us
    pallas_call x1, Pallas kernels, decode_project(): pl.pallas_call(functools.partial(decode_out_kernel, bit), out_shape=[jax....  1.28 us
  transfers between devices with their start and end apart: 15, of which 4 were waited for; matrix products, arithmetic and copies ran while one was open for 0% of the time, Pallas kernels for 25%

profile of v3, /device:TPU:0, one launch (start us, length us, event | category | flops | bytes accessed | tf_op | source)
XLA Modules:
  0.0 58.0 jit_solution(16225326312437006421)
XLA Ops:
  0.6 0.0 copy-start.1
  0.6 0.0 copy-start.2
  0.7 0.0 copy-start.3
  0.7 0.0 copy-start.4
  0.7 13.2 %project.1 = (bf16[256,1024]{1,0:T(8,128)(2,1)}, bf16[256,1024]{1,0:T(8,128)(2,1)}, bf16[272,2560]{1,0:T(8,128)(2,1)}, bf16[8,64,256]{2,1,0:T(8,128)(2,1)}, bf16[4,64,256]{2,1,0:T(8,128)(2,1)}) custom-call(s32[16]{0:T(128)} %refs_0_.3, s32[4]{0:T(128)} %refs_1_.3, s32[4]{0:T(128)} %refs_2_.3, f32[1,128]{1,0:T(1,128)} %bitcast.13, f32[1,128]{1,0:T(1,128)} %bitcast.14, ...), custom_call_target="tpu_custom_call" | custom-call | flops 1 | bytes 1 | tf_op jit(solution)/shard_map/project/pallas_call | solution.py:356
  13.9 3.0 %collective-permute-start.4 = (bf16[256,1024]{1,0:T(8,128)(2,1)}, bf16[256,1024]{1,0:T(8,128)(2,1)S(1)}, u32[]{:S(2)}, u32[]{:S(2)}) collective-permute-start(bf16[256,1024]{1,0:T(8,128)(2,1)} %get-tuple-element.46), channel_id=1, source_target_pairs={{0,8},{1,17},{2,10},{3,19},{4,12},{5,21},{6,14},{7,23},{8,0},{9,25... | collective-permute-start | bytes 1572872 | tf_op jit(solution)/shard_map/ppermute | solution.py:761
  16.9 0.1 collective-permute-start.5
  17.0 3.0 %collective-permute-start = (bf16[4,64,256]{2,1,0:T(8,128)(2,1)}, bf16[4,64,256]{2,1,0:T(8,128)(2,1)S(1)}, u32[]{:S(2)}, u32[]{:S(2)}) collective-permute-start(bf16[4,64,256]{2,1,0:T(8,128)(2,1)} %get-tuple-element.42), channel_id=1, source_target_pairs={{0,4},{1,5},{2,6},{3,7},{4,0},{5,1},{6,2},{7,3},{8,12},{9,13},{10,... | collective-permute-start | bytes 393224 | tf_op jit(solution)/shard_map/ppermute | solution.py:764
  20.0 0.0 copy-done.1
  20.0 0.0 copy-done.2
  20.0 0.0 copy-done.3
  20.0 0.0 copy-done.4
  20.1 7.0 %second.1 = (bf16[256,1024]{1,0:T(8,128)(2,1)S(1)}, bf16[256,1024]{1,0:T(8,128)(2,1)S(1)}, bf16[256,1024]{1,0:T(8,128)(2,1)S(1)}, bf16[256,2048]{1,0:T(8,128)(2,1)S(1)}, f32[136,128]{1,0:T(8,128)S(1)}) custom-call(s32[16]{0:T(128)S(1)} %copy-done.2, s32[4]{0:T(128)S(1)} %copy-done.3, s32[4]{0:T(128)S(1)} %copy-done.4, ...), custom_call_target="tpu_custom_call" | custom-call | flops 1 | bytes 1 | tf_op jit(solution)/shard_map/second/pallas_call | solution.py:461
  27.1 0.0 collective-permute-done
  27.1 1.6 %collective-permute-start.1 = (bf16[256,1024]{1,0:T(8,128)(2,1)S(1)}, bf16[256,1024]{1,0:T(8,128)(2,1)S(1)}, u32[]{:S(2)}, u32[]{:S(2)}) collective-permute-start(bf16[256,1024]{1,0:T(8,128)(2,1)S(1)} %get-tuple-element.43), channel_id=1, source_target_pairs={{0,8},{1,17},{2,10},{3,19},{4,12},{5,21},{6,14},{7,23},{8,0},{9,25... | collective-permute-start | bytes 1572872 | tf_op jit(solution)/shard_map/ppermute | solution.py:761
  28.6 0.5 collective-permute-start.2
  29.2 0.0 collective-permute-start.3
  29.2 0.0 copy-start
  29.2 3.6 %third.1 = (bf16[256,2048]{1,0:T(8,128)(2,1)S(1)}, bf16[2,1024,1024]{2,1,0:T(8,128)(2,1)S(1)}, bf16[2,1024,1024]{2,1,0:T(8,128)(2,1)S(1)}) custom-call(bf16[256,1024]{1,0:T(8,128)(2,1)S(1)} %get-tuple-element.38.attn, bf16[1024,4096]{1,0:T(8,128)(2,1)} %wo_hbm.1), custom_call_target="tpu_custom_call" | custom-call | flops 1 | bytes 1 | tf_op jit(solution)/shard_map/third/pallas_call | solution.py:515
  32.7 1.6 %collective-permute-done.3.other = f32[136,128]{1,0:T(8,128)S(1)} collective-permute-done((f32[136,128]{1,0:T(8,128)S(1)}, f32[136,128]{1,0:T(8,128)S(1)}, u32[]{:S(2)}, u32[]{:S(2)}) %collective-permute-start.3) | collective-permute-done | bytes 69664 | tf_op jit(solution)/shard_map/ppermute | solution.py:764
  34.4 0.0 collective-permute-done.4.got
  34.4 0.0 collective-permute-done.5.got
  34.4 0.1 join_4.1.mine
  34.5 1.6 %collective-permute-start.6 = (f32[136,128]{1,0:T(8,128)S(1)}, f32[136,128]{1,0:T(8,128)S(1)}, u32[]{:S(2)}, u32[]{:S(2)}) collective-permute-start(f32[136,128]{1,0:T(8,128)S(1)} %join_4.1.mine), channel_id=1, source_target_pairs={{0,2},{1,3},{2,0},{3,1},{4,6},{5,7},{6,4},{7,5},{8,10},{9,11},{10,... | collective-permute-start | bytes 208904 | tf_op jit(solution)/shard_map/ppermute | solution.py:764
  36.2 2.7 %collective-permute-done.6.other = f32[136,128]{1,0:T(8,128)S(1)} collective-permute-done((f32[136,128]{1,0:T(8,128)S(1)}, f32[136,128]{1,0:T(8,128)S(1)}, u32[]{:S(2)}, u32[]{:S(2)}) %collective-permute-start.6) | collective-permute-done | bytes 69664 | tf_op jit(solution)/shard_map/ppermute | solution.py:764
  38.9 0.1 join_2.1.mine
  39.0 0.0 copy-done
  39.1 1.6 %collective-permute-start.8 = (bf16[2,2,64,256]{3,2,1,0:T(8,128)(2,1)S(1)}, bf16[2,2,64,256]{3,2,1,0:T(8,128)(2,1)S(1)}, u32[]{:S(2)}, u32[]{:S(2)}) collective-permute-start(bf16[2,2,64,256]{3,2,1,0:T(8,128)(2,1)S(1)} %hop_4.1), channel_id=1, source_target_pairs={{0,2},{1,3},{2,0},{3,1},{4,6},{5,7},{6,4},{7,5},{8,10},{9,11},{10,... | collective-permute-start | bytes 393224 | tf_op jit(solution)/shard_map/ppermute | solution.py:764
  40.7 0.0 collective-permute-start.7
  40.7 0.1 pass_on_1.1
  40.9 1.6 %collective-permute-start.10 = (bf16[256,1024]{1,0:T(8,128)(2,1)S(1)}, bf16[256,1024]{1,0:T(8,128)(2,1)S(1)}, u32[]{:S(2)}, u32[]{:S(2)}) collective-permute-start(bf16[256,1024]{1,0:T(8,128)(2,1)S(1)} %pass_on_1.1), channel_id=1, source_target_pairs={{0,16},{1,9},{2,18},{3,11},{4,20},{5,13},{6,22},{7,15},{8,24},{9,1... | collective-permute-start | bytes 1572872 | tf_op jit(solution)/shard_map/ppermute | solution.py:761
  42.4 0.0 collective-permute-done.1.got
  42.4 0.0 collective-permute-done.2.got
  42.5 0.0 collective-permute-done.7.other
  42.5 1.7 %collective-permute-done.8.refs_2_ = bf16[2,2,64,256]{3,2,1,0:T(8,128)(2,1)S(1)} collective-permute-done((bf16[2,2,64,256]{3,2,1,0:T(8,128)(2,1)S(1)}, bf16[2,2,64,256]{3,2,1,0:T(8,128)(2,1)S(1)}, u32[]{:S(2)}, u32[]{:S(2)}) %collective-permute-start.8) | collective-permute-done | bytes 131104 | tf_op jit(solution)/shard_map/ppermute | solution.py:764
  44.1 0.1 pass_on_0.1
  44.2 1.6 %collective-permute-start.9 = (bf16[256,1024]{1,0:T(8,128)(2,1)S(1)}, bf16[256,1024]{1,0:T(8,128)(2,1)S(1)}, u32[]{:S(2)}, u32[]{:S(2)}) collective-permute-start(bf16[256,1024]{1,0:T(8,128)(2,1)S(1)} %pass_on_0.1), channel_id=1, source_target_pairs={{0,16},{1,9},{2,18},{3,11},{4,20},{5,13},{6,22},{7,15},{8,24},{9,1... | collective-permute-start | bytes 1572872 | tf_op jit(solution)/shard_map/ppermute | solution.py:761
  45.8 0.1 collective-permute-start.11
  45.9 1.3 %decode_project.1 = (bf16[16,1024]{1,0:T(8,128)(2,1)S(1)}, bf16[16,1024]{1,0:T(8,128)(2,1)S(1)}, bf16[16,1024]{1,0:T(8,128)(2,1)S(1)}, bf16[16,1024]{1,0:T(8,128)(2,1)S(1)}) custom-call(f32[136,128]{1,0:T(8,128)S(1)} %join_2.1.mine, f32[136,128]{1,0:T(8,128)S(1)} %collective-permute-done.7.other, bf16[2,1024,1024]{2,1,0:T(8,128)(2,1)S(1)} %get-tuple-element.64.wo_a, ...), custom_call_target="tpu_custom_call" | custom-call | flops 1 | bytes 1 | tf_op jit(solution)/shard_map/decode_project/pallas_call | solution.py:631
  47.2 0.5 collective-permute-start.12
  47.7 2.4 %collective-permute-start.13 = (bf16[16,1024]{1,0:T(8,128)(2,1)S(1)}, bf16[16,1024]{1,0:T(8,128)(2,1)S(1)}, u32[]{:S(2)}, u32[]{:S(2)}) collective-permute-start(bf16[16,1024]{1,0:T(8,128)(2,1)S(1)} %get-tuple-element.69), channel_id=1, source_target_pairs={{0,24},{1,25},{2,26},{3,27},{4,28},{5,29},{6,30},{7,31},{8,16},{9,... | collective-permute-start | bytes 98312 | tf_op jit(solution)/shard_map/ppermute | solution.py:761
  50.1 0.0 collective-permute-done.11.refs_3_
  50.2 0.5 collective-permute-start.14
  50.7 0.0 collective-permute-done.10.last
  50.7 1.0 %finish_1.1 = (bf16[2,256,1024]{2,1,0:T(8,128)(2,1)}, bf16[8,64,256]{2,1,0:T(8,128)(2,1)}) custom-call(bf16[256,2048]{1,0:T(8,128)(2,1)S(1)} %get-tuple-element.52.own, bf16[256,1024]{1,0:T(8,128)(2,1)S(1)} %collective-permute-done.5.got, bf16[256,1024]{1,0:T(8,128)(2,1)S(1)} %collective-permute-done.10.last, bf16[1,8,64,256]{3,2,1,0:T(8,128)(2,1)S(1)} %bitcast.8, ...), custom_call_target="tpu_custom_call" | custom-call | flops 1 | bytes 1 | tf_op jit(solution)/shard_map/finish_1/pallas_call | solution.py:681
  51.7 4.7 %collective-permute-done.9.last = bf16[256,1024]{1,0:T(8,128)(2,1)S(1)} collective-permute-done((bf16[256,1024]{1,0:T(8,128)(2,1)S(1)}, bf16[256,1024]{1,0:T(8,128)(2,1)S(1)}, u32[]{:S(2)}, u32[]{:S(2)}) %collective-permute-start.9) | collective-permute-done | bytes 524320 | tf_op jit(solution)/shard_map/ppermute | solution.py:761
  56.4 0.9 %finish_0.1 = bf16[2,256,1024]{2,1,0:T(8,128)(2,1)} custom-call(bf16[256,2048]{1,0:T(8,128)(2,1)S(1)} %get-tuple-element.39.own, bf16[256,1024]{1,0:T(8,128)(2,1)S(1)} %collective-permute-done.2.got, bf16[256,1024]{1,0:T(8,128)(2,1)S(1)} %collective-permute-done.9.last, bf16[2,256,1024]{2,1,0:T(8,128)(2,1)} %get-tuple-element.60._), custom_call_target="tpu_custom_call", output_to_operand_aliasing={{}: (3, {})} | custom-call | flops 1 | bytes 1 | tf_op jit(solution)/shard_map/finish_0/pallas_call | solution.py:707
  57.3 0.0 collective-permute-done.12.refs_1_
  57.4 0.0 collective-permute-done.13.refs_2_
  57.4 0.0 collective-permute-done.14.refs_3_
  57.4 0.6 %decode_sum.1 = bf16[4,4,1024]{2,1,0:T(4,128)(2,1)} custom-call(bf16[16,1024]{1,0:T(8,128)(2,1)S(1)} %get-tuple-element.66.refs_0_, bf16[16,1024]{1,0:T(8,128)(2,1)S(1)} %collective-permute-done.12.refs_1_, bf16[16,1024]{1,0:T(8,128)(2,1)S(1)} %collective-permute-done.13.refs_2_, bf16[16,1024]{1,0:T(8,128)(2,1)S(1)} %collective-permute-done.14.refs_3_), custom_call_target="tpu_custom_call" | custom-call | flops 1 | bytes 1 | tf_op jit(solution)/shard_map/decode_sum/pallas_call | solution.py:730
  (2 shorter events, 0.0 us)
Async XLA Ops:
  0.6 19.4 %copy-start.1 = (bf16[1,4,512,256]{3,2,1,0:T(8,128)(2,1)S(1)}, bf16[1,4,512,256]{3,2,1,0:T(8,128)(2,1)}, u32[]{:S(2)}) copy-start(bf16[1,4,512,256]{3,2,1,0:T(8,128)(2,1)} %param.17) | copy-start | bytes 3145732
  0.6 19.4 %copy-start.2 = (s32[16]{0:T(128)S(1)}, s32[16]{0:T(128)}, u32[]{:S(2)}) copy-start(s32[16]{0:T(128)} %refs_0_.3) | copy-start | bytes 196
  0.7 19.4 %copy-start.3 = (s32[4]{0:T(128)S(1)}, s32[4]{0:T(128)}, u32[]{:S(2)}) copy-start(s32[4]{0:T(128)} %refs_1_.3) | copy-start | bytes 52
  0.7 19.4 %copy-start.4 = (s32[4]{0:T(128)S(1)}, s32[4]{0:T(128)}, u32[]{:S(2)}) copy-start(s32[4]{0:T(128)} %refs_2_.3) | copy-start | bytes 52
  13.9 20.5 %collective-permute-start.4 = (bf16[256,1024]{1,0:T(8,128)(2,1)}, bf16[256,1024]{1,0:T(8,128)(2,1)S(1)}, u32[]{:S(2)}, u32[]{:S(2)}) collective-permute-start(bf16[256,1024]{1,0:T(8,128)(2,1)} %get-tuple-element.46), channel_id=1, source_target_pairs={{0,8},{1,17},{2,10},{3,19},{4,12},{5,21},{6,14},{7,23},{8,0},{9,25... | collective-permute-start | bytes 1572872 | tf_op jit(solution)/shard_map/ppermute | solution.py:761
  16.9 17.5 %collective-permute-start.5 = (bf16[256,1024]{1,0:T(8,128)(2,1)}, bf16[256,1024]{1,0:T(8,128)(2,1)S(1)}, u32[]{:S(2)}, u32[]{:S(2)}) collective-permute-start(bf16[256,1024]{1,0:T(8,128)(2,1)} %get-tuple-element.47), channel_id=1, source_target_pairs={{0,8},{1,17},{2,10},{3,19},{4,12},{5,21},{6,14},{7,23},{8,0},{9,25... | collective-permute-start | bytes 1572872 | tf_op jit(solution)/shard_map/ppermute | solution.py:761
  17.0 10.1 %collective-permute-start = (bf16[4,64,256]{2,1,0:T(8,128)(2,1)}, bf16[4,64,256]{2,1,0:T(8,128)(2,1)S(1)}, u32[]{:S(2)}, u32[]{:S(2)}) collective-permute-start(bf16[4,64,256]{2,1,0:T(8,128)(2,1)} %get-tuple-element.42), channel_id=1, source_target_pairs={{0,4},{1,5},{2,6},{3,7},{4,0},{5,1},{6,2},{7,3},{8,12},{9,13},{10,... | collective-permute-start | bytes 393224 | tf_op jit(solution)/shard_map/ppermute | solution.py:764
  27.1 15.4 %collective-permute-start.1 = (bf16[256,1024]{1,0:T(8,128)(2,1)S(1)}, bf16[256,1024]{1,0:T(8,128)(2,1)S(1)}, u32[]{:S(2)}, u32[]{:S(2)}) collective-permute-start(bf16[256,1024]{1,0:T(8,128)(2,1)S(1)} %get-tuple-element.43), channel_id=1, source_target_pairs={{0,8},{1,17},{2,10},{3,19},{4,12},{5,21},{6,14},{7,23},{8,0},{9,25... | collective-permute-start | bytes 1572872 | tf_op jit(solution)/shard_map/ppermute | solution.py:761
  28.6 13.8 %collective-permute-start.2 = (bf16[256,1024]{1,0:T(8,128)(2,1)S(1)}, bf16[256,1024]{1,0:T(8,128)(2,1)S(1)}, u32[]{:S(2)}, u32[]{:S(2)}) collective-permute-start(bf16[256,1024]{1,0:T(8,128)(2,1)S(1)} %get-tuple-element.44), channel_id=1, source_target_pairs={{0,8},{1,17},{2,10},{3,19},{4,12},{5,21},{6,14},{7,23},{8,0},{9,25... | collective-permute-start | bytes 1572872 | tf_op jit(solution)/shard_map/ppermute | solution.py:761
  29.2 5.2 %collective-permute-start.3 = (f32[136,128]{1,0:T(8,128)S(1)}, f32[136,128]{1,0:T(8,128)S(1)}, u32[]{:S(2)}, u32[]{:S(2)}) collective-permute-start(f32[136,128]{1,0:T(8,128)S(1)} %get-tuple-element.45.mine), channel_id=1, source_target_pairs={{0,4},{1,5},{2,6},{3,7},{4,0},{5,1},{6,2},{7,3},{8,12},{9,13},{10,... | collective-permute-start | bytes 208904 | tf_op jit(solution)/shard_map/ppermute | solution.py:764
  29.2 9.9 %copy-start = (bf16[8,64,256]{2,1,0:T(8,128)(2,1)S(1)}, bf16[8,64,256]{2,1,0:T(8,128)(2,1)}, u32[]{:S(2)}) copy-start(bf16[8,64,256]{2,1,0:T(8,128)(2,1)} %get-tuple-element.49) | copy-start | bytes 786436
  34.5 4.4 %collective-permute-start.6 = (f32[136,128]{1,0:T(8,128)S(1)}, f32[136,128]{1,0:T(8,128)S(1)}, u32[]{:S(2)}, u32[]{:S(2)}) collective-permute-start(f32[136,128]{1,0:T(8,128)S(1)} %join_4.1.mine), channel_id=1, source_target_pairs={{0,2},{1,3},{2,0},{3,1},{4,6},{5,7},{6,4},{7,5},{8,10},{9,11},{10,... | collective-permute-start | bytes 208904 | tf_op jit(solution)/shard_map/ppermute | solution.py:764
  39.1 5.0 %collective-permute-start.8 = (bf16[2,2,64,256]{3,2,1,0:T(8,128)(2,1)S(1)}, bf16[2,2,64,256]{3,2,1,0:T(8,128)(2,1)S(1)}, u32[]{:S(2)}, u32[]{:S(2)}) collective-permute-start(bf16[2,2,64,256]{3,2,1,0:T(8,128)(2,1)S(1)} %hop_4.1), channel_id=1, source_target_pairs={{0,2},{1,3},{2,0},{3,1},{4,6},{5,7},{6,4},{7,5},{8,10},{9,11},{10,... | collective-permute-start | bytes 393224 | tf_op jit(solution)/shard_map/ppermute | solution.py:764
  40.7 1.7 %collective-permute-start.7 = (f32[136,128]{1,0:T(8,128)S(1)}, f32[136,128]{1,0:T(8,128)S(1)}, u32[]{:S(2)}, u32[]{:S(2)}) collective-permute-start(f32[136,128]{1,0:T(8,128)S(1)} %join_2.1.mine), channel_id=1, source_target_pairs={{0,1},{1,0},{2,3},{3,2},{4,5},{5,4},{6,7},{7,6},{8,9},{9,8},{10,11... | collective-permute-start | bytes 208904 | tf_op jit(solution)/shard_map/ppermute | solution.py:764
  40.9 9.8 %collective-permute-start.10 = (bf16[256,1024]{1,0:T(8,128)(2,1)S(1)}, bf16[256,1024]{1,0:T(8,128)(2,1)S(1)}, u32[]{:S(2)}, u32[]{:S(2)}) collective-permute-start(bf16[256,1024]{1,0:T(8,128)(2,1)S(1)} %pass_on_1.1), channel_id=1, source_target_pairs={{0,16},{1,9},{2,18},{3,11},{4,20},{5,13},{6,22},{7,15},{8,24},{9,1... | collective-permute-start | bytes 1572872 | tf_op jit(solution)/shard_map/ppermute | solution.py:761
  44.2 12.2 %collective-permute-start.9 = (bf16[256,1024]{1,0:T(8,128)(2,1)S(1)}, bf16[256,1024]{1,0:T(8,128)(2,1)S(1)}, u32[]{:S(2)}, u32[]{:S(2)}) collective-permute-start(bf16[256,1024]{1,0:T(8,128)(2,1)S(1)} %pass_on_0.1), channel_id=1, source_target_pairs={{0,16},{1,9},{2,18},{3,11},{4,20},{5,13},{6,22},{7,15},{8,24},{9,1... | collective-permute-start | bytes 1572872 | tf_op jit(solution)/shard_map/ppermute | solution.py:761
  45.8 4.3 %collective-permute-start.11 = (bf16[4,1,64,256]{3,2,1,0:T(8,128)(2,1)S(1)}, bf16[4,1,64,256]{3,2,1,0:T(8,128)(2,1)S(1)}, u32[]{:S(2)}, u32[]{:S(2)}) collective-permute-start(bf16[4,1,64,256]{3,2,1,0:T(8,128)(2,1)S(1)} %hop_2.1), channel_id=1, source_target_pairs={{0,1},{1,0},{2,3},{3,2},{4,5},{5,4},{6,7},{7,6},{8,9},{9,8},{10,11... | collective-permute-start | bytes 393224 | tf_op jit(solution)/shard_map/ppermute | solution.py:764
  47.2 10.2 %collective-permute-start.12 = (bf16[16,1024]{1,0:T(8,128)(2,1)S(1)}, bf16[16,1024]{1,0:T(8,128)(2,1)S(1)}, u32[]{:S(2)}, u32[]{:S(2)}) collective-permute-start(bf16[16,1024]{1,0:T(8,128)(2,1)S(1)} %get-tuple-element.67), channel_id=1, source_target_pairs={{0,16},{1,9},{2,18},{3,11},{4,20},{5,13},{6,22},{7,15},{8,24},{9,1... | collective-permute-start | bytes 98312 | tf_op jit(solution)/shard_map/ppermute | solution.py:761
  47.7 9.6 %collective-permute-start.13 = (bf16[16,1024]{1,0:T(8,128)(2,1)S(1)}, bf16[16,1024]{1,0:T(8,128)(2,1)S(1)}, u32[]{:S(2)}, u32[]{:S(2)}) collective-permute-start(bf16[16,1024]{1,0:T(8,128)(2,1)S(1)} %get-tuple-element.69), channel_id=1, source_target_pairs={{0,24},{1,25},{2,26},{3,27},{4,28},{5,29},{6,30},{7,31},{8,16},{9,... | collective-permute-start | bytes 98312 | tf_op jit(solution)/shard_map/ppermute | solution.py:761
  50.2 7.2 %collective-permute-start.14 = (bf16[16,1024]{1,0:T(8,128)(2,1)S(1)}, bf16[16,1024]{1,0:T(8,128)(2,1)S(1)}, u32[]{:S(2)}, u32[]{:S(2)}) collective-permute-start(bf16[16,1024]{1,0:T(8,128)(2,1)S(1)} %get-tuple-element.70), channel_id=1, source_target_pairs={{0,8},{1,17},{2,10},{3,19},{4,12},{5,21},{6,14},{7,23},{8,0},{9,25... | collective-permute-start | bytes 98312 | tf_op jit(solution)/shard_map/ppermute | solution.py:761

commit v4 on v1

--- a/solution.py
+++ b/solution.py
@@ -66,6 +66,15 @@
     return values * lax.rsqrt(square + EPS) * gain
 
 
+def norm_rows(values, gain):
+    ones = jnp.ones((HD, HD), BF)
+    square = values * values
+    high = square.astype(BF)
+    low = (square - high.astype(F32)).astype(BF)
+    total = dot(high, ones) + dot(low, ones)
+    return values * lax.rsqrt(total * (1.0 / HD) + EPS) * gain
+
+
 def rope(values, cos2, sin2):
     return values * cos2 + pltpu.roll(values, HD // 2, 1) * sin2
 
@@ -105,7 +114,7 @@
     return jnp.where((col_at <= row_at) & (col_at < length), 0.0, NEG).astype(F32)
 
 
-def attention(heads, queries, kv, bias_v, s_v, w_v, attn):
+def attention(heads, queries, kv, values, bias_v, s_v, w_v, attn):
     rows = kv.shape[0]
     half = rows // 2
     quarter = rows // 4
@@ -119,13 +128,12 @@
             keys = half if block < 2 else rows
             scores = s_v[h, at, :keys] + bias_v[at, :keys]
             top = jnp.max(scores, axis=-1, keepdims=True)
-            expo = jnp.exp2((scores - top) * C2)
-            total = jnp.sum(expo, axis=-1, keepdims=True)
-            w_v[h, at, :keys] = (expo * (1.0 / total)).astype(BF)
+            w_v[h, at, :keys] = jnp.exp2((scores - top) * C2).astype(BF)
     for h in heads:
         at = slice(h * HD, (h + 1) * HD)
-        attn[:half, at] = dot(w_v[h, :half, :half], kv[:half, HD:]).astype(BF)
-        attn[half:, at] = dot(w_v[h, half:, :], kv[:, HD:]).astype(BF)
+        for part, keys in ((slice(0, half), half), (slice(half, rows), rows)):
+            mixed = dot(w_v[h, part, :keys], values[:keys])
+            attn[part, at] = (mixed[:, :HD] / mixed[:, HD:]).astype(BF)
 
 
 def attention_scratch(rows, heads):
@@ -133,6 +141,7 @@
         pltpu.VMEM((rows, rows), F32),
         pltpu.VMEM((heads, rows, rows), F32),
         pltpu.VMEM((heads, rows, rows), BF),
+        pltpu.VMEM((rows, 2 * HD), BF),
     ]
 
 
@@ -205,8 +214,8 @@
     send_h, pack_h, blocks_h, leave_h = refs[12:16]
     x_v, dec_v, flat_v, wkv_v, wq_v, wo_v, raw, raw_kv, send, pack, blocks = refs[16:27]
     plen, adm, clen, qg, kg, table = refs[27:33]
-    bias_v, s_v, w_v = refs[33:36]
-    x_sem, dec_sem, wkv_sem, wq_sem, wo_sem, small_sem, out_sem = refs[36:]
+    bias_v, s_v, w_v, values = refs[33:37]
+    x_sem, dec_sem, wkv_sem, wq_sem, wo_sem, small_sem, out_sem = refs[37:]
     prompts, rows, width = x_hbm.shape
     steps, slots, _ = dec_hbm.shape
     dec_rows = steps * slots
@@ -281,8 +290,10 @@
     kvs = [pack.at[whole, pl.ds(p * both, both)] for p in range(prompts)]
     for p, start in ((lead, 0), (0, front)):
         at = slice(start, start + rows)
-        kvs[p][:, :HD] = rope(norm(raw_kv[at, :HD], kg[...]), cos2, sin2).astype(BF)
+        kvs[p][:, :HD] = rope(norm_rows(raw_kv[at, :HD], kg[...]), cos2, sin2).astype(BF)
         kvs[p][:, HD:] = raw_kv[at, HD:].astype(BF)
+    values[:, :HD] = kvs[lead][:, HD:]
+    values[:, HD:] = jnp.ones((rows, HD), BF)
     each = rows // n_seq
     to_row = lax.broadcasted_iota(jnp.int32, (rows, rows), 0)
     from_row = lax.broadcasted_iota(jnp.int32, (rows, rows), 1)
@@ -317,12 +328,12 @@
         later = dot(x_v[front:, :], wq_v[:, j * pair : (j + 1) * pair])
         for h in (2 * j, 2 * j + 1):
             piece = raw[:rows, h * HD : (h + 1) * HD]
-            mine[:, h * HD : (h + 1) * HD] = rope(norm(piece, qg[...]), cos2, sin2).astype(BF)
-        attention((2 * j, 2 * j + 1), mine, kvs[lead], bias_v, s_v, w_v, mine)
+            mine[:, h * HD : (h + 1) * HD] = rope(norm_rows(piece, qg[...]), cos2, sin2).astype(BF)
+        attention((2 * j, 2 * j + 1), mine, kvs[lead], values, bias_v, s_v, w_v, mine)
         for i in range(2):
             col = base + local + (2 * j + i) * HD
             piece = later[:, i * HD : (i + 1) * HD]
-            pack[:rows, col : col + HD] = rope(norm(piece, qg[...]), cos2, sin2).astype(BF)
+            pack[:rows, col : col + HD] = rope(norm_rows(piece, qg[...]), cos2, sin2).astype(BF)
     outs.append(pltpu.make_async_copy(pack, pack_h, out_sem.at[2]))
     outs[-1].start()
     for j in range(2):
@@ -398,8 +409,8 @@
     plen_h, adm_h, clen_h, pack_h, cache_h, wo_hbm = refs[:6]
     send, attn, own1, part = refs[6:10]
     pack, cache, wo_v, plen, adm, clen = refs[10:16]
-    bias_v, s_v, w_v = refs[16:19]
-    pack_sem, small_sem, wo_sem, cache_sem = refs[19:]
+    bias_v, s_v, w_v, values = refs[16:20]
+    pack_sem, small_sem, wo_sem, cache_sem = refs[20:]
     rows = attn.shape[0]
     dec_rows = pack.shape[0] - rows
     _, local, nb = wo_v.shape
@@ -429,7 +440,8 @@
     other = pack.at[whole, pl.ds(base, local)]
     queries = pack.at[whole, pl.ds(base + local, local)]
     hb = nb // 2
-
+    values[:, :HD] = kvs[0][:, HD:]
+    values[:, HD:] = jnp.ones((rows, HD), BF)
     for j in range(local // both):
         if j in (1, 2):
             copies[j - 1].wait()
@@ -437,7 +449,7 @@
                 at = slice(i * hb, (i + 1) * hb)
                 to = slice((j - 1) * nb + i * hb, (j - 1) * nb + (i + 1) * hb)
                 own1[:, to] = dot(other[...], wo_v[j - 1, :, at]).astype(BF)
-        attention((2 * j, 2 * j + 1), queries, kvs[0], bias_v, s_v, w_v, attn)
+        attention((2 * j, 2 * j + 1), queries, kvs[0], values, bias_v, s_v, w_v, attn)
     cache_copy.wait()
     for copy in copies[2:]:
         copy.wait()

time: 57.9 us -> 60.2 us (1.040)
  Pallas kernels: 28 us -> 30 us
  waiting for transfers between devices: 12.7 us -> 14.4 us
  starting transfers between devices: 16.1 us -> 14.7 us
    pallas_call x1, Pallas kernels: 13.1 us -> 15.4 us  [project(): pl.pallas_call(functools.partial(project_kernel, n_head, n_seq), out_shap...]
    ppermute x6, waiting for transfers between devices: 5.25 us -> 6.87 us  [seq_move(): return lax.ppermute(value, 'seq', [(i, i ^ bit) for i in range(n_seq)])]
    ppermute x6, starting transfers between devices: 7.25 us -> 6.17 us  [seq_move(): return lax.ppermute(value, 'seq', [(i, i ^ bit) for i in range(n_seq)])]
  transfers between devices with their start and end apart: 13 -> 13, of which waited for: 6 -> 6; matrix products, arithmetic and copies ran while one was open for 0% -> 0% of each run, Pallas kernels for 23% -> 22%
where the time goes in v4:
time: 60.2 us; the launch traced here: 60.1 us
  Pallas kernels  30 us (50%)
  starting transfers between devices  14.7 us (24%)
  waiting for transfers between devices  14.4 us (24%)
  between operations  0.93 us (2%)
    pallas_call x1, Pallas kernels, project(): pl.pallas_call(functools.partial(project_kernel, n_head, n_seq), out_shap...  15.4 us
    ppermute x7, starting transfers between devices, head_move(): return lax.ppermute(value, ('head', 'seq'), pairs)  8.51 us
    ppermute x7, waiting for transfers between devices, head_move(): return lax.ppermute(value, ('head', 'seq'), pairs)  7.51 us
    ppermute x6, waiting for transfers between devices, seq_move(): return lax.ppermute(value, 'seq', [(i, i ^ bit) for i in range(n_seq)])  6.87 us
    pallas_call x1, Pallas kernels, second(): pl.pallas_call(functools.partial(second_kernel, n_seq, prompts), out_shap...  6.65 us
    ppermute x6, starting transfers between devices, seq_move(): return lax.ppermute(value, 'seq', [(i, i ^ bit) for i in range(n_seq)])  6.17 us
    pallas_call x1, Pallas kernels, third(): pl.pallas_call(third_kernel, out_shape=[jax.ShapeDtypeStruct((rows, 2 * n...  3.56 us
    pallas_call x1, Pallas kernels, finish_last(): pl.pallas_call(functools.partial(finish_last_kernel, p, slots), out_shape...  1.53 us
  transfers between devices with their start and end apart: 13, of which 6 were waited for; matrix products, arithmetic and copies ran while one was open for 0% of the time, Pallas kernels for 22%

profile of v4, /device:TPU:0, one launch (start us, length us, event | category | flops | bytes accessed | tf_op | source)
XLA Modules:
  0.0 60.1 jit_solution(11568582814502626782)
XLA Ops:
  0.6 0.0 copy-start.1
  0.6 0.0 copy-start.2
  0.7 0.0 copy-start.3
  0.7 0.0 copy-start.4
  0.7 15.4 %project.1 = (bf16[256,2048]{1,0:T(8,128)(2,1)}, bf16[272,2560]{1,0:T(8,128)(2,1)}, bf16[8,64,256]{2,1,0:T(8,128)(2,1)}, bf16[4,64,256]{2,1,0:T(8,128)(2,1)}) custom-call(s32[16]{0:T(128)} %refs_0_.3, s32[4]{0:T(128)} %refs_1_.3, s32[4]{0:T(128)} %refs_2_.3, f32[1,128]{1,0:T(1,128)} %bitcast.13, f32[1,128]{1,0:T(1,128)} %bitcast.14, ...), custom_call_target="tpu_custom_call" | custom-call | flops 1 | bytes 1 | tf_op jit(solution)/shard_map/project/pallas_call | solution.py:363
  16.1 3.0 %collective-permute-start.3 = (bf16[256,2048]{1,0:T(8,128)(2,1)}, bf16[256,2048]{1,0:T(8,128)(2,1)S(1)}, u32[]{:S(2)}, u32[]{:S(2)}) collective-permute-start(bf16[256,2048]{1,0:T(8,128)(2,1)} %get-tuple-element.40), channel_id=1, source_target_pairs={{0,8},{1,17},{2,10},{3,19},{4,12},{5,21},{6,14},{7,23},{8,0},{9,25... | collective-permute-start | bytes 3145736 | tf_op jit(solution)/shard_map/ppermute | solution.py:757
  19.1 2.6 %collective-permute-start = (bf16[4,64,256]{2,1,0:T(8,128)(2,1)}, bf16[4,64,256]{2,1,0:T(8,128)(2,1)S(1)}, u32[]{:S(2)}, u32[]{:S(2)}) collective-permute-start(bf16[4,64,256]{2,1,0:T(8,128)(2,1)} %get-tuple-element.37), channel_id=1, source_target_pairs={{0,4},{1,5},{2,6},{3,7},{4,0},{5,1},{6,2},{7,3},{8,12},{9,13},{10,... | collective-permute-start | bytes 393224 | tf_op jit(solution)/shard_map/ppermute | solution.py:760
  21.7 0.0 copy-done.1
  21.7 0.0 copy-done.2
  21.7 0.0 copy-done.3
  21.7 0.0 copy-done.4
  21.7 6.7 %second.1 = (bf16[256,2048]{1,0:T(8,128)(2,1)S(1)}, bf16[256,1024]{1,0:T(8,128)(2,1)S(1)}, bf16[256,2048]{1,0:T(8,128)(2,1)S(1)}, f32[136,128]{1,0:T(8,128)S(1)}) custom-call(s32[16]{0:T(128)S(1)} %copy-done.2, s32[4]{0:T(128)S(1)} %copy-done.3, s32[4]{0:T(128)S(1)} %copy-done.4, bf16[272,2560]{1,0:T(8,128)(2,1)} %get-tuple-element.33.refs_3_, ...), custom_call_target="tpu_custom_call" | custom-call | flops 1 | bytes 1 | tf_op jit(solution)/shard_map/second/pallas_call | solution.py:468
  28.4 0.0 collective-permute-done
  28.4 1.1 %collective-permute-start.1 = (bf16[256,2048]{1,0:T(8,128)(2,1)S(1)}, bf16[256,2048]{1,0:T(8,128)(2,1)S(1)}, u32[]{:S(2)}, u32[]{:S(2)}) collective-permute-start(bf16[256,2048]{1,0:T(8,128)(2,1)S(1)} %get-tuple-element.38), channel_id=1, source_target_pairs={{0,8},{1,17},{2,10},{3,19},{4,12},{5,21},{6,14},{7,23},{8,0},{9,25... | collective-permute-start | bytes 3145736 | tf_op jit(solution)/shard_map/ppermute | solution.py:757
  29.5 0.0 collective-permute-start.2
  29.5 0.0 copy-start
  29.5 3.6 %third.1 = (bf16[256,2048]{1,0:T(8,128)(2,1)S(1)}, bf16[2,1024,1024]{2,1,0:T(8,128)(2,1)S(1)}, bf16[2,1024,1024]{2,1,0:T(8,128)(2,1)S(1)}) custom-call(bf16[256,1024]{1,0:T(8,128)(2,1)S(1)} %get-tuple-element.34.attn, bf16[1024,4096]{1,0:T(8,128)(2,1)} %wo_hbm.1), custom_call_target="tpu_custom_call" | custom-call | flops 1 | bytes 1 | tf_op jit(solution)/shard_map/third/pallas_call | solution.py:521
  33.1 2.4 %collective-permute-done.2.other = f32[136,128]{1,0:T(8,128)S(1)} collective-permute-done((f32[136,128]{1,0:T(8,128)S(1)}, f32[136,128]{1,0:T(8,128)S(1)}, u32[]{:S(2)}, u32[]{:S(2)}) %collective-permute-start.2) | collective-permute-done | bytes 69664 | tf_op jit(solution)/shard_map/ppermute | solution.py:760
  35.5 0.0 collective-permute-done.3.got
  35.5 0.1 join_4.1.mine
  35.6 1.8 %collective-permute-start.4 = (f32[136,128]{1,0:T(8,128)S(1)}, f32[136,128]{1,0:T(8,128)S(1)}, u32[]{:S(2)}, u32[]{:S(2)}) collective-permute-start(f32[136,128]{1,0:T(8,128)S(1)} %join_4.1.mine), channel_id=1, source_target_pairs={{0,2},{1,3},{2,0},{3,1},{4,6},{5,7},{6,4},{7,5},{8,10},{9,11},{10,... | collective-permute-start | bytes 208904 | tf_op jit(solution)/shard_map/ppermute | solution.py:760
  37.4 2.6 %collective-permute-done.4.other = f32[136,128]{1,0:T(8,128)S(1)} collective-permute-done((f32[136,128]{1,0:T(8,128)S(1)}, f32[136,128]{1,0:T(8,128)S(1)}, u32[]{:S(2)}, u32[]{:S(2)}) %collective-permute-start.4) | collective-permute-done | bytes 69664 | tf_op jit(solution)/shard_map/ppermute | solution.py:760
  40.0 0.1 join_2.1.mine
  40.1 0.0 copy-done
  40.2 1.8 %collective-permute-start.6 = (bf16[2,2,64,256]{3,2,1,0:T(8,128)(2,1)S(1)}, bf16[2,2,64,256]{3,2,1,0:T(8,128)(2,1)S(1)}, u32[]{:S(2)}, u32[]{:S(2)}) collective-permute-start(bf16[2,2,64,256]{3,2,1,0:T(8,128)(2,1)S(1)} %hop_4.1), channel_id=1, source_target_pairs={{0,2},{1,3},{2,0},{3,1},{4,6},{5,7},{6,4},{7,5},{8,10},{9,11},{10,... | collective-permute-start | bytes 393224 | tf_op jit(solution)/shard_map/ppermute | solution.py:760
  41.9 0.0 collective-permute-start.5
  41.9 0.1 pass_on_1.1
  42.1 0.6 collective-permute-start.11
  42.7 0.7 %collective-permute-done.1.got = bf16[256,2048]{1,0:T(8,128)(2,1)S(1)} collective-permute-done((bf16[256,2048]{1,0:T(8,128)(2,1)S(1)}, bf16[256,2048]{1,0:T(8,128)(2,1)S(1)}, u32[]{:S(2)}, u32[]{:S(2)}) %collective-permute-start.1) | collective-permute-done | bytes 1048608 | tf_op jit(solution)/shard_map/ppermute | solution.py:757
  43.4 0.0 collective-permute-done.5.other
  43.4 1.9 %collective-permute-done.6.refs_2_ = bf16[2,2,64,256]{3,2,1,0:T(8,128)(2,1)S(1)} collective-permute-done((bf16[2,2,64,256]{3,2,1,0:T(8,128)(2,1)S(1)}, bf16[2,2,64,256]{3,2,1,0:T(8,128)(2,1)S(1)}, u32[]{:S(2)}, u32[]{:S(2)}) %collective-permute-start.6) | collective-permute-done | bytes 131104 | tf_op jit(solution)/shard_map/ppermute | solution.py:760
  45.2 0.1 pass_on_0.1
  45.3 0.3 collective-permute-start.7
  45.7 0.1 collective-permute-start.12
  45.8 1.3 %decode_project.1 = (bf16[16,1024]{1,0:T(8,128)(2,1)S(1)}, bf16[16,1024]{1,0:T(8,128)(2,1)S(1)}, bf16[16,1024]{1,0:T(8,128)(2,1)S(1)}, bf16[16,1024]{1,0:T(8,128)(2,1)S(1)}) custom-call(f32[136,128]{1,0:T(8,128)S(1)} %join_2.1.mine, f32[136,128]{1,0:T(8,128)S(1)} %collective-permute-done.5.other, bf16[2,1024,1024]{2,1,0:T(8,128)(2,1)S(1)} %get-tuple-element.53.wo_a, ...), custom_call_target="tpu_custom_call" | custom-call | flops 1 | bytes 1 | tf_op jit(solution)/shard_map/decode_project/pallas_call | solution.py:638
  47.0 1.8 %collective-permute-start.8 = (bf16[16,1024]{1,0:T(8,128)(2,1)S(1)}, bf16[16,1024]{1,0:T(8,128)(2,1)S(1)}, u32[]{:S(2)}, u32[]{:S(2)}) collective-permute-start(bf16[16,1024]{1,0:T(8,128)(2,1)S(1)} %get-tuple-element.56), channel_id=1, source_target_pairs={{0,16},{1,9},{2,18},{3,11},{4,20},{5,13},{6,22},{7,15},{8,24},{9,1... | collective-permute-start | bytes 98312 | tf_op jit(solution)/shard_map/ppermute | solution.py:757
  48.8 1.2 %collective-permute-start.9 = (bf16[16,1024]{1,0:T(8,128)(2,1)S(1)}, bf16[16,1024]{1,0:T(8,128)(2,1)S(1)}, u32[]{:S(2)}, u32[]{:S(2)}) collective-permute-start(bf16[16,1024]{1,0:T(8,128)(2,1)S(1)} %get-tuple-element.57), channel_id=1, source_target_pairs={{0,24},{1,25},{2,26},{3,27},{4,28},{5,29},{6,30},{7,31},{8,16},{9,... | collective-permute-start | bytes 98312 | tf_op jit(solution)/shard_map/ppermute | solution.py:757
  50.0 0.0 collective-permute-done.12.refs_3_
  50.0 0.5 collective-permute-start.10
  50.5 0.8 %collective-permute-done.11.last = bf16[256,1024]{1,0:T(8,128)(2,1)S(1)} collective-permute-done((bf16[256,1024]{1,0:T(8,128)(2,1)S(1)}, bf16[256,1024]{1,0:T(8,128)(2,1)S(1)}, u32[]{:S(2)}, u32[]{:S(2)}) %collective-permute-start.11) | collective-permute-done | bytes 524320 | tf_op jit(solution)/shard_map/ppermute | solution.py:757
  51.3 1.0 %finish_1.1 = (bf16[2,256,1024]{2,1,0:T(8,128)(2,1)}, bf16[8,64,256]{2,1,0:T(8,128)(2,1)}) custom-call(bf16[256,2048]{1,0:T(8,128)(2,1)S(1)} %get-tuple-element.45.own, bf16[256,2048]{1,0:T(8,128)(2,1)S(1)} %collective-permute-done.3.got, bf16[256,1024]{1,0:T(8,128)(2,1)S(1)} %collective-permute-done.11.last, bf16[1,8,64,256]{3,2,1,0:T(8,128)(2,1)S(1)} %bitcast.8, ...), custom_call_target="tpu_custom_call" | custom-call | flops 1 | bytes 1 | tf_op jit(solution)/shard_map/finish_1/pallas_call | solution.py:688
  52.4 6.0 %collective-permute-done.8.refs_1_ = bf16[16,1024]{1,0:T(8,128)(2,1)S(1)} collective-permute-done((bf16[16,1024]{1,0:T(8,128)(2,1)S(1)}, bf16[16,1024]{1,0:T(8,128)(2,1)S(1)}, u32[]{:S(2)}, u32[]{:S(2)}) %collective-permute-start.8) | collective-permute-done | bytes 32800 | tf_op jit(solution)/shard_map/ppermute | solution.py:757
  58.4 0.0 collective-permute-done.9.refs_2_
  58.4 0.0 collective-permute-done.10.refs_3_
  58.4 0.0 collective-permute-done.7.last
  58.4 1.5 %finish_0.1 = (bf16[2,256,1024]{2,1,0:T(8,128)(2,1)}, bf16[4,4,1024]{2,1,0:T(4,128)(2,1)}) custom-call(bf16[256,2048]{1,0:T(8,128)(2,1)S(1)} %get-tuple-element.35.own, bf16[256,2048]{1,0:T(8,128)(2,1)S(1)} %collective-permute-done.1.got, bf16[256,1024]{1,0:T(8,128)(2,1)S(1)} %collective-permute-done.7.last, ...), custom_call_target="tpu_custom_call", output_to_operand_aliasing={{0}: (7, {})} | custom-call | flops 1 | bytes 1 | tf_op jit(solution)/shard_map/finish_0/pallas_call | solution.py:721
  (2 shorter events, 0.0 us)
Async XLA Ops:
  0.6 21.1 %copy-start.1 = (bf16[1,4,512,256]{3,2,1,0:T(8,128)(2,1)S(1)}, bf16[1,4,512,256]{3,2,1,0:T(8,128)(2,1)}, u32[]{:S(2)}) copy-start(bf16[1,4,512,256]{3,2,1,0:T(8,128)(2,1)} %param.17) | copy-start | bytes 3145732
  0.6 21.1 %copy-start.2 = (s32[16]{0:T(128)S(1)}, s32[16]{0:T(128)}, u32[]{:S(2)}) copy-start(s32[16]{0:T(128)} %refs_0_.3) | copy-start | bytes 196
  0.7 21.1 %copy-start.3 = (s32[4]{0:T(128)S(1)}, s32[4]{0:T(128)}, u32[]{:S(2)}) copy-start(s32[4]{0:T(128)} %refs_1_.3) | copy-start | bytes 52
  0.7 21.1 %copy-start.4 = (s32[4]{0:T(128)S(1)}, s32[4]{0:T(128)}, u32[]{:S(2)}) copy-start(s32[4]{0:T(128)} %refs_2_.3) | copy-start | bytes 52
  16.1 19.4 %collective-permute-start.3 = (bf16[256,2048]{1,0:T(8,128)(2,1)}, bf16[256,2048]{1,0:T(8,128)(2,1)S(1)}, u32[]{:S(2)}, u32[]{:S(2)}) collective-permute-start(bf16[256,2048]{1,0:T(8,128)(2,1)} %get-tuple-element.40), channel_id=1, source_target_pairs={{0,8},{1,17},{2,10},{3,19},{4,12},{5,21},{6,14},{7,23},{8,0},{9,25... | collective-permute-start | bytes 3145736 | tf_op jit(solution)/shard_map/ppermute | solution.py:757
  19.1 9.3 %collective-permute-start = (bf16[4,64,256]{2,1,0:T(8,128)(2,1)}, bf16[4,64,256]{2,1,0:T(8,128)(2,1)S(1)}, u32[]{:S(2)}, u32[]{:S(2)}) collective-permute-start(bf16[4,64,256]{2,1,0:T(8,128)(2,1)} %get-tuple-element.37), channel_id=1, source_target_pairs={{0,4},{1,5},{2,6},{3,7},{4,0},{5,1},{6,2},{7,3},{8,12},{9,13},{10,... | collective-permute-start | bytes 393224 | tf_op jit(solution)/shard_map/ppermute | solution.py:760
  28.4 15.0 %collective-permute-start.1 = (bf16[256,2048]{1,0:T(8,128)(2,1)S(1)}, bf16[256,2048]{1,0:T(8,128)(2,1)S(1)}, u32[]{:S(2)}, u32[]{:S(2)}) collective-permute-start(bf16[256,2048]{1,0:T(8,128)(2,1)S(1)} %get-tuple-element.38), channel_id=1, source_target_pairs={{0,8},{1,17},{2,10},{3,19},{4,12},{5,21},{6,14},{7,23},{8,0},{9,25... | collective-permute-start | bytes 3145736 | tf_op jit(solution)/shard_map/ppermute | solution.py:757
  29.5 6.0 %collective-permute-start.2 = (f32[136,128]{1,0:T(8,128)S(1)}, f32[136,128]{1,0:T(8,128)S(1)}, u32[]{:S(2)}, u32[]{:S(2)}) collective-permute-start(f32[136,128]{1,0:T(8,128)S(1)} %get-tuple-element.39.mine), channel_id=1, source_target_pairs={{0,4},{1,5},{2,6},{3,7},{4,0},{5,1},{6,2},{7,3},{8,12},{9,13},{10,... | collective-permute-start | bytes 208904 | tf_op jit(solution)/shard_map/ppermute | solution.py:760
  29.5 10.6 %copy-start = (bf16[8,64,256]{2,1,0:T(8,128)(2,1)S(1)}, bf16[8,64,256]{2,1,0:T(8,128)(2,1)}, u32[]{:S(2)}) copy-start(bf16[8,64,256]{2,1,0:T(8,128)(2,1)} %get-tuple-element.42) | copy-start | bytes 786436
  35.6 4.4 %collective-permute-start.4 = (f32[136,128]{1,0:T(8,128)S(1)}, f32[136,128]{1,0:T(8,128)S(1)}, u32[]{:S(2)}, u32[]{:S(2)}) collective-permute-start(f32[136,128]{1,0:T(8,128)S(1)} %join_4.1.mine), channel_id=1, source_target_pairs={{0,2},{1,3},{2,0},{3,1},{4,6},{5,7},{6,4},{7,5},{8,10},{9,11},{10,... | collective-permute-start | bytes 208904 | tf_op jit(solution)/shard_map/ppermute | solution.py:760
  40.2 5.0 %collective-permute-start.6 = (bf16[2,2,64,256]{3,2,1,0:T(8,128)(2,1)S(1)}, bf16[2,2,64,256]{3,2,1,0:T(8,128)(2,1)S(1)}, u32[]{:S(2)}, u32[]{:S(2)}) collective-permute-start(bf16[2,2,64,256]{3,2,1,0:T(8,128)(2,1)S(1)} %hop_4.1), channel_id=1, source_target_pairs={{0,2},{1,3},{2,0},{3,1},{4,6},{5,7},{6,4},{7,5},{8,10},{9,11},{10,... | collective-permute-start | bytes 393224 | tf_op jit(solution)/shard_map/ppermute | solution.py:760
  41.9 1.4 %collective-permute-start.5 = (f32[136,128]{1,0:T(8,128)S(1)}, f32[136,128]{1,0:T(8,128)S(1)}, u32[]{:S(2)}, u32[]{:S(2)}) collective-permute-start(f32[136,128]{1,0:T(8,128)S(1)} %join_2.1.mine), channel_id=1, source_target_pairs={{0,1},{1,0},{2,3},{3,2},{4,5},{5,4},{6,7},{7,6},{8,9},{9,8},{10,11... | collective-permute-start | bytes 208904 | tf_op jit(solution)/shard_map/ppermute | solution.py:760
  42.1 9.2 %collective-permute-start.11 = (bf16[256,1024]{1,0:T(8,128)(2,1)S(1)}, bf16[256,1024]{1,0:T(8,128)(2,1)S(1)}, u32[]{:S(2)}, u32[]{:S(2)}) collective-permute-start(bf16[256,1024]{1,0:T(8,128)(2,1)S(1)} %pass_on_1.1), channel_id=1, source_target_pairs={{0,16},{1,9},{2,18},{3,11},{4,20},{5,13},{6,22},{7,15},{8,24},{9,1... | collective-permute-start | bytes 1572872 | tf_op jit(solution)/shard_map/ppermute | solution.py:757
  45.3 13.0 %collective-permute-start.7 = (bf16[256,1024]{1,0:T(8,128)(2,1)S(1)}, bf16[256,1024]{1,0:T(8,128)(2,1)S(1)}, u32[]{:S(2)}, u32[]{:S(2)}) collective-permute-start(bf16[256,1024]{1,0:T(8,128)(2,1)S(1)} %pass_on_0.1), channel_id=1, source_target_pairs={{0,16},{1,9},{2,18},{3,11},{4,20},{5,13},{6,22},{7,15},{8,24},{9,1... | collective-permute-start | bytes 1572872 | tf_op jit(solution)/shard_map/ppermute | solution.py:757
  45.7 4.3 %collective-permute-start.12 = (bf16[4,1,64,256]{3,2,1,0:T(8,128)(2,1)S(1)}, bf16[4,1,64,256]{3,2,1,0:T(8,128)(2,1)S(1)}, u32[]{:S(2)}, u32[]{:S(2)}) collective-permute-start(bf16[4,1,64,256]{3,2,1,0:T(8,128)(2,1)S(1)} %hop_2.1), channel_id=1, source_target_pairs={{0,1},{1,0},{2,3},{3,2},{4,5},{5,4},{6,7},{7,6},{8,9},{9,8},{10,11... | collective-permute-start | bytes 393224 | tf_op jit(solution)/shard_map/ppermute | solution.py:760
  47.0 11.3 %collective-permute-start.8 = (bf16[16,1024]{1,0:T(8,128)(2,1)S(1)}, bf16[16,1024]{1,0:T(8,128)(2,1)S(1)}, u32[]{:S(2)}, u32[]{:S(2)}) collective-permute-start(bf16[16,1024]{1,0:T(8,128)(2,1)S(1)} %get-tuple-element.56), channel_id=1, source_target_pairs={{0,16},{1,9},{2,18},{3,11},{4,20},{5,13},{6,22},{7,15},{8,24},{9,1... | collective-permute-start | bytes 98312 | tf_op jit(solution)/shard_map/ppermute | solution.py:757
  48.8 9.5 %collective-permute-start.9 = (bf16[16,1024]{1,0:T(8,128)(2,1)S(1)}, bf16[16,1024]{1,0:T(8,128)(2,1)S(1)}, u32[]{:S(2)}, u32[]{:S(2)}) collective-permute-start(bf16[16,1024]{1,0:T(8,128)(2,1)S(1)} %get-tuple-element.57), channel_id=1, source_target_pairs={{0,24},{1,25},{2,26},{3,27},{4,28},{5,29},{6,30},{7,31},{8,16},{9,... | collective-permute-start | bytes 98312 | tf_op jit(solution)/shard_map/ppermute | solution.py:757
  50.0 8.4 %collective-permute-start.10 = (bf16[16,1024]{1,0:T(8,128)(2,1)S(1)}, bf16[16,1024]{1,0:T(8,128)(2,1)S(1)}, u32[]{:S(2)}, u32[]{:S(2)}) collective-permute-start(bf16[16,1024]{1,0:T(8,128)(2,1)S(1)} %get-tuple-element.58), channel_id=1, source_target_pairs={{0,8},{1,17},{2,10},{3,19},{4,12},{5,21},{6,14},{7,23},{8,0},{9,25... | collective-permute-start | bytes 98312 | tf_op jit(solution)/shard_map/ppermute | solution.py:757

commit v5 on v1

--- a/solution.py
+++ b/solution.py
@@ -105,27 +105,30 @@
     return jnp.where((col_at <= row_at) & (col_at < length), 0.0, NEG).astype(F32)
 
 
-def attention(heads, queries, kv, bias_v, s_v, w_v, attn):
+def attention(heads, q_v, kv, values, bias_v, s_v, w_v, attn):
     rows = kv.shape[0]
     half = rows // 2
     quarter = rows // 4
-    for h in heads:
-        at = slice(h * HD, (h + 1) * HD)
-        s_v[h, :half, :half] = dot_nt(queries[:half, at], kv[:half, :HD])
-        s_v[h, half:, :] = dot_nt(queries[half:, at], kv[:, :HD])
+    low, count = heads[0], len(heads)
+    group = pl.ds(low, count)
+    parts = ((pl.ds(0, half), half), (pl.ds(half, half), rows))
+    for part, keys in parts:
+        queries = q_v[group, part].reshape(count * half, HD)
+        scores = dot_nt(queries, kv[:keys, :HD])
+        s_v[group, part, :keys] = scores.reshape(count, half, keys)
     for h in heads:
         for block in range(4):
             at = slice(block * quarter, (block + 1) * quarter)
             keys = half if block < 2 else rows
             scores = s_v[h, at, :keys] + bias_v[at, :keys]
             top = jnp.max(scores, axis=-1, keepdims=True)
-            expo = jnp.exp2((scores - top) * C2)
-            total = jnp.sum(expo, axis=-1, keepdims=True)
-            w_v[h, at, :keys] = (expo * (1.0 / total)).astype(BF)
-    for h in heads:
-        at = slice(h * HD, (h + 1) * HD)
-        attn[:half, at] = dot(w_v[h, :half, :half], kv[:half, HD:]).astype(BF)
-        attn[half:, at] = dot(w_v[h, half:, :], kv[:, HD:]).astype(BF)
+            w_v[h, at, :keys] = jnp.exp2((scores - top) * C2).astype(BF)
+    for part, keys in parts:
+        weights = w_v[group, part, :keys].reshape(count * half, keys)
+        mixed = dot(weights, values[:keys])
+        mixed = (mixed[:, :HD] / mixed[:, HD:]).astype(BF)
+        for i, h in enumerate(heads):
+            attn[part, h * HD : (h + 1) * HD] = mixed[i * half : (i + 1) * half]
 
 
 def attention_scratch(rows, heads):
@@ -133,6 +136,8 @@
         pltpu.VMEM((rows, rows), F32),
         pltpu.VMEM((heads, rows, rows), F32),
         pltpu.VMEM((heads, rows, rows), BF),
+        pltpu.VMEM((rows, 2 * HD), BF),
+        pltpu.VMEM((heads, rows, HD), BF),
     ]
 
 
@@ -205,8 +210,8 @@
     send_h, pack_h, blocks_h, leave_h = refs[12:16]
     x_v, dec_v, flat_v, wkv_v, wq_v, wo_v, raw, raw_kv, send, pack, blocks = refs[16:27]
     plen, adm, clen, qg, kg, table = refs[27:33]
-    bias_v, s_v, w_v = refs[33:36]
-    x_sem, dec_sem, wkv_sem, wq_sem, wo_sem, small_sem, out_sem = refs[36:]
+    bias_v, s_v, w_v, values, q_v = refs[33:38]
+    x_sem, dec_sem, wkv_sem, wq_sem, wo_sem, small_sem, out_sem = refs[38:]
     prompts, rows, width = x_hbm.shape
     steps, slots, _ = dec_hbm.shape
     dec_rows = steps * slots
@@ -283,6 +288,8 @@
         at = slice(start, start + rows)
         kvs[p][:, :HD] = rope(norm(raw_kv[at, :HD], kg[...]), cos2, sin2).astype(BF)
         kvs[p][:, HD:] = raw_kv[at, HD:].astype(BF)
+    values[:, :HD] = kvs[lead][:, HD:]
+    values[:, HD:] = jnp.ones((rows, HD), BF)
     each = rows // n_seq
     to_row = lax.broadcasted_iota(jnp.int32, (rows, rows), 0)
     from_row = lax.broadcasted_iota(jnp.int32, (rows, rows), 1)
@@ -312,15 +319,16 @@
     for copy in o_copies:
         copy.wait()
     mine = pack.at[whole, pl.ds(base, local)]
-    pair = 2 * HD
-    for j in range(local // pair):
-        later = dot(x_v[front:, :], wq_v[:, j * pair : (j + 1) * pair])
-        for h in (2 * j, 2 * j + 1):
+    wide = 4 * HD
+    for j in range(local // wide):
+        later = dot(x_v[front:, :], wq_v[:, j * wide : (j + 1) * wide])
+        heads = range(4 * j, 4 * j + 4)
+        for h in heads:
             piece = raw[:rows, h * HD : (h + 1) * HD]
-            mine[:, h * HD : (h + 1) * HD] = rope(norm(piece, qg[...]), cos2, sin2).astype(BF)
-        attention((2 * j, 2 * j + 1), mine, kvs[lead], bias_v, s_v, w_v, mine)
-        for i in range(2):
-            col = base + local + (2 * j + i) * HD
+            q_v[h] = rope(norm(piece, qg[...]), cos2, sin2).astype(BF)
+        attention(heads, q_v, kvs[lead], values, bias_v, s_v, w_v, mine)
+        for i, h in enumerate(heads):
+            col = base + local + h * HD
             piece = later[:, i * HD : (i + 1) * HD]
             pack[:rows, col : col + HD] = rope(norm(piece, qg[...]), cos2, sin2).astype(BF)
     outs.append(pltpu.make_async_copy(pack, pack_h, out_sem.at[2]))
@@ -398,8 +406,8 @@
     plen_h, adm_h, clen_h, pack_h, cache_h, wo_hbm = refs[:6]
     send, attn, own1, part = refs[6:10]
     pack, cache, wo_v, plen, adm, clen = refs[10:16]
-    bias_v, s_v, w_v = refs[16:19]
-    pack_sem, small_sem, wo_sem, cache_sem = refs[19:]
+    bias_v, s_v, w_v, values, q_v = refs[16:21]
+    pack_sem, small_sem, wo_sem, cache_sem = refs[21:]
     rows = attn.shape[0]
     dec_rows = pack.shape[0] - rows
     _, local, nb = wo_v.shape
@@ -428,16 +436,16 @@
     kvs = [pack.at[whole, pl.ds(p * both, both)] for p in range(prompts)]
     other = pack.at[whole, pl.ds(base, local)]
     queries = pack.at[whole, pl.ds(base + local, local)]
-    hb = nb // 2
-
-    for j in range(local // both):
-        if j in (1, 2):
-            copies[j - 1].wait()
+    values[:, :HD] = kvs[0][:, HD:]
+    values[:, HD:] = jnp.ones((rows, HD), BF)
+    for h in range(local // HD):
+        q_v[h] = queries[:, h * HD : (h + 1) * HD]
+    for j in range(local // (4 * HD)):
+        if j == 1:
             for i in range(2):
-                at = slice(i * hb, (i + 1) * hb)
-                to = slice((j - 1) * nb + i * hb, (j - 1) * nb + (i + 1) * hb)
-                own1[:, to] = dot(other[...], wo_v[j - 1, :, at]).astype(BF)
-        attention((2 * j, 2 * j + 1), queries, kvs[0], bias_v, s_v, w_v, attn)
+                copies[i].wait()
+                own1[:, i * nb : (i + 1) * nb] = dot(other[...], wo_v[i]).astype(BF)
+        attention(range(4 * j, 4 * j + 4), q_v, kvs[0], values, bias_v, s_v, w_v, attn)
     cache_copy.wait()
     for copy in copies[2:]:
         copy.wait()

time: 57.9 us -> 57.6 us (level)
  waiting for transfers between devices: 12.7 us -> 14.5 us
  starting transfers between devices: 16.1 us -> 15 us
  Pallas kernels: 28 us -> 27.1 us
    ppermute x6, waiting for transfers between devices: 5.25 us -> 6.91 us  [seq_move(): return lax.ppermute(value, 'seq', [(i, i ^ bit) for i in range(n_seq)])]
    ppermute x6, starting transfers between devices: 7.25 us -> 6.18 us  [seq_move(): return lax.ppermute(value, 'seq', [(i, i ^ bit) for i in range(n_seq)])]
    pallas_call x1, Pallas kernels: 6.95 us -> 6.25 us  [second(): pl.pallas_call(functools.partial(second_kernel, n_seq, prompts), out_shap...]
  transfers between devices with their start and end apart: 13 -> 13, of which waited for: 6 -> 6; matrix products, arithmetic and copies ran while one was open for 0% -> 0% of each run, Pallas kernels for 23% -> 22%
where the time goes in v5:
time: 57.6 us; the launch traced here: 57.5 us
  Pallas kernels  27.1 us (47%)
  starting transfers between devices  15 us (26%)
  waiting for transfers between devices  14.5 us (25%)
  between operations  0.93 us (2%)
    pallas_call x1, Pallas kernels, project(): pl.pallas_call(functools.partial(project_kernel, n_head, n_seq), out_shap...  12.9 us
    ppermute x7, starting transfers between devices, head_move(): return lax.ppermute(value, ('head', 'seq'), pairs)  8.81 us
    ppermute x7, waiting for transfers between devices, head_move(): return lax.ppermute(value, ('head', 'seq'), pairs)  7.57 us
    ppermute x6, waiting for transfers between devices, seq_move(): return lax.ppermute(value, 'seq', [(i, i ^ bit) for i in range(n_seq)])  6.91 us
    pallas_call x1, Pallas kernels, second(): pl.pallas_call(functools.partial(second_kernel, n_seq, prompts), out_shap...  6.25 us
    ppermute x6, starting transfers between devices, seq_move(): return lax.ppermute(value, 'seq', [(i, i ^ bit) for i in range(n_seq)])  6.18 us
    pallas_call x1, Pallas kernels, third(): pl.pallas_call(third_kernel, out_shape=[jax.ShapeDtypeStruct((rows, 2 * n...  3.56 us
    pallas_call x1, Pallas kernels, finish_last(): pl.pallas_call(functools.partial(finish_last_kernel, p, slots), out_shape...  1.53 us
  transfers between devices with their start and end apart: 13, of which 6 were waited for; matrix products, arithmetic and copies ran while one was open for 0% of the time, Pallas kernels for 22%

profile of v5, /device:TPU:0, one launch (start us, length us, event | category | flops | bytes accessed | tf_op | source)
XLA Modules:
  0.0 57.5 jit_solution(11494535878767553972)
XLA Ops:
  0.6 0.0 copy-start.1
  0.6 0.0 copy-start.2
  0.7 0.0 copy-start.3
  0.7 0.0 copy-start.4
  0.7 12.9 %project.1 = (bf16[256,2048]{1,0:T(8,128)(2,1)}, bf16[272,2560]{1,0:T(8,128)(2,1)}, bf16[8,64,256]{2,1,0:T(8,128)(2,1)}, bf16[4,64,256]{2,1,0:T(8,128)(2,1)}) custom-call(s32[16]{0:T(128)} %refs_0_.3, s32[4]{0:T(128)} %refs_1_.3, s32[4]{0:T(128)} %refs_2_.3, f32[1,128]{1,0:T(1,128)} %bitcast.13, f32[1,128]{1,0:T(1,128)} %bitcast.14, ...), custom_call_target="tpu_custom_call" | custom-call | flops 1 | bytes 1 | tf_op jit(solution)/shard_map/project/pallas_call | solution.py:360
  13.6 3.0 %collective-permute-start.3 = (bf16[256,2048]{1,0:T(8,128)(2,1)}, bf16[256,2048]{1,0:T(8,128)(2,1)S(1)}, u32[]{:S(2)}, u32[]{:S(2)}) collective-permute-start(bf16[256,2048]{1,0:T(8,128)(2,1)} %get-tuple-element.40), channel_id=1, source_target_pairs={{0,8},{1,17},{2,10},{3,19},{4,12},{5,21},{6,14},{7,23},{8,0},{9,25... | collective-permute-start | bytes 3145736 | tf_op jit(solution)/shard_map/ppermute | solution.py:753
  16.6 2.6 %collective-permute-start = (bf16[4,64,256]{2,1,0:T(8,128)(2,1)}, bf16[4,64,256]{2,1,0:T(8,128)(2,1)S(1)}, u32[]{:S(2)}, u32[]{:S(2)}) collective-permute-start(bf16[4,64,256]{2,1,0:T(8,128)(2,1)} %get-tuple-element.37), channel_id=1, source_target_pairs={{0,4},{1,5},{2,6},{3,7},{4,0},{5,1},{6,2},{7,3},{8,12},{9,13},{10,... | collective-permute-start | bytes 393224 | tf_op jit(solution)/shard_map/ppermute | solution.py:756
  19.2 0.0 copy-done.1
  19.2 0.0 copy-done.2
  19.2 0.0 copy-done.3
  19.2 0.0 copy-done.4
  19.2 6.2 %second.1 = (bf16[256,2048]{1,0:T(8,128)(2,1)S(1)}, bf16[256,1024]{1,0:T(8,128)(2,1)S(1)}, bf16[256,2048]{1,0:T(8,128)(2,1)S(1)}, f32[136,128]{1,0:T(8,128)S(1)}) custom-call(s32[16]{0:T(128)S(1)} %copy-done.2, s32[4]{0:T(128)S(1)} %copy-done.3, s32[4]{0:T(128)S(1)} %copy-done.4, bf16[272,2560]{1,0:T(8,128)(2,1)} %get-tuple-element.33.refs_3_, ...), custom_call_target="tpu_custom_call" | custom-call | flops 1 | bytes 1 | tf_op jit(solution)/shard_map/second/pallas_call | solution.py:464
  25.4 0.0 collective-permute-done
  25.5 1.5 %collective-permute-start.1 = (bf16[256,2048]{1,0:T(8,128)(2,1)S(1)}, bf16[256,2048]{1,0:T(8,128)(2,1)S(1)}, u32[]{:S(2)}, u32[]{:S(2)}) collective-permute-start(bf16[256,2048]{1,0:T(8,128)(2,1)S(1)} %get-tuple-element.38), channel_id=1, source_target_pairs={{0,8},{1,17},{2,10},{3,19},{4,12},{5,21},{6,14},{7,23},{8,0},{9,25... | collective-permute-start | bytes 3145736 | tf_op jit(solution)/shard_map/ppermute | solution.py:753
  27.0 0.0 collective-permute-start.2
  27.0 0.0 copy-start
  27.0 3.6 %third.1 = (bf16[256,2048]{1,0:T(8,128)(2,1)S(1)}, bf16[2,1024,1024]{2,1,0:T(8,128)(2,1)S(1)}, bf16[2,1024,1024]{2,1,0:T(8,128)(2,1)S(1)}) custom-call(bf16[256,1024]{1,0:T(8,128)(2,1)S(1)} %get-tuple-element.34.attn, bf16[1024,4096]{1,0:T(8,128)(2,1)} %wo_hbm.1), custom_call_target="tpu_custom_call" | custom-call | flops 1 | bytes 1 | tf_op jit(solution)/shard_map/third/pallas_call | solution.py:517
  30.5 2.4 %collective-permute-done.2.other = f32[136,128]{1,0:T(8,128)S(1)} collective-permute-done((f32[136,128]{1,0:T(8,128)S(1)}, f32[136,128]{1,0:T(8,128)S(1)}, u32[]{:S(2)}, u32[]{:S(2)}) %collective-permute-start.2) | collective-permute-done | bytes 69664 | tf_op jit(solution)/shard_map/ppermute | solution.py:756
  32.9 0.0 collective-permute-done.3.got
  32.9 0.1 join_4.1.mine
  33.1 1.8 %collective-permute-start.4 = (f32[136,128]{1,0:T(8,128)S(1)}, f32[136,128]{1,0:T(8,128)S(1)}, u32[]{:S(2)}, u32[]{:S(2)}) collective-permute-start(f32[136,128]{1,0:T(8,128)S(1)} %join_4.1.mine), channel_id=1, source_target_pairs={{0,2},{1,3},{2,0},{3,1},{4,6},{5,7},{6,4},{7,5},{8,10},{9,11},{10,... | collective-permute-start | bytes 208904 | tf_op jit(solution)/shard_map/ppermute | solution.py:756
  34.8 2.6 %collective-permute-done.4.other = f32[136,128]{1,0:T(8,128)S(1)} collective-permute-done((f32[136,128]{1,0:T(8,128)S(1)}, f32[136,128]{1,0:T(8,128)S(1)}, u32[]{:S(2)}, u32[]{:S(2)}) %collective-permute-start.4) | collective-permute-done | bytes 69664 | tf_op jit(solution)/shard_map/ppermute | solution.py:756
  37.4 0.1 join_2.1.mine
  37.6 0.0 copy-done
  37.6 1.8 %collective-permute-start.6 = (bf16[2,2,64,256]{3,2,1,0:T(8,128)(2,1)S(1)}, bf16[2,2,64,256]{3,2,1,0:T(8,128)(2,1)S(1)}, u32[]{:S(2)}, u32[]{:S(2)}) collective-permute-start(bf16[2,2,64,256]{3,2,1,0:T(8,128)(2,1)S(1)} %hop_4.1), channel_id=1, source_target_pairs={{0,2},{1,3},{2,0},{3,1},{4,6},{5,7},{6,4},{7,5},{8,10},{9,11},{10,... | collective-permute-start | bytes 393224 | tf_op jit(solution)/shard_map/ppermute | solution.py:756
  39.4 0.0 collective-permute-start.5
  39.4 0.1 pass_on_1.1
  39.5 0.6 collective-permute-start.11
  40.1 0.7 %collective-permute-done.1.got = bf16[256,2048]{1,0:T(8,128)(2,1)S(1)} collective-permute-done((bf16[256,2048]{1,0:T(8,128)(2,1)S(1)}, bf16[256,2048]{1,0:T(8,128)(2,1)S(1)}, u32[]{:S(2)}, u32[]{:S(2)}) %collective-permute-start.1) | collective-permute-done | bytes 1048608 | tf_op jit(solution)/shard_map/ppermute | solution.py:753
  40.8 0.0 collective-permute-done.5.other
  40.8 1.9 %collective-permute-done.6.refs_2_ = bf16[2,2,64,256]{3,2,1,0:T(8,128)(2,1)S(1)} collective-permute-done((bf16[2,2,64,256]{3,2,1,0:T(8,128)(2,1)S(1)}, bf16[2,2,64,256]{3,2,1,0:T(8,128)(2,1)S(1)}, u32[]{:S(2)}, u32[]{:S(2)}) %collective-permute-start.6) | collective-permute-done | bytes 131104 | tf_op jit(solution)/shard_map/ppermute | solution.py:756
  42.7 0.1 pass_on_0.1
  42.8 0.3 collective-permute-start.7
  43.0 0.1 collective-permute-start.12
  43.1 1.3 %decode_project.1 = (bf16[16,1024]{1,0:T(8,128)(2,1)S(1)}, bf16[16,1024]{1,0:T(8,128)(2,1)S(1)}, bf16[16,1024]{1,0:T(8,128)(2,1)S(1)}, bf16[16,1024]{1,0:T(8,128)(2,1)S(1)}) custom-call(f32[136,128]{1,0:T(8,128)S(1)} %join_2.1.mine, f32[136,128]{1,0:T(8,128)S(1)} %collective-permute-done.5.other, bf16[2,1024,1024]{2,1,0:T(8,128)(2,1)S(1)} %get-tuple-element.53.wo_a, ...), custom_call_target="tpu_custom_call" | custom-call | flops 1 | bytes 1 | tf_op jit(solution)/shard_map/decode_project/pallas_call | solution.py:634
  44.4 1.8 %collective-permute-start.8 = (bf16[16,1024]{1,0:T(8,128)(2,1)S(1)}, bf16[16,1024]{1,0:T(8,128)(2,1)S(1)}, u32[]{:S(2)}, u32[]{:S(2)}) collective-permute-start(bf16[16,1024]{1,0:T(8,128)(2,1)S(1)} %get-tuple-element.56), channel_id=1, source_target_pairs={{0,16},{1,9},{2,18},{3,11},{4,20},{5,13},{6,22},{7,15},{8,24},{9,1... | collective-permute-start | bytes 98312 | tf_op jit(solution)/shard_map/ppermute | solution.py:753
  46.3 1.4 %collective-permute-start.9 = (bf16[16,1024]{1,0:T(8,128)(2,1)S(1)}, bf16[16,1024]{1,0:T(8,128)(2,1)S(1)}, u32[]{:S(2)}, u32[]{:S(2)}) collective-permute-start(bf16[16,1024]{1,0:T(8,128)(2,1)S(1)} %get-tuple-element.57), channel_id=1, source_target_pairs={{0,24},{1,25},{2,26},{3,27},{4,28},{5,29},{6,30},{7,31},{8,16},{9,... | collective-permute-start | bytes 98312 | tf_op jit(solution)/shard_map/ppermute | solution.py:753
  47.6 0.0 collective-permute-done.12.refs_3_
  47.6 0.3 collective-permute-start.10
  47.9 0.9 %collective-permute-done.11.last = bf16[256,1024]{1,0:T(8,128)(2,1)S(1)} collective-permute-done((bf16[256,1024]{1,0:T(8,128)(2,1)S(1)}, bf16[256,1024]{1,0:T(8,128)(2,1)S(1)}, u32[]{:S(2)}, u32[]{:S(2)}) %collective-permute-start.11) | collective-permute-done | bytes 524320 | tf_op jit(solution)/shard_map/ppermute | solution.py:753
  48.8 1.0 %finish_1.1 = (bf16[2,256,1024]{2,1,0:T(8,128)(2,1)}, bf16[8,64,256]{2,1,0:T(8,128)(2,1)}) custom-call(bf16[256,2048]{1,0:T(8,128)(2,1)S(1)} %get-tuple-element.45.own, bf16[256,2048]{1,0:T(8,128)(2,1)S(1)} %collective-permute-done.3.got, bf16[256,1024]{1,0:T(8,128)(2,1)S(1)} %collective-permute-done.11.last, bf16[1,8,64,256]{3,2,1,0:T(8,128)(2,1)S(1)} %bitcast.8, ...), custom_call_target="tpu_custom_call" | custom-call | flops 1 | bytes 1 | tf_op jit(solution)/shard_map/finish_1/pallas_call | solution.py:684
  49.8 6.0 %collective-permute-done.8.refs_1_ = bf16[16,1024]{1,0:T(8,128)(2,1)S(1)} collective-permute-done((bf16[16,1024]{1,0:T(8,128)(2,1)S(1)}, bf16[16,1024]{1,0:T(8,128)(2,1)S(1)}, u32[]{:S(2)}, u32[]{:S(2)}) %collective-permute-start.8) | collective-permute-done | bytes 32800 | tf_op jit(solution)/shard_map/ppermute | solution.py:753
  55.8 0.0 collective-permute-done.9.refs_2_
  55.8 0.0 collective-permute-done.10.refs_3_
  55.8 0.0 collective-permute-done.7.last
  55.8 1.5 %finish_0.1 = (bf16[2,256,1024]{2,1,0:T(8,128)(2,1)}, bf16[4,4,1024]{2,1,0:T(4,128)(2,1)}) custom-call(bf16[256,2048]{1,0:T(8,128)(2,1)S(1)} %get-tuple-element.35.own, bf16[256,2048]{1,0:T(8,128)(2,1)S(1)} %collective-permute-done.1.got, bf16[256,1024]{1,0:T(8,128)(2,1)S(1)} %collective-permute-done.7.last, ...), custom_call_target="tpu_custom_call", output_to_operand_aliasing={{0}: (7, {})} | custom-call | flops 1 | bytes 1 | tf_op jit(solution)/shard_map/finish_0/pallas_call | solution.py:717
  (2 shorter events, 0.0 us)
Async XLA Ops:
  0.6 18.5 %copy-start.1 = (bf16[1,4,512,256]{3,2,1,0:T(8,128)(2,1)S(1)}, bf16[1,4,512,256]{3,2,1,0:T(8,128)(2,1)}, u32[]{:S(2)}) copy-start(bf16[1,4,512,256]{3,2,1,0:T(8,128)(2,1)} %param.17) | copy-start | bytes 3145732
  0.6 18.5 %copy-start.2 = (s32[16]{0:T(128)S(1)}, s32[16]{0:T(128)}, u32[]{:S(2)}) copy-start(s32[16]{0:T(128)} %refs_0_.3) | copy-start | bytes 196
  0.7 18.5 %copy-start.3 = (s32[4]{0:T(128)S(1)}, s32[4]{0:T(128)}, u32[]{:S(2)}) copy-start(s32[4]{0:T(128)} %refs_1_.3) | copy-start | bytes 52
  0.7 18.5 %copy-start.4 = (s32[4]{0:T(128)S(1)}, s32[4]{0:T(128)}, u32[]{:S(2)}) copy-start(s32[4]{0:T(128)} %refs_2_.3) | copy-start | bytes 52
  13.6 19.4 %collective-permute-start.3 = (bf16[256,2048]{1,0:T(8,128)(2,1)}, bf16[256,2048]{1,0:T(8,128)(2,1)S(1)}, u32[]{:S(2)}, u32[]{:S(2)}) collective-permute-start(bf16[256,2048]{1,0:T(8,128)(2,1)} %get-tuple-element.40), channel_id=1, source_target_pairs={{0,8},{1,17},{2,10},{3,19},{4,12},{5,21},{6,14},{7,23},{8,0},{9,25... | collective-permute-start | bytes 3145736 | tf_op jit(solution)/shard_map/ppermute | solution.py:753
  16.6 8.9 %collective-permute-start = (bf16[4,64,256]{2,1,0:T(8,128)(2,1)}, bf16[4,64,256]{2,1,0:T(8,128)(2,1)S(1)}, u32[]{:S(2)}, u32[]{:S(2)}) collective-permute-start(bf16[4,64,256]{2,1,0:T(8,128)(2,1)} %get-tuple-element.37), channel_id=1, source_target_pairs={{0,4},{1,5},{2,6},{3,7},{4,0},{5,1},{6,2},{7,3},{8,12},{9,13},{10,... | collective-permute-start | bytes 393224 | tf_op jit(solution)/shard_map/ppermute | solution.py:756
  25.5 15.3 %collective-permute-start.1 = (bf16[256,2048]{1,0:T(8,128)(2,1)S(1)}, bf16[256,2048]{1,0:T(8,128)(2,1)S(1)}, u32[]{:S(2)}, u32[]{:S(2)}) collective-permute-start(bf16[256,2048]{1,0:T(8,128)(2,1)S(1)} %get-tuple-element.38), channel_id=1, source_target_pairs={{0,8},{1,17},{2,10},{3,19},{4,12},{5,21},{6,14},{7,23},{8,0},{9,25... | collective-permute-start | bytes 3145736 | tf_op jit(solution)/shard_map/ppermute | solution.py:753
  27.0 6.0 %collective-permute-start.2 = (f32[136,128]{1,0:T(8,128)S(1)}, f32[136,128]{1,0:T(8,128)S(1)}, u32[]{:S(2)}, u32[]{:S(2)}) collective-permute-start(f32[136,128]{1,0:T(8,128)S(1)} %get-tuple-element.39.mine), channel_id=1, source_target_pairs={{0,4},{1,5},{2,6},{3,7},{4,0},{5,1},{6,2},{7,3},{8,12},{9,13},{10,... | collective-permute-start | bytes 208904 | tf_op jit(solution)/shard_map/ppermute | solution.py:756
  27.0 10.6 %copy-start = (bf16[8,64,256]{2,1,0:T(8,128)(2,1)S(1)}, bf16[8,64,256]{2,1,0:T(8,128)(2,1)}, u32[]{:S(2)}) copy-start(bf16[8,64,256]{2,1,0:T(8,128)(2,1)} %get-tuple-element.42) | copy-start | bytes 786436
  33.1 4.4 %collective-permute-start.4 = (f32[136,128]{1,0:T(8,128)S(1)}, f32[136,128]{1,0:T(8,128)S(1)}, u32[]{:S(2)}, u32[]{:S(2)}) collective-permute-start(f32[136,128]{1,0:T(8,128)S(1)} %join_4.1.mine), channel_id=1, source_target_pairs={{0,2},{1,3},{2,0},{3,1},{4,6},{5,7},{6,4},{7,5},{8,10},{9,11},{10,... | collective-permute-start | bytes 208904 | tf_op jit(solution)/shard_map/ppermute | solution.py:756
  37.6 5.0 %collective-permute-start.6 = (bf16[2,2,64,256]{3,2,1,0:T(8,128)(2,1)S(1)}, bf16[2,2,64,256]{3,2,1,0:T(8,128)(2,1)S(1)}, u32[]{:S(2)}, u32[]{:S(2)}) collective-permute-start(bf16[2,2,64,256]{3,2,1,0:T(8,128)(2,1)S(1)} %hop_4.1), channel_id=1, source_target_pairs={{0,2},{1,3},{2,0},{3,1},{4,6},{5,7},{6,4},{7,5},{8,10},{9,11},{10,... | collective-permute-start | bytes 393224 | tf_op jit(solution)/shard_map/ppermute | solution.py:756
  39.4 1.4 %collective-permute-start.5 = (f32[136,128]{1,0:T(8,128)S(1)}, f32[136,128]{1,0:T(8,128)S(1)}, u32[]{:S(2)}, u32[]{:S(2)}) collective-permute-start(f32[136,128]{1,0:T(8,128)S(1)} %join_2.1.mine), channel_id=1, source_target_pairs={{0,1},{1,0},{2,3},{3,2},{4,5},{5,4},{6,7},{7,6},{8,9},{9,8},{10,11... | collective-permute-start | bytes 208904 | tf_op jit(solution)/shard_map/ppermute | solution.py:756
  39.5 9.2 %collective-permute-start.11 = (bf16[256,1024]{1,0:T(8,128)(2,1)S(1)}, bf16[256,1024]{1,0:T(8,128)(2,1)S(1)}, u32[]{:S(2)}, u32[]{:S(2)}) collective-permute-start(bf16[256,1024]{1,0:T(8,128)(2,1)S(1)} %pass_on_1.1), channel_id=1, source_target_pairs={{0,16},{1,9},{2,18},{3,11},{4,20},{5,13},{6,22},{7,15},{8,24},{9,1... | collective-permute-start | bytes 1572872 | tf_op jit(solution)/shard_map/ppermute | solution.py:753
  42.8 13.0 %collective-permute-start.7 = (bf16[256,1024]{1,0:T(8,128)(2,1)S(1)}, bf16[256,1024]{1,0:T(8,128)(2,1)S(1)}, u32[]{:S(2)}, u32[]{:S(2)}) collective-permute-start(bf16[256,1024]{1,0:T(8,128)(2,1)S(1)} %pass_on_0.1), channel_id=1, source_target_pairs={{0,16},{1,9},{2,18},{3,11},{4,20},{5,13},{6,22},{7,15},{8,24},{9,1... | collective-permute-start | bytes 1572872 | tf_op jit(solution)/shard_map/ppermute | solution.py:753
  43.0 4.6 %collective-permute-start.12 = (bf16[4,1,64,256]{3,2,1,0:T(8,128)(2,1)S(1)}, bf16[4,1,64,256]{3,2,1,0:T(8,128)(2,1)S(1)}, u32[]{:S(2)}, u32[]{:S(2)}) collective-permute-start(bf16[4,1,64,256]{3,2,1,0:T(8,128)(2,1)S(1)} %hop_2.1), channel_id=1, source_target_pairs={{0,1},{1,0},{2,3},{3,2},{4,5},{5,4},{6,7},{7,6},{8,9},{9,8},{10,11... | collective-permute-start | bytes 393224 | tf_op jit(solution)/shard_map/ppermute | solution.py:756
  44.4 11.4 %collective-permute-start.8 = (bf16[16,1024]{1,0:T(8,128)(2,1)S(1)}, bf16[16,1024]{1,0:T(8,128)(2,1)S(1)}, u32[]{:S(2)}, u32[]{:S(2)}) collective-permute-start(bf16[16,1024]{1,0:T(8,128)(2,1)S(1)} %get-tuple-element.56), channel_id=1, source_target_pairs={{0,16},{1,9},{2,18},{3,11},{4,20},{5,13},{6,22},{7,15},{8,24},{9,1... | collective-permute-start | bytes 98312 | tf_op jit(solution)/shard_map/ppermute | solution.py:753
  46.3 9.5 %collective-permute-start.9 = (bf16[16,1024]{1,0:T(8,128)(2,1)S(1)}, bf16[16,1024]{1,0:T(8,128)(2,1)S(1)}, u32[]{:S(2)}, u32[]{:S(2)}) collective-permute-start(bf16[16,1024]{1,0:T(8,128)(2,1)S(1)} %get-tuple-element.57), channel_id=1, source_target_pairs={{0,24},{1,25},{2,26},{3,27},{4,28},{5,29},{6,30},{7,31},{8,16},{9,... | collective-permute-start | bytes 98312 | tf_op jit(solution)/shard_map/ppermute | solution.py:753
  47.6 8.2 %collective-permute-start.10 = (bf16[16,1024]{1,0:T(8,128)(2,1)S(1)}, bf16[16,1024]{1,0:T(8,128)(2,1)S(1)}, u32[]{:S(2)}, u32[]{:S(2)}) collective-permute-start(bf16[16,1024]{1,0:T(8,128)(2,1)S(1)} %get-tuple-element.58), channel_id=1, source_target_pairs={{0,8},{1,17},{2,10},{3,19},{4,12},{5,21},{6,14},{7,23},{8,0},{9,25... | collective-permute-start | bytes 98312 | tf_op jit(solution)/shard_map/ppermute | solution.py:753
